TPU v7x, 128 devices: a whole 4x4x4 slice. The times are simulated.
128 devices in a mesh: dp: 32 (over x, z, core), hid: 4 (over y).
Axes of the slice: x: 4, y: 4, z: 4, core: 2. Of those that a mesh axis runs over, the one named last changes fastest.
Arguments:
- tokens: bfloat16 [16384, 1024], P(('dp', 'hid')), may hold values from -6 to 6
- w_query: bfloat16 [1024, 1024], replicated, may hold values from -0.1875 to 0.1875
- w_key: bfloat16 [1024, 512], replicated, may hold values from -0.1875 to 0.1875
- w_value: bfloat16 [1024, 512], replicated, may hold values from -0.1875 to 0.1875
- w_output: bfloat16 [1024, 1024], replicated, may hold values from -1 to 1
- gain_attn: float32 [1024], replicated, may hold values from 0.5 to 1.5
- gain_moe: float32 [1024], replicated, may hold values from 0.5 to 1.5
- router: bfloat16 [1024, 32], replicated, may hold values from -0.09375 to 0.09375
- w_gate: bfloat16 [32, 1024, 512], P('dp', None, 'hid'), may hold values from -0.1875 to 0.1875
- w_up: bfloat16 [32, 1024, 512], P('dp', None, 'hid'), may hold values from -0.1875 to 0.1875
- w_down: bfloat16 [32, 512, 1024], P('dp', 'hid'), may hold values from -0.75 to 0.75
- cotangent: bfloat16 [16384, 1024], P(('dp', 'hid')), may hold values from -6 to 6
- routes: int32 [16384, 8], P(('dp', 'hid')), may hold values from 0 to 31, all different within a row; in each aligned block of 128 rows (0 to 127, 128 to 255, ...) at most 48 rows name the same one
- lengths: int32 [32], P('dp'), may hold values from 385 to 512, as said below
Outputs:
- layer_out: bfloat16 [16384, 1024], P(('dp', 'hid'))
- grad_input: float32 [16384, 1024], P(('dp', 'hid'))
- grad_w_query: float32 [1024, 1024], replicated
- grad_w_key: float32 [1024, 512], replicated
- grad_w_value: float32 [1024, 512], replicated
- grad_w_output: float32 [1024, 1024], replicated
- grad_gain_attn: float32 [1024], replicated
- grad_gain_moe: float32 [1024], replicated
- grad_router: float32 [1024, 32], replicated
- grad_gate: float32 [32, 1024, 512], P('dp', None, 'hid')
- grad_up: float32 [32, 1024, 512], P('dp', None, 'hid')
- grad_down: float32 [32, 512, 1024], P('dp', 'hid')
- counts: int32 [32], replicated
Inputs may be any that keep to these rules, and one draw needn't show every extreme that they name: `routes`: each row names 8 different experts. Among the 128 rows of one device no expert is named more than 48 times, and in every draw some expert is named exactly 48 times by the rows of some device. `lengths`: every length exceeds 3 * 128; in every draw some sequence has exactly 512 tokens.
All inputs are finite; a program needn't handle non-finite values.
Results may differ from a plain program's by a relative error of at most 0.018.
Values may be sent and summed in bfloat16 or wider, within the bound.
A program may use at most 256 MiB of HBM per device.

v0:
```python
import jax
import jax.numpy as jnp
from jax import lax
from jax.sharding import PartitionSpec as P

D = 1024
HEADS = 16
KV_HEADS = 8
HEAD_DIM = 64
EXPERTS = 32
TOP = 8
CAP = 48


def rms_forward(values, gain_vector):
    inverse_root = lax.rsqrt(jnp.mean(values * values, axis=-1, keepdims=True) + 1e-06)
    return (values * inverse_root * gain_vector, inverse_root)


def rms_backward(values, inverse_root, gain_vector, upstream):
    scaled = upstream * gain_vector
    grad_gain = jnp.sum(upstream * values * inverse_root, axis=0)
    grad_values = inverse_root * scaled - values * inverse_root**3 * jnp.mean(
        scaled * values, axis=-1, keepdims=True
    )
    return (grad_values, grad_gain)


def rope_tables(first_pos, row_count, head_width):
    half_dim = head_width // 2
    inverse = 10000.0 ** (-jnp.arange(half_dim, dtype=jnp.float32) / half_dim)
    phases = (first_pos + jnp.arange(row_count, dtype=jnp.float32))[:, None] * inverse[None, :]
    return (jnp.sin(phases)[:, None, :], jnp.cos(phases)[:, None, :])


def rotate(values, sine_table, cosine_table):
    half_dim = values.shape[-1] // 2
    front_half = values[..., :half_dim]
    back_half = values[..., half_dim:]
    return jnp.concatenate(
        [
            front_half * cosine_table - back_half * sine_table,
            back_half * cosine_table + front_half * sine_table,
        ],
        axis=-1,
    )


def unrotate(grad_values, sine_table, cosine_table):
    half_dim = grad_values.shape[-1] // 2
    front_half = grad_values[..., :half_dim]
    back_half = grad_values[..., half_dim:]
    return jnp.concatenate(
        [
            front_half * cosine_table + back_half * sine_table,
            back_half * cosine_table - front_half * sine_table,
        ],
        axis=-1,
    )


def expert_front(rows, gate_mat, up_mat):
    gate_part = jnp.einsum("red,edf->ref", rows, gate_mat, preferred_element_type=jnp.float32)
    up_part = jnp.einsum("red,edf->ref", rows, up_mat, preferred_element_type=jnp.float32)
    act_low = (gate_part * jax.nn.sigmoid(gate_part) * up_part).astype(jnp.bfloat16)
    return (gate_part, up_part, act_low)


def expert_back(rows, grad_rows_in, gate_part, up_part, act_low, down_mat):
    grad_act = jnp.einsum(
        "red,efd->ref", grad_rows_in, down_mat, preferred_element_type=jnp.float32
    )
    grad_down_mat = jnp.einsum(
        "ref,red->efd", act_low, grad_rows_in, preferred_element_type=jnp.float32
    )
    sigmoid_gate = jax.nn.sigmoid(gate_part)
    grad_gate_part = (
        grad_act * up_part * sigmoid_gate * (1.0 + gate_part * (1.0 - sigmoid_gate))
    ).astype(jnp.bfloat16)
    grad_up_part = (grad_act * gate_part * sigmoid_gate).astype(jnp.bfloat16)
    grad_gate_mat = jnp.einsum(
        "red,ref->edf", rows, grad_gate_part, preferred_element_type=jnp.float32
    )
    grad_up_mat = jnp.einsum("red,ref->edf", rows, grad_up_part, preferred_element_type=jnp.float32)
    return (grad_gate_part, grad_up_part, grad_gate_mat, grad_up_mat, grad_down_mat)


def input_grads(grad_gate_part, grad_up_part, gate_mat, up_mat):
    return jnp.einsum(
        "ref,edf->red", grad_gate_part, gate_mat, preferred_element_type=jnp.float32
    ) + jnp.einsum("ref,edf->red", grad_up_part, up_mat, preferred_element_type=jnp.float32)


def shards(
    tokens,
    w_query,
    w_key,
    w_value,
    w_output,
    gain_attn,
    gain_moe,
    router,
    w_gate,
    w_up,
    w_down,
    cotangent,
    routes,
    lengths,
):
    tok_count = tokens.shape[0]
    hid_pos = lax.axis_index("hid")
    first_pos = (hid_pos * tok_count).astype(jnp.float32)
    group_size = HEADS // KV_HEADS
    score_scale = HEAD_DIM ** (-0.5)
    inputs = tokens.astype(jnp.float32)
    normed, root_attn = rms_forward(inputs, gain_attn)
    normed_low = normed.astype(jnp.bfloat16)
    sine_table, cosine_table = rope_tables(first_pos, tok_count, HEAD_DIM)
    query_raw = jnp.dot(normed_low, w_query, preferred_element_type=jnp.float32).reshape(
        tok_count, HEADS, HEAD_DIM
    )
    key_raw = jnp.dot(normed_low, w_key, preferred_element_type=jnp.float32).reshape(
        tok_count, KV_HEADS, HEAD_DIM
    )
    value_low = (
        jnp.dot(normed_low, w_value, preferred_element_type=jnp.float32)
        .astype(jnp.bfloat16)
        .reshape(tok_count, KV_HEADS, HEAD_DIM)
    )
    query_low = rotate(query_raw, sine_table, cosine_table).astype(jnp.bfloat16)
    key_low = rotate(key_raw, sine_table, cosine_table).astype(jnp.bfloat16)
    keys_all, values_all = (
        lax.all_gather(key_low, "hid", axis=0, tiled=True),
        lax.all_gather(value_low, "hid", axis=0, tiled=True),
    )
    seq_count = keys_all.shape[0]
    grouped = query_low.reshape(tok_count, KV_HEADS, group_size, HEAD_DIM)
    query_pos = hid_pos * tok_count + jnp.arange(tok_count, dtype=jnp.int32)
    key_pos = jnp.arange(seq_count, dtype=jnp.int32)
    allowed = (key_pos[None, :] <= query_pos[:, None]) & (key_pos[None, :] < lengths[0])

    def masked_scores():
        raw_scores = (
            jnp.einsum("tkgd,skd->kgts", grouped, keys_all, preferred_element_type=jnp.float32)
            * score_scale
        )
        return jnp.where(allowed, raw_scores, -1e30)

    masked = masked_scores()
    top_score = jnp.max(masked, axis=-1, keepdims=True)
    log_total = top_score + jnp.log(jnp.sum(jnp.exp(masked - top_score), axis=-1, keepdims=True))
    softmaxed_low = jnp.exp(masked - log_total).astype(jnp.bfloat16)
    mixed_low = jnp.einsum(
        "kgts,skd->tkgd", softmaxed_low, values_all, preferred_element_type=jnp.float32
    )
    mixed_low = mixed_low.reshape(tok_count, HEADS * HEAD_DIM).astype(jnp.bfloat16)
    hidden = inputs + jnp.dot(mixed_low, w_output, preferred_element_type=jnp.float32)
    normed_two, root_moe = rms_forward(hidden, gain_moe)
    normed_two_low = normed_two.astype(jnp.bfloat16)
    logits = jnp.dot(normed_two_low, router, preferred_element_type=jnp.float32)
    route_onehot = (routes[:, :, None] == jnp.arange(EXPERTS, dtype=jnp.int32)).astype(jnp.float32)
    picked = jnp.sum(logits[:, None, :] * route_onehot, axis=-1)
    gate_weights = jax.nn.softmax(picked, axis=-1)
    flat_routes = routes.reshape(-1)
    flat_onehot = (flat_routes[:, None] == jnp.arange(EXPERTS, dtype=jnp.int32)).astype(jnp.int32)
    slot_rank = jnp.sum((jnp.cumsum(flat_onehot, axis=0) - 1) * flat_onehot, axis=1)
    slot_index = slot_rank * EXPERTS + flat_routes
    slot_total = CAP * EXPERTS
    owner_pair = (
        jnp.full((slot_total,), tok_count * TOP, jnp.int32)
        .at[slot_index]
        .set(jnp.arange(tok_count * TOP, dtype=jnp.int32))
    )
    rows_pad = jnp.concatenate([normed_two_low, jnp.zeros((1, D), jnp.bfloat16)], axis=0)
    send_rows = rows_pad[owner_pair // TOP].reshape(CAP, EXPERTS, D)
    received = lax.all_to_all(send_rows, "dp", split_axis=1, concat_axis=0, tiled=True)
    rows_all = lax.all_gather(received, "hid", axis=0, tiled=True)
    gate_part, up_part, act_low = expert_front(rows_all, w_gate, w_up)
    expert_out = lax.psum_scatter(
        jnp.einsum("ref,efd->red", act_low, w_down, preferred_element_type=jnp.float32).astype(
            jnp.bfloat16
        ),
        "hid",
        scatter_dimension=0,
        tiled=True,
    )
    returned = lax.all_to_all(expert_out, "dp", split_axis=0, concat_axis=1, tiled=True)
    pair_out = returned.reshape(slot_total, D)[slot_index].reshape(tok_count, TOP, D)
    layer_out = (hidden + jnp.sum(gate_weights[:, :, None] * pair_out, axis=1)).astype(jnp.bfloat16)
    live_rows = (query_pos < lengths[0]).astype(jnp.float32)
    upstream = cotangent.astype(jnp.float32) * live_rows[:, None]
    grad_gates = jnp.sum(upstream[:, None, :] * pair_out, axis=-1)
    grad_picked = gate_weights * (
        grad_gates - jnp.sum(gate_weights * grad_gates, axis=-1, keepdims=True)
    )
    grad_logits = jnp.einsum("tk,tke->te", grad_picked, route_onehot).astype(jnp.bfloat16)
    grad_router = jnp.einsum(
        "td,te->de", normed_two_low, grad_logits, preferred_element_type=jnp.float32
    )
    slot_grads = (
        (gate_weights[:, :, None] * upstream[:, None, :])
        .astype(jnp.bfloat16)
        .reshape(tok_count * TOP, D)
    )
    grads_pad = jnp.concatenate([slot_grads, jnp.zeros((1, D), jnp.bfloat16)], axis=0)
    send_grads = grads_pad[owner_pair].reshape(CAP, EXPERTS, D)
    grad_received = lax.all_to_all(send_grads, "dp", split_axis=1, concat_axis=0, tiled=True)
    grad_all = lax.all_gather(grad_received, "hid", axis=0, tiled=True)
    grad_gate_part, grad_up_part, grad_gate, grad_up, grad_down = expert_back(
        rows_all, grad_all, gate_part, up_part, act_low, w_down
    )
    grad_rows = lax.psum_scatter(
        input_grads(grad_gate_part, grad_up_part, w_gate, w_up).astype(jnp.bfloat16),
        "hid",
        scatter_dimension=0,
        tiled=True,
    )
    returned_grads = lax.all_to_all(grad_rows, "dp", split_axis=0, concat_axis=1, tiled=True)
    pair_grads = returned_grads.reshape(slot_total, D)[slot_index].reshape(tok_count, TOP, D)
    grad_normed_two = jnp.einsum(
        "te,de->td", grad_logits, router, preferred_element_type=jnp.float32
    )
    grad_normed_two = grad_normed_two + jnp.sum(pair_grads.astype(jnp.float32), axis=1)
    grad_hidden_part, grad_gain_moe = rms_backward(hidden, root_moe, gain_moe, grad_normed_two)
    grad_hidden = upstream + grad_hidden_part
    grad_hidden_low = grad_hidden.astype(jnp.bfloat16)
    grad_w_output = jnp.einsum(
        "tf,td->fd", mixed_low, grad_hidden_low, preferred_element_type=jnp.float32
    )
    grad_mixed = jnp.einsum(
        "td,fd->tf", grad_hidden_low, w_output, preferred_element_type=jnp.float32
    )
    grad_mixed = grad_mixed.astype(jnp.bfloat16).reshape(tok_count, KV_HEADS, group_size, HEAD_DIM)
    softmaxed = jnp.exp(masked_scores() - log_total)
    grad_probs = jnp.einsum(
        "tkgd,skd->kgts", grad_mixed, values_all, preferred_element_type=jnp.float32
    )
    grad_scores = (
        softmaxed * (grad_probs - jnp.sum(softmaxed * grad_probs, axis=-1, keepdims=True))
    ).astype(jnp.bfloat16)
    grad_query = (
        jnp.einsum("kgts,skd->tkgd", grad_scores, keys_all, preferred_element_type=jnp.float32)
        * score_scale
    )
    grad_key_part = (
        jnp.einsum("kgts,tkgd->skd", grad_scores, grouped, preferred_element_type=jnp.float32)
        * score_scale
    )
    grad_value_part = jnp.einsum(
        "kgts,tkgd->skd", softmaxed_low, grad_mixed, preferred_element_type=jnp.float32
    )
    grad_key, grad_value = (
        lax.psum_scatter(
            grad_key_part.astype(jnp.bfloat16), "hid", scatter_dimension=0, tiled=True
        ).astype(jnp.float32),
        lax.psum_scatter(
            grad_value_part.astype(jnp.bfloat16), "hid", scatter_dimension=0, tiled=True
        ).astype(jnp.float32),
    )
    grad_query_low = unrotate(
        grad_query.reshape(tok_count, HEADS, HEAD_DIM), sine_table, cosine_table
    )
    grad_query_low = grad_query_low.astype(jnp.bfloat16).reshape(tok_count, HEADS * HEAD_DIM)
    grad_key_low = (
        unrotate(grad_key, sine_table, cosine_table)
        .astype(jnp.bfloat16)
        .reshape(tok_count, KV_HEADS * HEAD_DIM)
    )
    grad_value_low = grad_value.astype(jnp.bfloat16).reshape(tok_count, KV_HEADS * HEAD_DIM)
    grad_w_query = jnp.einsum(
        "td,tf->df", normed_low, grad_query_low, preferred_element_type=jnp.float32
    )
    grad_w_key = jnp.einsum(
        "td,tf->df", normed_low, grad_key_low, preferred_element_type=jnp.float32
    )
    grad_w_value = jnp.einsum(
        "td,tf->df", normed_low, grad_value_low, preferred_element_type=jnp.float32
    )
    grad_normed = (
        jnp.einsum("tf,df->td", grad_query_low, w_query, preferred_element_type=jnp.float32)
        + jnp.einsum("tf,df->td", grad_key_low, w_key, preferred_element_type=jnp.float32)
        + jnp.einsum("tf,df->td", grad_value_low, w_value, preferred_element_type=jnp.float32)
    )
    grad_input_part, grad_gain_attn = rms_backward(inputs, root_attn, gain_attn, grad_normed)
    grad_input = grad_hidden + grad_input_part
    counts_local = jnp.sum(flat_onehot, axis=0).astype(jnp.float32)
    summed = lax.psum(
        (
            grad_w_query,
            grad_w_key,
            grad_w_value,
            grad_w_output,
            grad_gain_attn,
            grad_gain_moe,
            grad_router,
            counts_local,
        ),
        ("dp", "hid"),
    )
    counts = summed[7].astype(jnp.int32)
    return (
        layer_out,
        grad_input,
        summed[0],
        summed[1],
        summed[2],
        summed[3],
        summed[4],
        summed[5],
        summed[6],
        grad_gate,
        grad_up,
        grad_down,
        counts,
    )


def solution(mesh):
    in_specs = (
        P(("dp", "hid"), None),
        P(),
        P(),
        P(),
        P(),
        P(),
        P(),
        P(),
        P("dp", None, "hid"),
        P("dp", None, "hid"),
        P("dp", "hid", None),
        P(("dp", "hid"), None),
        P(("dp", "hid"), None),
        P("dp"),
    )
    out_specs = (
        P(("dp", "hid"), None),
        P(("dp", "hid"), None),
        P(),
        P(),
        P(),
        P(),
        P(),
        P(),
        P(),
        P("dp", None, "hid"),
        P("dp", None, "hid"),
        P("dp", "hid", None),
        P(),
    )
    return jax.shard_map(shards, mesh=mesh, in_specs=in_specs, out_specs=out_specs, check_vma=False)
```

profile of v0, /device:TPU:1, one launch (start us, length us, event | category | flops | bytes accessed | tf_op | source)
XLA Modules:
  0.0 964.4 jit_solution(10209701708645618830)
XLA Ops:
  10.8 9.0 reduce-window.6
  21.0 4.3 scatter_custom_fusion
  25.4 1.7 convolution_convert_fusion.2
  27.2 2.0 fusion.108
  29.4 13.3 %all_gather.13 = bf16[512,8,64]{0,2,1:T(8,128)(2,1)S(1)} all-gather(bf16[128,8,64]{0,2,1:T(8,128)(2,1)S(1)} %pad_maximum_fusion.4), channel_id=1, replica_groups=mesh['dp'=32,'hid'=4] {'hid'}, dimensions={0}, use_global_device_ids=true | all-gather | bytes 655360 | tf_op jit(solution)/shard_map/all_gather | solution.py:133
  42.7 10.3 %all_gather.12 = bf16[512,8,64]{0,2,1:T(8,128)(2,1)S(1)} all-gather(bf16[128,8,64]{0,2,1:T(8,128)(2,1)S(1)} %bitcast.287), channel_id=1, replica_groups=mesh['dp'=32,'hid'=4] {'hid'}, dimensions={0}, use_global_device_ids=true | all-gather | bytes 655360 | tf_op jit(solution)/shard_map/all_gather | solution.py:134
  59.1 5.8 gather_fusion
  64.9 3.6 copy.138
  68.5 52.4 %all_to_all.66 = bf16[48,32,1024]{2,0,1:T(8,128)(2,1)} all-to-all(bf16[48,32,1024]{2,0,1:T(8,128)(2,1)S(1)} %copy.138), channel_id=1, replica_groups=mesh['dp'=32,'hid'=4] {'dp'}, dimensions={1} | all-to-all | bytes 6291456 | tf_op jit(solution)/shard_map/all_to_all | solution.py:176
  125.2 1.6 concatenate.32
  126.7 9.9 %gather_fusion.2 = bf16[1536,1024]{1,0:T(8,128)(2,1)} fusion(bf16[1025,1024]{1,0:T(8,128)(2,1)} %concatenate.32, s32[2048]{0:T(1024)S(1)} %copy-done.49), kind=kCustom, calls=%fused_computation.2 | custom fusion | bytes 6297600 | tf_op jit(solution)/shard_map/gather | solution.py:206
  136.7 3.8 copy.144
  140.5 43.1 %all_to_all.67 = bf16[48,32,1024]{2,0,1:T(8,128)(2,1)} all-to-all(bf16[48,32,1024]{2,0,1:T(8,128)(2,1)S(1)} %copy.144), channel_id=1, replica_groups=mesh['dp'=32,'hid'=4] {'dp'}, dimensions={1} | all-to-all | bytes 6291456 | tf_op jit(solution)/shard_map/all_to_all | solution.py:207
  183.6 53.4 %all-gather.3.cloned.1.call-done = bf16[6144,1,1024]{2,0,1:T(8,128)(2,1)} async-done(((bf16[1536,1,1024]{2,0,1:T(8,128)(2,1)}), bf16[6144,1,1024]{2,0,1:T(8,128)(2,1)}) %all-gather.3.cloned.1.call-update) | async-done | bytes 12582928 | tf_op jit(solution)/shard_map/all_gather | solution.py:177
  237.0 9.8 %fusion.16 = f32[6144,1,128]{2,0,1:T(8,128)} fusion(bf16[6144,1,1024]{2,0,1:T(8,128)(2,1)} %all-gather.3.cloned.1.call-done, bf16[1,1024,128]{2,1,0:T(8,128)(2,1)} %param.23), kind=kOutput, calls=%fused_computation.21 | convolution fusion | flops 1610612736 | bytes 15990784 | tf_op jit(solution)/shard_map/red,edf->ref/dot_general | solution.py:64
  246.8 5.3 fusion.13
  252.1 106.2 %all-gather.5.cloned.1.call-done = bf16[6144,1,1024]{2,0,1:T(8,128)(2,1)} async-done(((bf16[1536,1,1024]{2,0,1:T(8,128)(2,1)}), bf16[6144,1,1024]{2,0,1:T(8,128)(2,1)}) %all-gather.5.cloned.1.call-update) | async-done | bytes 12582928 | tf_op jit(solution)/shard_map/all_gather | solution.py:208
  358.3 12.6 %multiply_convert_fusion = (bf16[6144,1,128]{2,0,1:T(8,128)(2,1)}, bf16[6144,1,128]{2,0,1:T(8,128)(2,1)}, bf16[6144,1,128]{2,0,1:T(8,128)(2,1)S(1)}) fusion(f32[6144,1,128]{2,0,1:T(8,128)} %fusion.13, f32[6144,1,128]{2,0,1:T(8,128)} %fusion.16, bf16[1,128,1024]{2,1,0:T(8,128)(2,1)} %param.24, bf16[6144,1,1024]{2,0,1:T(8,128)(2,1)} %all-gather.5.cloned.1.call-done), kind=kOutput, calls=%fused_computation.39 | convolution fusion | flops 1623195648 | bytes 23855104 | tf_op jit(solution)/shard_map/red,efd->ref/dot_general | solution.py:70
  370.9 1.1 copy-done.6
  372.0 6.4 convert_bitcast_fusion
  378.5 12.4 %fusion.33 = f32[6144,1024]{1,0:T(8,128)} fusion(bf16[6144,1,128]{2,0,1:T(8,128)(2,1)} %get-tuple-element.30, bf16[1,1024,128]{2,1,0:T(8,128)(2,1)S(1)} %copy-done.27), kind=kOutput, calls=%fused_computation.47 | convolution fusion | flops 1610612736 | bytes 27000832 | tf_op jit(solution)/shard_map/ref,edf->red/dot_general | solution.py:89
  390.9 15.7 %fusion = bf16[6144,1,1024]{2,0,1:T(8,128)(2,1)} fusion(f32[6144,1024]{1,0:T(8,128)} %fusion.33, bf16[6144,1,128]{2,0,1:T(8,128)(2,1)} %get-tuple-element.29, bf16[1,1024,128]{2,1,0:T(8,128)(2,1)} %param.23), kind=kOutput, calls=%fused_computation.6 | convolution fusion | flops 1623195648 | bytes 39583744 | tf_op jit(solution)/shard_map/ref,edf->red/dot_general | solution.py:91
  406.6 87.5 %reduce-scatter.9.cloned.1.call-done = bf16[1536,1,1024]{2,0,1:T(8,128)(2,1)} async-done(((bf16[6144,1,1024]{2,0,1:T(8,128)(2,1)}), bf16[1536,1,1024]{2,0,1:T(8,128)(2,1)}) %reduce-scatter.9.cloned.1.call-update) | async-done | bytes 3145744 | tf_op jit(solution)/shard_map/reduce_scatter | solution.py:179
  494.7 6.1 reduce.7
  500.7 8.5 reshape.426
  509.3 7.7 all-to-all-start.1
  517.0 93.7 %reduce-scatter.11.cloned.1.call-done = bf16[1536,1,1024]{2,0,1:T(8,128)(2,1)} async-done(((bf16[6144,1,1024]{2,0,1:T(8,128)(2,1)}), bf16[1536,1,1024]{2,0,1:T(8,128)(2,1)}) %reduce-scatter.11.cloned.1.call-update) | async-done | bytes 3145744 | tf_op jit(solution)/shard_map/reduce_scatter | solution.py:212
  610.7 6.1 reduce.6
  616.8 8.4 reshape.428
  625.2 7.8 all-to-all-start.3
  633.1 19.1 %reshape.427 = bf16[1536,1,1024]{2,1,0:T(2,128)(2,1)} reshape(bf16[32,2,24576]{2,1,0:T(2,128)(2,1)} %all-to-all-done.1) | data formatting | bytes 6291456
  652.2 4.0 copy.174
  656.3 3.4 copy.140
  659.7 8.3 gather_fusion.1
  668.0 4.1 fusion.23
  672.9 18.9 %reshape.429 = bf16[1536,1,1024]{2,1,0:T(2,128)(2,1)} reshape(bf16[32,2,24576]{2,1,0:T(2,128)(2,1)} %all-to-all-done.3) | data formatting | bytes 6291456
  691.8 4.0 copy.175
  695.8 3.4 copy.146
  699.2 8.7 gather_fusion.3
  708.0 3.1 convert_reduce_fusion
  714.2 3.8 fusion.24
  718.1 1.2 fusion.26
  719.3 1.3 copy-done.5
  722.5 4.1 fusion.39
  726.6 2.1 copy.172
  728.6 2.1 convolution_multiply_fusion
  730.9 2.8 fusion.104
  734.6 3.7 fusion.79
  738.3 3.0 reduce-scatter.13.cloned.1.call-done
  742.4 1.9 fusion.102
  744.3 21.0 %reduce-scatter.15.cloned.1.call-done = bf16[128,512]{1,0:T(8,128)(2,1)} async-done(((bf16[512,512]{1,0:T(8,128)(2,1)}), bf16[128,512]{1,0:T(8,128)(2,1)}) %reduce-scatter.15.cloned.1.call-update) | async-done | bytes 131088 | tf_op jit(solution)/shard_map/reshape | solution.py:269
  765.3 2.8 fusion.100
  768.7 7.8 fusion.50
  776.5 7.5 fusion.45
  784.1 4.2 fusion.40
  790.1 1.3 fusion.63
  791.5 68.0 %all-reduce.2 = (f32[1024]{0:T(1024)}, f32[1024]{0:T(1024)}, f32[32]{0:T(128)S(1)}) all-reduce(f32[1024]{0:T(1024)S(1)} %get-tuple-element.17, f32[1024]{0:T(1024)S(1)} %get-tuple-element.15, f32[32]{0:T(128)S(1)} %convert_element_type.191), channel_id=1, replica_groups=mesh['dp'=32,'hid'=4] {'dp','hid'}, use_global_device_ids=true, to_apply=%region_27.28 | all-reduce | flops 2080 | bytes 16640 | tf_op jit(solution)/shard_map/psum | solution.py:287
  860.0 2.1 fusion.60
  862.1 82.4 %all-reduce.6.cloned.1.call-done = (f32[1024,1024]{1,0:T(8,128)}, f32[1024,512]{1,0:T(8,128)}, f32[1024,512]{1,0:T(8,128)}, f32[1024,1024]{1,0:T(8,128)}, f32[1024,32]{0,1:T(8,128)}) async-done(((f32[1024,1024]{1,0:T(8,128)}, f32[1024,512]{1,0:T(8,128)}, f32[1024,512]{1,0:T(8,128)}, f32[1024,1024]{1,0:T(8,128)}, f32[1024,32]{0,1:T(8,128)}), (f32[1024,1024]{1,0:T(8,128)}, f32[1024,512]{1,0:T(8,128)}, ...) | async-done | bytes 12714000 | tf_op jit(solution)/shard_map/psum | solution.py:287
  944.4 4.9 copy.187
  949.4 1.3 copy.188
  951.7 1.3 copy.189
  953.0 1.6 copy-done.15
  954.7 2.0 copy.190
  (221 shorter events, 27.7 us)
Async XLA Ops:
  7.2 50.1 %copy-start = (bf16[1024,1024]{1,0:T(8,128)(2,1)S(1)}, bf16[1024,1024]{1,0:T(8,128)(2,1)}, u32[]{:S(2)}) copy-start(bf16[1024,1024]{1,0:T(8,128)(2,1)} %param.18) | copy-start | bytes 6291460
  7.2 20.0 %copy-start.4 = (bf16[128,1024]{1,0:T(8,128)(2,1)S(1)}, bf16[128,1024]{1,0:T(8,128)(2,1)}, u32[]{:S(2)}) copy-start(bf16[128,1024]{1,0:T(8,128)(2,1)} %param.14) | copy-start | bytes 786436
  7.2 20.0 %copy-start.39 = (f32[1024]{0:T(1024)S(1)}, f32[1024]{0:T(1024)}, u32[]{:S(2)}) copy-start(f32[1024]{0:T(1024)} %param.19) | copy-start | bytes 12292
  7.2 229.8 %all-gather.3.cloned.1.call-start = ((), (), s32[]{:S(2)}) async-start(), calls=%async_computation.8 | async-start | bytes 15728640 | tf_op jit(solution)/shard_map/all_gather | solution.py:177
  10.8 42.3 %copy-start.47 = (f32[128]{0:T(128)}, f32[128]{0:T(128)S(1)}, u32[]{:S(2)}) copy-start(f32[128]{0:T(128)S(1)} %get-tuple-element.47) | copy-start | bytes 1540
  21.0 4.4 copy-start.50
  27.2 25.9 %copy-start.7 = (bf16[1024,1024]{1,0:T(8,128)(2,1)S(1)}, bf16[1024,1024]{1,0:T(8,128)(2,1)}, u32[]{:S(2)}) copy-start(bf16[1024,1024]{1,0:T(8,128)(2,1)} %param.15) | copy-start | bytes 6291460
  29.4 25.8 %copy-start.32 = (f32[128,32]{0,1:T(8,128)}, f32[128,32]{0,1:T(8,128)S(1)}, u32[]{:S(2)}) copy-start(f32[128,32]{0,1:T(8,128)S(1)} %get-tuple-element.44) | copy-start | bytes 49156
  29.4 25.8 %copy-start.34 = (f32[128,32]{0,1:T(8,128)}, f32[128,32]{0,1:T(8,128)S(1)}, u32[]{:S(2)}) copy-start(f32[128,32]{0,1:T(8,128)S(1)} %get-tuple-element.45) | copy-start | bytes 49156
  42.7 12.5 %copy-start.13 = (bf16[512,8,64]{0,2,1:T(8,128)(2,1)}, bf16[512,8,64]{0,2,1:T(8,128)(2,1)S(1)}, u32[]{:S(2)}) copy-start(bf16[512,8,64]{0,2,1:T(8,128)(2,1)S(1)} %all_gather.13) | copy-start | bytes 1572868
  53.1 3.1 copy-start.18
  54.2 1.9 copy-start.23
  54.2 1.9 copy-start.25
  55.2 2.0 copy-start.2
  56.2 2.8 copy-start.44
  57.2 1.7 copy-start.30
  120.9 3.1 copy-start.28
  120.9 237.4 %all-gather.5.cloned.1.call-start = ((), (), s32[]{:S(2)}) async-start(), calls=%async_computation.10 | async-start | bytes 15728640 | tf_op jit(solution)/shard_map/all_gather | solution.py:208
  122.0 1.4 copy-start.52
  124.1 2.6 copy-start.12
  124.1 2.6 copy-start.49
  183.5 63.3 %copy-start.27 = (bf16[1,1024,128]{2,1,0:T(8,128)(2,1)S(1)}, bf16[1,1024,128]{2,1,0:T(8,128)(2,1)}, u32[]{:S(2)}) copy-start(bf16[1,1024,128]{2,1,0:T(8,128)(2,1)} %param.22) | copy-start | bytes 786436
  183.6 310.6 %reduce-scatter.9.cloned.1.call-start = ((), (), s32[]{:S(2)}) async-start(), calls=%async_computation.9 | async-start | bytes 15728640 | tf_op jit(solution)/shard_map/reduce_scatter | solution.py:179
  237.0 9.8 %copy-start.1 = (bf16[6144,1,1024]{2,0,1:T(8,128)(2,1)S(1)}, bf16[6144,1,1024]{2,0,1:T(8,128)(2,1)}, u32[]{:S(2)}) copy-start(bf16[6144,1,1024]{2,0,1:T(8,128)(2,1)} %all-gather.3.cloned.1.call-done) | copy-start | bytes 37748740
  358.3 13.7 %copy-start.36 = (bf16[1,128,1024]{2,1,0:T(8,128)(2,1)S(1)}, bf16[1,128,1024]{2,1,0:T(8,128)(2,1)}, u32[]{:S(2)}) copy-start(bf16[1,128,1024]{2,1,0:T(8,128)(2,1)} %param.24) | copy-start | bytes 786436
  378.5 232.2 %reduce-scatter.11.cloned.1.call-start = ((), (), s32[]{:S(2)}) async-start(), calls=%async_computation.11 | async-start | bytes 15728640 | tf_op jit(solution)/shard_map/reduce_scatter | solution.py:212
  509.3 116.0 %all-to-all-start.1 = ((bf16[32,2,24576]{2,1,0:T(2,128)(2,1)}), bf16[32,2,24576]{2,1,0:T(2,128)(2,1)}, u32[]{:S(2)}, u32[]{:S(2)}) async-start(bf16[32,2,24576]{2,1,0:T(2,128)(2,1)} %reshape.426), calls=%async_computation.2 | async-start | bytes 6291456 | tf_op jit(solution)/shard_map/all_to_all | solution.py:187
  625.2 7.9 copy-start.51
  625.2 47.6 %all-to-all-start.3 = ((bf16[32,2,24576]{2,1,0:T(2,128)(2,1)}), bf16[32,2,24576]{2,1,0:T(2,128)(2,1)}, u32[]{:S(2)}, u32[]{:S(2)}) async-start(bf16[32,2,24576]{2,1,0:T(2,128)(2,1)} %reshape.428), calls=%async_computation.5 | async-start | bytes 6291456 | tf_op jit(solution)/shard_map/all_to_all | solution.py:218
  633.0 108.3 %reduce-scatter.13.cloned.1.call-start = ((), (), s32[]{:S(2)}) async-start(), calls=%async_computation.12 | async-start | bytes 655360
  668.0 4.2 copy-start.53
  668.0 4.2 copy-start.55
  699.2 11.8 %copy-start.38 = (bf16[1024,32]{0,1:T(8,128)(2,1)S(1)}, bf16[1024,32]{0,1:T(8,128)(2,1)}, u32[]{:S(2)}) copy-start(bf16[1024,32]{0,1:T(8,128)(2,1)} %param.21) | copy-start | bytes 196612
  699.2 11.9 %copy-start.45 = (f32[1024]{0:T(1024)S(1)}, f32[1024]{0:T(1024)}, u32[]{:S(2)}) copy-start(f32[1024]{0:T(1024)} %param.20) | copy-start | bytes 12292
  699.2 11.9 %copy-start.57 = (f32[128]{0:T(128)S(1)}, f32[128]{0:T(128)}, u32[]{:S(2)}) copy-start(f32[128]{0:T(128)} %copy-done.56) | copy-start | bytes 1540
  707.9 3.5 copy-start.21
  707.9 3.5 copy-start.29
  708.0 3.5 copy-start.59
  708.0 3.5 copy-start.61
  711.4 2.8 copy-start.43
  714.2 3.8 copy-start.3
  718.0 2.6 copy-start.24
  718.1 2.6 copy-start.26
  722.4 6.2 copy-start.14
  722.4 42.9 %reduce-scatter.15.cloned.1.call-start = ((), (), s32[]{:S(2)}) async-start(), calls=%async_computation.13 | async-start | bytes 655360 | tf_op jit(solution)/shard_map/reshape | solution.py:269
  726.5 4.2 copy-start.33
  726.5 4.2 copy-start.35
  726.5 4.3 copy-start.40
  726.6 4.3 copy-start.48
  730.8 3.8 copy-start.10
  733.7 210.7 %all-reduce.6.cloned.1.call-start = ((), (), s32[]{:S(2)}) async-start(), calls=%async_computation.14 | async-start | bytes 25427968 | tf_op jit(solution)/shard_map/psum | solution.py:287
  768.7 7.8 copy-start.11
  768.7 15.4 %slice-start = ((s8[12582912]{0:T(1024)(128)(4,1)}), s8[4194304]{0:T(1024)(128)(4,1)S(1)}, s32[]{:S(2)}) async-start(s8[12582912]{0:T(1024)(128)(4,1)} %bitcast.263), calls=%async_computation.15 | async-start | bytes 8388608
  768.7 15.4 %slice-start.1 = ((s8[12582912]{0:T(1024)(128)(4,1)}), s8[4194304]{0:T(1024)(128)(4,1)S(1)}, s32[]{:S(2)}) async-start(s8[12582912]{0:T(1024)(128)(4,1)} %bitcast.263), calls=%async_computation.16 | async-start | bytes 8388608
  776.5 7.6 slice-start.2
  776.5 7.6 copy-start.22
  784.1 4.2 copy-start.8
  788.4 1.8 copy-start.17
  788.4 1.8 copy-start.31
  788.4 71.6 %copy-start.62 = (f32[128]{0:T(128)S(1)}, f32[128]{0:T(128)}, u32[]{:S(2)}) copy-start(f32[128]{0:T(128)} %get-tuple-element.46) | copy-start | bytes 1540
  944.4 4.9 copy-start.20
  949.4 2.3 copy-start.19
  951.7 2.9 copy-start.15
  954.7 2.0 copy-start.41
  (11 other events, 10.0 us)
Sparse Core Ops, SparseCore 0:
  121.0 115.9 all-gather.2
  238.7 119.5 all-gather.4
  378.6 115.5 reduce-scatter.8
  496.5 114.1 reduce-scatter.10
  722.5 18.7 reduce-scatter.12
  744.1 21.1 reduce-scatter.14
  772.4 171.9 all-reduce.5
where the time goes:
time: 975 us; the launch traced here: 964 us
  waiting for transfers between devices  448 us (46%)
  blocking collectives  187 us (19%)
  local copies, waits for them, and re-layouts  142 us (15%)
  matrix products  115 us (12%)
  other arithmetic  39.6 us (4%)
  starting transfers between devices  16.3 us (2%)
  between operations  15.9 us (2%)
    all_gather x1, waiting for transfers between devices, shards(): grad_all = lax.all_gather(grad_received, 'hid', axis=0, tiled=True)  106 us
    reduce_scatter x1, waiting for transfers between devices, shards(): lax.psum_scatter(input_grads(grad_gate_part, grad_up_part, w_gate, w_up)....  93.7 us
    reduce_scatter x1, waiting for transfers between devices, shards(): lax.psum_scatter(jnp.einsum('ref,efd->red', act_low, w_down, preferred_el...  87.5 us
    unnamed x147, local copies, waits for them, and re-layouts  87.1 us
    psum x1, waiting for transfers between devices, shards(): lax.psum((grad_w_query, grad_w_key, grad_w_value, grad_w_output, grad_gai...  82.4 us
    psum x1, blocking collectives, shards(): lax.psum((grad_w_query, grad_w_key, grad_w_value, grad_w_output, grad_gai...  68 us
    all_gather x1, waiting for transfers between devices, shards(): rows_all = lax.all_gather(received, 'hid', axis=0, tiled=True)  53.4 us
    all_to_all x1, blocking collectives, shards(): lax.all_to_all(send_rows, 'dp', split_axis=1, concat_axis=0, tiled=True)  52.4 us
  transfers between devices with their start and end apart: 9, of which 8 were waited for; matrix products, arithmetic and copies ran while one was open for 18% of the time, Pallas kernels for 0%

commit v1 on v0

--- a/solution.py
+++ b/solution.py
@@ -1,6 +1,8 @@
 import jax
 import jax.numpy as jnp
 from jax import lax
+from jax.experimental import pallas as pl
+from jax.experimental.pallas import tpu as pltpu
 from jax.sharding import PartitionSpec as P
 
 D = 1024
@@ -9,7 +11,487 @@
 HEAD_DIM = 64
 EXPERTS = 32
 TOP = 8
-CAP = 48
+FF = 512
+TOK = 128
+
+MESH = pl.DeviceIdType.MESH
+BF = jnp.bfloat16
+F32 = jnp.float32
+SLOTS = 48
+VMEM_BYTES = 60 * 2**20
+
+
+def wrap(value):
+    return lax.rem(value + 4, 4)
+
+
+def place():
+    dp = lax.axis_index("dp")
+    y = lax.axis_index("hid")
+    core = lax.rem(dp, 2)
+    x = lax.div(dp, 8)
+    z = lax.rem(lax.div(dp, 2), 4)
+    p = jnp.where(core == 0, x, z)
+    q = jnp.where(core == 0, z, x)
+    return p, q, y, core
+
+
+def device(p, q, y, core):
+    p, q = wrap(p), wrap(q)
+    return (jnp.where(core == 0, p * 8 + q * 2, q * 8 + p * 2) + core, wrap(y))
+
+
+def chip_of(p, q, core):
+    p, q = wrap(p), wrap(q)
+    return jnp.where(core == 0, p * 4 + q, q * 4 + p)
+
+
+def greet(devices):
+    barrier = pltpu.get_barrier_semaphore()
+    for other in devices:
+        pl.semaphore_signal(barrier, inc=1, device_id=other, device_id_type=MESH)
+    pl.semaphore_wait(barrier, len(devices))
+
+
+class Sends:
+    def __init__(self, send_sem, recv_sem):
+        self.send_sem, self.recv_sem, self.made = send_sem, recv_sem, []
+
+    def start(self, source, target, recv, to):
+        copy = pltpu.make_async_remote_copy(
+            src_ref=source,
+            dst_ref=target,
+            send_sem=self.send_sem.at[len(self.made)],
+            recv_sem=self.recv_sem.at[recv],
+            device_id=to,
+            device_id_type=MESH,
+        )
+        copy.start()
+        self.made.append(copy)
+
+    def arrived(self, ref, recv):
+        pltpu.make_async_copy(ref, ref, self.recv_sem.at[recv]).wait()
+
+    def drain(self):
+        for copy in self.made:
+            copy.wait_send()
+        self.made = []
+
+
+def slab(buffer, p, q):
+    return buffer.at[wrap(p) * 4 + wrap(q)]
+
+
+def moe_kernel(
+    x_ref, gt_ref, u_hbm, wg_hbm, wu_hbm, wd_hbm,
+    grad_out, o_hbm, gg_out, dwg_hbm, dwu_hbm, dwd_hbm,
+    xs, us, wg, wu, wd, gin, rank, ggo, picks, rows, rows_up, slot_grads, acts, gparts, uparts,
+    outs, pairs, o_buf, p_buf, rb, rc, rd, re, dwg, dwu, dwd,
+    send_sem, recv_sem, g_send, g_recv, gg_send, gg_recv, local_sem,
+):
+    p, q, y, core = place()
+    me = device(p, q, y, core)
+    right, left = device(p + 1, q, y, core), device(p - 1, q, y, core)
+    up, down = device(p, q + 1, y, core), device(p, q - 1, y, core)
+    others = [device(p + a, q + b, y, core) for a in range(4) for b in range(4) if a or b]
+    loads = [
+        pltpu.make_async_copy(src, dst, local_sem.at[i])
+        for i, (src, dst) in enumerate(((u_hbm, us), (wg_hbm, wg), (wu_hbm, wu), (wd_hbm, wd)))
+    ]
+    for load in loads:
+        load.start()
+    greet(others)
+    net = Sends(send_sem, recv_sem)
+    my_chip = chip_of(p, q, core)
+
+    own = slab(xs, p, q)
+    net.start(x_ref, own, 0, right)
+    net.start(x_ref, own, 1, left)
+    net.start(x_ref, own, 4, up)
+    net.start(x_ref, own, 8, down)
+
+    def gate_copy(i):
+        a, b = lax.div(i, 4), lax.rem(i, 4)
+        return pltpu.make_async_remote_copy(
+            src_ref=gt_ref.at[chip_of(p + a, q + b, core)],
+            dst_ref=gin.at[p * 4 + q],
+            send_sem=g_send.at[i],
+            recv_sem=g_recv.at[wrap(-a) * 4 + wrap(-b)],
+            device_id=device(p + a, q + b, y, core),
+            device_id_type=MESH,
+        )
+
+    def start_gate(i, _):
+        gate_copy(i).start()
+        return 0
+
+    lax.fori_loop(1, 16, start_gate, 0)
+    gin[p * 4 + q] = gt_ref[my_chip]
+    own[...] = x_ref[...]
+
+    s = slab(xs, p - 1, q)
+    net.arrived(s, 0)
+    net.start(s.at[0:64], s.at[0:64], 2, right)
+    net.start(s, s, 5, up)
+    s = slab(xs, p + 1, q)
+    net.arrived(s, 1)
+    net.start(s.at[64:128], s.at[64:128], 3, left)
+    net.start(s, s, 10, down)
+    s = slab(xs, p, q - 1)
+    net.arrived(s, 4)
+    net.start(s, s, 12, up)
+    s = slab(xs, p + 2, q)
+    net.arrived(s.at[0:64], 2)
+    net.arrived(s.at[64:128], 3)
+    net.start(s, s, 11, down)
+    s = slab(xs, p - 1, q - 1)
+    net.arrived(s, 5)
+    net.start(s, s, 13, up)
+    s = slab(xs, p + 1, q)
+    net.start(s, s, 6, up)
+    s = slab(xs, p + 2, q)
+    net.start(s, s, 7, up)
+    s = slab(xs, p - 1, q)
+    net.start(s, s, 9, down)
+
+    def take_gate(i, _):
+        pltpu.make_async_copy(gin.at[0], gin.at[0], g_recv.at[i]).wait()
+        return 0
+
+    lax.fori_loop(1, 16, take_gate, 0)
+    ids = lax.broadcasted_iota(jnp.int32, (TOK, TOK), 0)
+    cols = lax.broadcasted_iota(jnp.int32, (TOK, TOK), 1)
+    before = jnp.where(ids < cols, 1.0, 0.0).astype(BF)
+    routed = jnp.where(gin[...].reshape(TOK, TOK) > 0, 1.0, 0.0).astype(BF)
+    rank[...] = jnp.dot(routed, before, preferred_element_type=F32).reshape(16, 8, TOK)
+    for load in loads:
+        load.wait()
+    ggo[...] = jnp.zeros_like(ggo)
+    slot_ids = lax.broadcasted_iota(jnp.int32, (SLOTS, TOK), 0).astype(F32)
+
+    def source_of(g, j):
+        b = jnp.where(g == 0, 0, jnp.where(g == 1, 2, jnp.where(g == 2, 3, 1)))
+        a = jnp.where(j == 0, 0, jnp.where(j == 1, 3, jnp.where(j == 2, 1, 2)))
+        return wrap(p + a) * 4 + wrap(q + b)
+
+    def pick_source(g, j):
+        src = source_of(g, j)
+        token_rows, up_rows = xs[src], us[src]
+        base = pl.multiple_of(g * 4 * SLOTS + j * SLOTS, 16)
+        for e in range(2):
+            gate_row = gin[src, e : e + 1, :]
+            hit = (rank[src, e : e + 1, :] == slot_ids) & (gate_row > 0)
+            pick = jnp.where(hit, 1.0, 0.0)
+            pick_low = pick.astype(BF)
+            picks[src, e * SLOTS : (e + 1) * SLOTS, :] = pick_low
+            gate_col = jnp.sum(pick * gate_row, axis=1, keepdims=True)
+            rows[e, pl.ds(base, SLOTS), :] = jnp.dot(
+                pick_low, token_rows, preferred_element_type=F32
+            ).astype(BF)
+            picked = jnp.dot(pick_low, up_rows, preferred_element_type=F32)
+            rows_up[e, pl.ds(pl.multiple_of(j * SLOTS, 16), SLOTS), :] = picked.astype(BF)
+            slot_grads[e, pl.ds(base, SLOTS), :] = (picked * gate_col).astype(BF)
+
+    def run_expert(g, e):
+        base = pl.multiple_of(g * 4 * SLOTS, 16)
+        span = pl.ds(base, 4 * SLOTS)
+        taken = rows[e, span, :]
+        gate = jnp.dot(taken, wg[e], preferred_element_type=F32)
+        upv = jnp.dot(taken, wu[e], preferred_element_type=F32)
+        sig = 1.0 / (1.0 + jnp.exp(-gate))
+        silu = gate * sig
+        act = (silu * upv).astype(BF)
+        acts[e, span, :] = act
+        out = jnp.dot(act, wd[e], preferred_element_type=F32).astype(BF)
+        outs[e] = out
+        gg_col = jnp.sum(out.astype(F32) * rows_up[e].astype(F32), axis=1, keepdims=True)
+        for j in range(4):
+            src = source_of(g, j)
+            pick = picks[src, pl.ds(pl.multiple_of(e * SLOTS, 16), SLOTS), :].astype(F32)
+            part = gg_col[j * SLOTS : (j + 1) * SLOTS]
+            ggo[src, pl.ds(e, 1), :] = jnp.sum(pick * part, axis=0, keepdims=True)
+        grad_act = lax.dot_general(
+            slot_grads[e, span, :], wd[e], (((1,), (1,)), ((), ())), preferred_element_type=F32
+        )
+        ggp = (grad_act * upv * sig * (1.0 + gate * (1.0 - sig))).astype(BF)
+        gup = (grad_act * silu).astype(BF)
+        gparts[e, span, :] = ggp
+        uparts[e, span, :] = gup
+        pair = lax.dot_general(ggp, wg[e], (((1,), (1,)), ((), ())), preferred_element_type=F32)
+        pair += lax.dot_general(gup, wu[e], (((1,), (1,)), ((), ())), preferred_element_type=F32)
+        pairs[e] = pair.astype(BF)
+
+    def spread(g, j):
+        src = source_of(g, j)
+        pick = picks[src]
+        span = pl.ds(pl.multiple_of(j * SLOTS, 16), SLOTS)
+        gates = jnp.concatenate(
+            [
+                pick[e * SLOTS : (e + 1) * SLOTS].astype(F32) * gin[src, e : e + 1, :]
+                for e in range(2)
+            ],
+            axis=0,
+        ).astype(BF)
+        both = jnp.concatenate([outs[0, span, :], outs[1, span, :]], axis=0)
+        o_buf[src] = lax.dot_general(
+            gates, both, (((0,), (0,)), ((), ())), preferred_element_type=F32
+        ).astype(BF)
+        both = jnp.concatenate([pairs[0, span, :], pairs[1, span, :]], axis=0)
+        p_buf[src] = lax.dot_general(
+            pick, both, (((0,), (0,)), ((), ())), preferred_element_type=F32
+        ).astype(BF)
+
+    def chunk(g):
+        lax.fori_loop(0, 4, lambda j, c: (pick_source(g, j), c)[1], 0)
+        lax.fori_loop(0, 2, lambda e, c: (run_expert(g, e), c)[1], 0)
+        lax.fori_loop(0, 4, lambda j, c: (spread(g, j), c)[1], 0)
+
+    OFF = (0, -1, 1, 2)
+    R = 16
+
+    def make(source, target, recv, to, index):
+        return pltpu.make_async_remote_copy(
+            src_ref=source,
+            dst_ref=target,
+            send_sem=send_sem.at[index],
+            recv_sem=recv_sem.at[recv],
+            device_id=to,
+            device_id_type=MESH,
+        )
+
+    first = len(net.made)
+    far = [
+        lambda: make(slab(xs, p + 1, q + 1), slab(xs, p + 1, q + 1), 14, down, first),
+        lambda: make(slab(xs, p + 2, q + 1), slab(xs, p + 2, q + 1), 15, down, first + 1),
+    ]
+    bounce = [
+        (lambda j=j: make(slab(p_buf, p + OFF[j], q + 2), rb.at[j], R + j, up if j < 2 else down, first + 2 + j))
+        for j in range(4)
+    ]
+    to_down = [
+        (lambda j=j: make(slab(p_buf, p + OFF[j], q - 1), rc.at[4 + j], R + 8 + j, down, first + 6 + j))
+        for j in range(4)
+    ]
+    to_up = [
+        (lambda j=j: make(slab(p_buf, p + OFF[j], q + 1), rc.at[j], R + 4 + j, up, first + 10 + j))
+        for j in range(4)
+    ]
+
+    def add_bounce(j):
+        net.arrived(rb.at[j], R + j)
+        target = slab(p_buf, p + OFF[j], q + 1 if j < 2 else q - 1)
+        target[...] = (target[...].astype(F32) + rb[j].astype(F32)).astype(BF)
+
+    def step(g, carry):
+        @pl.when(g == 1)
+        def _():
+            net.arrived(slab(xs, p + 1, q + 1), 10)
+            far[0]().start()
+            net.arrived(slab(xs, p + 2, q + 1), 11)
+            far[1]().start()
+            net.arrived(slab(xs, p, q + 2), 12)
+            net.arrived(slab(xs, p - 1, q + 2), 13)
+            net.arrived(slab(xs, p + 1, q + 2), 14)
+            net.arrived(slab(xs, p + 2, q + 2), 15)
+
+        @pl.when(g == 2)
+        def _():
+            net.arrived(slab(xs, p + 1, q - 1), 6)
+            net.arrived(slab(xs, p + 2, q - 1), 7)
+
+        @pl.when(g == 3)
+        def _():
+            net.arrived(slab(xs, p, q + 1), 8)
+            net.arrived(slab(xs, p - 1, q + 1), 9)
+
+        chunk(g)
+
+        @pl.when(g == 1)
+        def _():
+            for j in range(4):
+                bounce[j]().start()
+
+        @pl.when(g == 2)
+        def _():
+            to_down[0]().start()
+            to_down[1]().start()
+            for j in (3, 2):
+                add_bounce(j)
+                to_down[j]().start()
+
+        @pl.when(g == 3)
+        def _():
+            to_up[3]().start()
+            to_up[2]().start()
+            for j in (1, 0):
+                add_bounce(j)
+                to_up[j]().start()
+
+        return carry
+
+    lax.fori_loop(0, 4, step, 0)
+
+    def gg_copy(i):
+        a, b = lax.div(i, 4), lax.rem(i, 4)
+        return pltpu.make_async_remote_copy(
+            src_ref=ggo.at[wrap(p + a) * 4 + wrap(q + b)],
+            dst_ref=gg_out.at[my_chip],
+            send_sem=gg_send.at[i],
+            recv_sem=gg_recv.at[wrap(-a) * 4 + wrap(-b)],
+            device_id=device(p + a, q + b, y, core),
+            device_id_type=MESH,
+        )
+
+    def start_gg(i, _):
+        gg_copy(i).start()
+        return 0
+
+    lax.fori_loop(1, 16, start_gg, 0)
+    gg_out[my_chip] = ggo[p * 4 + q]
+    o_store = pltpu.make_async_copy(o_buf, o_hbm, local_sem.at[4])
+    o_store.start()
+
+    def weight_tile(e, t):
+        cols = pl.ds(pl.multiple_of(t * 256, 256), 256)
+        dims = (((0,), (0,)), ((), ()))
+        lhs = rows[e, :, cols]
+        dwg[e, cols, :] = lax.dot_general(lhs, gparts[e], dims, preferred_element_type=F32).astype(BF)
+        dwu[e, cols, :] = lax.dot_general(lhs, uparts[e], dims, preferred_element_type=F32).astype(BF)
+        dwd[e, :, cols] = lax.dot_general(
+            acts[e], slot_grads[e, :, cols], dims, preferred_element_type=F32
+        ).astype(BF)
+
+    def weight_grads(e):
+        lax.fori_loop(0, 4, lambda t, c: (weight_tile(e, t), c)[1], 0)
+
+    weight_grads(0)
+
+    def gather_sum(j):
+        net.arrived(rc.at[j], R + 4 + j)
+        net.arrived(rc.at[4 + j], R + 8 + j)
+        target = slab(p_buf, p + OFF[j], q)
+        target[...] = (
+            target[...].astype(F32) + rc[j].astype(F32) + rc[4 + j].astype(F32)
+        ).astype(BF)
+
+    last = first + 14
+    lo, hi = pl.ds(0, 64), pl.ds(64, 64)
+    far_slab, next_slab, prev_slab = slab(p_buf, p + 2, q), slab(p_buf, p + 1, q), slab(p_buf, p - 1, q)
+    tail = [
+        make(far_slab.at[lo], rd.at[lo], R + 12, right, last),
+        make(far_slab.at[hi], rd.at[hi], R + 13, left, last + 1),
+        make(next_slab.at[hi], re.at[0, hi], R + 14, right, last + 2),
+        make(prev_slab.at[lo], re.at[1, lo], R + 15, left, last + 3),
+        make(next_slab.at[lo], re.at[0, lo], R + 16, right, last + 4),
+        make(prev_slab.at[hi], re.at[1, hi], R + 17, left, last + 5),
+    ]
+    gather_sum(3)
+    tail[0].start()
+    tail[1].start()
+    gather_sum(2)
+    tail[2].start()
+    gather_sum(1)
+    tail[3].start()
+    net.arrived(rd.at[lo], R + 12)
+    next_slab[lo] = (next_slab[lo].astype(F32) + rd[lo].astype(F32)).astype(BF)
+    tail[4].start()
+    net.arrived(rd.at[hi], R + 13)
+    prev_slab[hi] = (prev_slab[hi].astype(F32) + rd[hi].astype(F32)).astype(BF)
+    tail[5].start()
+    gather_sum(0)
+    weight_grads(1)
+    stores = [
+        pltpu.make_async_copy(src, dst, local_sem.at[i])
+        for i, (src, dst) in enumerate(((dwg, dwg_hbm), (dwu, dwu_hbm), (dwd, dwd_hbm)))
+    ]
+    for store in stores:
+        store.start()
+    net.arrived(re.at[0, hi], R + 14)
+    net.arrived(re.at[1, lo], R + 15)
+    net.arrived(re.at[0, lo], R + 16)
+    net.arrived(re.at[1, hi], R + 17)
+    grad_out[...] = slab(p_buf, p, q)[...].astype(F32) + re[0].astype(F32) + re[1].astype(F32)
+
+    def take_gg(i, _):
+        pltpu.make_async_copy(ggo.at[0], ggo.at[0], gg_recv.at[i]).wait()
+        return 0
+
+    lax.fori_loop(1, 16, take_gg, 0)
+    net.drain()
+    for copy in far + bounce + to_down + to_up:
+        copy().wait_send()
+    for copy in tail:
+        copy.wait_send()
+
+    def drain_small(i, _):
+        gate_copy(i).wait_send()
+        gg_copy(i).wait_send()
+        return 0
+
+    lax.fori_loop(1, 16, drain_small, 0)
+    o_store.wait()
+    for store in stores:
+        store.wait()
+
+
+def moe(x, gt, u, wg, wu, wd):
+    any_space = pl.BlockSpec(memory_space=pl.ANY)
+    vmem = pl.BlockSpec(memory_space=pltpu.VMEM)
+    shape = jax.ShapeDtypeStruct
+    slots = 16 * SLOTS
+    dma = pltpu.SemaphoreType.DMA
+    return pl.pallas_call(
+        moe_kernel,
+        out_shape=(
+            shape((TOK, D), F32),
+            shape((16, TOK, D), BF),
+            shape((16, 8, TOK), F32),
+            shape((2, D, FF), BF),
+            shape((2, D, FF), BF),
+            shape((2, FF, D), BF),
+        ),
+        in_specs=[vmem, vmem, any_space, any_space, any_space, any_space],
+        out_specs=(vmem, any_space, vmem, any_space, any_space, any_space),
+        scratch_shapes=[
+            pltpu.VMEM((16, TOK, D), BF),
+            pltpu.VMEM((16, TOK, D), BF),
+            pltpu.VMEM((2, D, FF), BF),
+            pltpu.VMEM((2, D, FF), BF),
+            pltpu.VMEM((2, FF, D), BF),
+            pltpu.VMEM((16, 8, TOK), F32),
+            pltpu.VMEM((16, 8, TOK), F32),
+            pltpu.VMEM((16, 8, TOK), F32),
+            pltpu.VMEM((16, 2 * SLOTS, TOK), BF),
+            pltpu.VMEM((2, slots, D), BF),
+            pltpu.VMEM((2, 4 * SLOTS, D), BF),
+            pltpu.VMEM((2, slots, D), BF),
+            pltpu.VMEM((2, slots, FF), BF),
+            pltpu.VMEM((2, slots, FF), BF),
+            pltpu.VMEM((2, slots, FF), BF),
+            pltpu.VMEM((2, 4 * SLOTS, D), BF),
+            pltpu.VMEM((2, 4 * SLOTS, D), BF),
+            pltpu.VMEM((16, TOK, D), BF),
+            pltpu.VMEM((16, TOK, D), BF),
+            pltpu.VMEM((4, TOK, D), BF),
+            pltpu.VMEM((8, TOK, D), BF),
+            pltpu.VMEM((TOK, D), BF),
+            pltpu.VMEM((2, TOK, D), BF),
+            pltpu.VMEM((2, D, FF), BF),
+            pltpu.VMEM((2, D, FF), BF),
+            pltpu.VMEM((2, FF, D), BF),
+            dma((40,)),
+            dma((34,)),
+            dma((16,)),
+            dma((16,)),
+            dma((16,)),
+            dma((16,)),
+            dma((5,)),
+        ],
+        compiler_params=pltpu.CompilerParams(
+            collective_id=1, has_side_effects=True, vmem_limit_bytes=VMEM_BYTES
+        ),
+        name="experts",
+    )(x, gt, u, wg, wu, wd)
 
 
 def rms_forward(values, gain_vector):
@@ -57,38 +539,6 @@
         ],
         axis=-1,
     )
-
-
-def expert_front(rows, gate_mat, up_mat):
-    gate_part = jnp.einsum("red,edf->ref", rows, gate_mat, preferred_element_type=jnp.float32)
-    up_part = jnp.einsum("red,edf->ref", rows, up_mat, preferred_element_type=jnp.float32)
-    act_low = (gate_part * jax.nn.sigmoid(gate_part) * up_part).astype(jnp.bfloat16)
-    return (gate_part, up_part, act_low)
-
-
-def expert_back(rows, grad_rows_in, gate_part, up_part, act_low, down_mat):
-    grad_act = jnp.einsum(
-        "red,efd->ref", grad_rows_in, down_mat, preferred_element_type=jnp.float32
-    )
-    grad_down_mat = jnp.einsum(
-        "ref,red->efd", act_low, grad_rows_in, preferred_element_type=jnp.float32
-    )
-    sigmoid_gate = jax.nn.sigmoid(gate_part)
-    grad_gate_part = (
-        grad_act * up_part * sigmoid_gate * (1.0 + gate_part * (1.0 - sigmoid_gate))
-    ).astype(jnp.bfloat16)
-    grad_up_part = (grad_act * gate_part * sigmoid_gate).astype(jnp.bfloat16)
-    grad_gate_mat = jnp.einsum(
-        "red,ref->edf", rows, grad_gate_part, preferred_element_type=jnp.float32
-    )
-    grad_up_mat = jnp.einsum("red,ref->edf", rows, grad_up_part, preferred_element_type=jnp.float32)
-    return (grad_gate_part, grad_up_part, grad_gate_mat, grad_up_mat, grad_down_mat)
-
-
-def input_grads(grad_gate_part, grad_up_part, gate_mat, up_mat):
-    return jnp.einsum(
-        "ref,edf->red", grad_gate_part, gate_mat, preferred_element_type=jnp.float32
-    ) + jnp.einsum("ref,edf->red", grad_up_part, up_mat, preferred_element_type=jnp.float32)
 
 
 def shards(
@@ -161,66 +611,50 @@
     route_onehot = (routes[:, :, None] == jnp.arange(EXPERTS, dtype=jnp.int32)).astype(jnp.float32)
     picked = jnp.sum(logits[:, None, :] * route_onehot, axis=-1)
     gate_weights = jax.nn.softmax(picked, axis=-1)
-    flat_routes = routes.reshape(-1)
-    flat_onehot = (flat_routes[:, None] == jnp.arange(EXPERTS, dtype=jnp.int32)).astype(jnp.int32)
-    slot_rank = jnp.sum((jnp.cumsum(flat_onehot, axis=0) - 1) * flat_onehot, axis=1)
-    slot_index = slot_rank * EXPERTS + flat_routes
-    slot_total = CAP * EXPERTS
-    owner_pair = (
-        jnp.full((slot_total,), tok_count * TOP, jnp.int32)
-        .at[slot_index]
-        .set(jnp.arange(tok_count * TOP, dtype=jnp.int32))
-    )
-    rows_pad = jnp.concatenate([normed_two_low, jnp.zeros((1, D), jnp.bfloat16)], axis=0)
-    send_rows = rows_pad[owner_pair // TOP].reshape(CAP, EXPERTS, D)
-    received = lax.all_to_all(send_rows, "dp", split_axis=1, concat_axis=0, tiled=True)
-    rows_all = lax.all_gather(received, "hid", axis=0, tiled=True)
-    gate_part, up_part, act_low = expert_front(rows_all, w_gate, w_up)
-    expert_out = lax.psum_scatter(
-        jnp.einsum("ref,efd->red", act_low, w_down, preferred_element_type=jnp.float32).astype(
-            jnp.bfloat16
-        ),
-        "hid",
-        scatter_dimension=0,
-        tiled=True,
-    )
-    returned = lax.all_to_all(expert_out, "dp", split_axis=0, concat_axis=1, tiled=True)
-    pair_out = returned.reshape(slot_total, D)[slot_index].reshape(tok_count, TOP, D)
-    layer_out = (hidden + jnp.sum(gate_weights[:, :, None] * pair_out, axis=1)).astype(jnp.bfloat16)
+    core_groups = [[2 * i for i in range(16)], [2 * i + 1 for i in range(16)]]
+    pair_groups = [[2 * i, 2 * i + 1] for i in range(16)]
+    dense_gates = jnp.sum(gate_weights[:, :, None] * route_onehot, axis=1)
+    gate_tiles = jnp.pad(dense_gates.T.reshape(16, 2, TOK), ((0, 0), (0, 6), (0, 0)))
     live_rows = (query_pos < lengths[0]).astype(jnp.float32)
-    upstream = cotangent.astype(jnp.float32) * live_rows[:, None]
-    grad_gates = jnp.sum(upstream[:, None, :] * pair_out, axis=-1)
+    upstream_low = jnp.where(live_rows[:, None] > 0, cotangent, jnp.zeros_like(cotangent))
+    upstream = upstream_low.astype(jnp.float32)
+    core = lax.rem(lax.axis_index("dp"), 2)
+
+    def by_place(rows):
+        rows = rows.reshape(4, 4, TOK, D)
+        return jnp.where(core == 0, rows, rows.transpose(1, 0, 2, 3)).reshape(16, TOK, D)
+
+    upstream_all = by_place(lax.all_gather(upstream_low, "dp", axis_index_groups=core_groups))
+    weights = jnp.stack([w_gate[0], w_up[0], w_down[0].T])
+    weights = lax.all_gather(weights, "hid")
+    weights = lax.all_gather(weights, "dp", axis_index_groups=pair_groups)
+    full = weights.transpose(0, 2, 3, 1, 4).reshape(2, 3, D, FF)
+    grad_rows, out_parts, grad_gates_t, part_gate, part_up, part_down = moe(
+        normed_two_low,
+        gate_tiles,
+        upstream_all,
+        full[:, 0],
+        full[:, 1],
+        full[:, 2].transpose(0, 2, 1),
+    )
+    moe_out = lax.psum_scatter(by_place(out_parts), "dp", axis_index_groups=core_groups)
+    layer_out = (hidden + moe_out.astype(jnp.float32)).astype(jnp.bfloat16)
+    parts = jnp.stack([part_gate, part_up, part_down.transpose(0, 2, 1)], axis=1)
+    parts = parts.reshape(2, 3, D, 4, TOK).transpose(0, 3, 1, 2, 4)
+    parts = lax.psum_scatter(parts, "dp", axis_index_groups=pair_groups)
+    parts = lax.psum_scatter(parts, "hid").astype(jnp.float32)
+    grad_gate, grad_up, grad_down = parts[0][None], parts[1][None], parts[2].T[None]
+    grad_gates = jnp.einsum("et,tke->tk", grad_gates_t[:, :2].reshape(EXPERTS, TOK), route_onehot, precision=lax.Precision.HIGHEST)
     grad_picked = gate_weights * (
         grad_gates - jnp.sum(gate_weights * grad_gates, axis=-1, keepdims=True)
     )
-    grad_logits = jnp.einsum("tk,tke->te", grad_picked, route_onehot).astype(jnp.bfloat16)
+    grad_logits = jnp.sum(grad_picked[:, :, None] * route_onehot, axis=1).astype(jnp.bfloat16)
     grad_router = jnp.einsum(
         "td,te->de", normed_two_low, grad_logits, preferred_element_type=jnp.float32
     )
-    slot_grads = (
-        (gate_weights[:, :, None] * upstream[:, None, :])
-        .astype(jnp.bfloat16)
-        .reshape(tok_count * TOP, D)
-    )
-    grads_pad = jnp.concatenate([slot_grads, jnp.zeros((1, D), jnp.bfloat16)], axis=0)
-    send_grads = grads_pad[owner_pair].reshape(CAP, EXPERTS, D)
-    grad_received = lax.all_to_all(send_grads, "dp", split_axis=1, concat_axis=0, tiled=True)
-    grad_all = lax.all_gather(grad_received, "hid", axis=0, tiled=True)
-    grad_gate_part, grad_up_part, grad_gate, grad_up, grad_down = expert_back(
-        rows_all, grad_all, gate_part, up_part, act_low, w_down
-    )
-    grad_rows = lax.psum_scatter(
-        input_grads(grad_gate_part, grad_up_part, w_gate, w_up).astype(jnp.bfloat16),
-        "hid",
-        scatter_dimension=0,
-        tiled=True,
-    )
-    returned_grads = lax.all_to_all(grad_rows, "dp", split_axis=0, concat_axis=1, tiled=True)
-    pair_grads = returned_grads.reshape(slot_total, D)[slot_index].reshape(tok_count, TOP, D)
-    grad_normed_two = jnp.einsum(
+    grad_normed_two = grad_rows + jnp.einsum(
         "te,de->td", grad_logits, router, preferred_element_type=jnp.float32
     )
-    grad_normed_two = grad_normed_two + jnp.sum(pair_grads.astype(jnp.float32), axis=1)
     grad_hidden_part, grad_gain_moe = rms_backward(hidden, root_moe, gain_moe, grad_normed_two)
     grad_hidden = upstream + grad_hidden_part
     grad_hidden_low = grad_hidden.astype(jnp.bfloat16)
@@ -283,7 +717,7 @@
     )
     grad_input_part, grad_gain_attn = rms_backward(inputs, root_attn, gain_attn, grad_normed)
     grad_input = grad_hidden + grad_input_part
-    counts_local = jnp.sum(flat_onehot, axis=0).astype(jnp.float32)
+    counts_local = jnp.sum(route_onehot, axis=(0, 1))
     summed = lax.psum(
         (
             grad_w_query,

time: 975 us -> 625 us (0.64)
  waiting for transfers between devices: 448 us -> 300 us
  blocking collectives: 187 us -> 91.6 us
  matrix products: 115 us -> 35.8 us
  Pallas kernels: 0 us -> 78.7 us
  local copies, waits for them, and re-layouts: 142 us -> 67.3 us
  starting transfers between devices: 16.3 us -> 0.59 us
    reduce_scatter x2, waiting for transfers between devices: 181 us -> 3.87 us  [the longest x1 3.86 us: shards(): parts = lax.psum_scatter(parts, 'dp', axis_index_groups=pair_groups)]
    all_to_all x2 -> x0, blocking collectives: 95.4 us -> none  [the longest x1 52.4 us: shards(): lax.all_to_all(send_rows, 'dp', split_axis=1, concat_axis=0, tiled=True)]
    all_gather x2 -> x3, waiting for transfers between devices: 160 us -> 71.6 us  [the longest x1 39.8 us: shards(): weights = lax.all_gather(weights, 'hid')]
    dot_general x9 -> x0, matrix products: 81.8 us -> none  [the longest x1 15.7 us: input_grads(): jnp.einsum('ref,edf->red', grad_up_part, up_mat, preferred_element_type=j...]
    pallas_call x0 -> x1, Pallas kernels: none -> 78.7 us  [moe(): pl.pallas_call(moe_kernel, out_shape=(shape((TOK, D), F32), shape((16, TO...]
    unnamed x147 -> x104, local copies, waits for them, and re-layouts: 87.1 us -> 23 us
    unnamed x8 -> x11, waiting for transfers between devices: 3.11 us -> 63.4 us
    psum x1, waiting for transfers between devices: 82.4 us -> 140 us  [shards(): lax.psum((grad_w_query, grad_w_key, grad_w_value, grad_w_output, grad_gai...]
  transfers between devices with their start and end apart: 9 -> 9, of which waited for: 8 -> 8; matrix products, arithmetic and copies ran while one was open for 18% -> 14% of each run, Pallas kernels for 0% -> 0%
where the time goes in v1:
time: 625 us; the launch traced here: 624 us
  waiting for transfers between devices  300 us (48%)
  blocking collectives  91.6 us (15%)
  Pallas kernels  78.7 us (13%)
  local copies, waits for them, and re-layouts  67.3 us (11%)
  matrix products  35.8 us (6%)
  other arithmetic  34.9 us (6%)
  between operations  15.2 us (2%)
    psum x1, waiting for transfers between devices, shards(): lax.psum((grad_w_query, grad_w_key, grad_w_value, grad_w_output, grad_gai...  140 us
    pallas_call x1, Pallas kernels, moe(): pl.pallas_call(moe_kernel, out_shape=(shape((TOK, D), F32), shape((16, TO...  78.7 us
    psum x1, blocking collectives, shards(): lax.psum((grad_w_query, grad_w_key, grad_w_value, grad_w_output, grad_gai...  68.5 us
    unnamed x11, waiting for transfers between devices  63.4 us
    all_gather x1, waiting for transfers between devices, shards(): weights = lax.all_gather(weights, 'hid')  39.8 us
    unnamed x104, local copies, waits for them, and re-layouts  23 us
    reshape x1, waiting for transfers between devices, shards(): grad_value.astype(jnp.bfloat16).reshape(tok_count, KV_HEADS * HEAD_DIM)  21.1 us
    another operation x5, local copies, waits for them, and re-layouts, shards(): jnp.stack([part_gate, part_up, part_down.transpose(0, 2, 1)], axis=1)  18.3 us
  transfers between devices with their start and end apart: 9, of which 8 were waited for; matrix products, arithmetic and copies ran while one was open for 14% of the time, Pallas kernels for 0%

profile of v1, /device:TPU:1, one launch (start us, length us, event | category | flops | bytes accessed | tf_op | source)
XLA Modules:
  0.0 623.7 jit_solution(5366714715992217485)
XLA Ops:
  7.3 1.9 copy.100
  9.2 2.2 pad_maximum_fusion
  12.7 1.7 broadcast_select_fusion
  14.5 39.8 %all-gather.9.cloned.1.call-done = bf16[12,1024,128]{2,1,0:T(8,128)(2,1)} async-done(((bf16[3,1024,128]{2,1,0:T(8,128)(2,1)}), bf16[12,1024,128]{2,1,0:T(8,128)(2,1)}) %all-gather.9.cloned.1.call-update) | async-done | bytes 3145744 | tf_op jit(solution)/shard_map/all_gather | solution.py:629
  55.6 2.2 convolution_convert_fusion.2
  57.8 1.0 copy.95
  59.1 1.4 fusion.51
  60.6 11.9 %all_gather.25 = bf16[512,8,64]{0,2,1:T(8,128)(2,1)S(1)} all-gather(bf16[128,8,64]{0,2,1:T(8,128)(2,1)S(1)} %pad_maximum_fusion.5), channel_id=1, replica_groups=mesh['dp'=32,'hid'=4] {'hid'}, dimensions={0}, use_global_device_ids=true | all-gather | bytes 655360 | tf_op jit(solution)/shard_map/all_gather | solution.py:583
  72.5 11.2 %all_gather.24 = bf16[512,8,64]{0,2,1:T(8,128)(2,1)S(1)} all-gather(bf16[128,8,64]{0,2,1:T(8,128)(2,1)S(1)} %bitcast.193), channel_id=1, replica_groups=mesh['dp'=32,'hid'=4] {'hid'}, dimensions={0}, use_global_device_ids=true | all-gather | bytes 655360 | tf_op jit(solution)/shard_map/all_gather | solution.py:584
  83.8 1.7 fusion.49
  85.7 0.8 fusion.4
  86.6 0.9 exponential_reduce_fusion
  87.5 1.0 convolution_convert_fusion.1
  92.4 16.5 %all-gather.7.cloned.1.call-done = bf16[2048,1024]{1,0:T(8,128)(2,1)} async-done(((bf16[128,1024]{1,0:T(8,128)(2,1)}), bf16[2048,1024]{1,0:T(8,128)(2,1)}) %all-gather.7.cloned.1.call-update) | async-done | bytes 4194320 | tf_op jit(solution)/shard_map/all_gather | solution.py:627
  108.9 5.9 bitcast_select_fusion.1
  114.8 15.2 %all-gather.11.cloned.1.call-done = bf16[8,3,1024,128]{3,2,1,0:T(8,128)(2,1)} async-done(((bf16[4,3,1024,128]{3,2,1,0:T(8,128)(2,1)}), bf16[8,3,1024,128]{3,2,1,0:T(8,128)(2,1)}) %all-gather.11.cloned.1.call-update) | async-done | bytes 6291472 | tf_op jit(solution)/shard_map/all_gather | solution.py:630
  130.1 8.6 %copy.101 = bf16[2,4,3,1024,128]{3,4,1,0,2:T(8,128)(2,1)} copy(bf16[2,4,3,1024,128]{4,3,2,1,0:T(8,128)(2,1)} %bitcast.170) | data formatting | bytes 12582912 | tf_op jit(solution)/shard_map/all_gather | solution.py:630
  138.7 5.7 slice_bitcast_fusion
  144.4 3.9 copy.103.wu_hbm
  148.4 3.9 copy.102.wg_hbm
  152.3 78.7 %experts.1 = (f32[128,1024]{1,0:T(8,128)}, bf16[16,128,1024]{2,1,0:T(8,128)(2,1)}, f32[16,8,128]{2,1,0:T(8,128)}, bf16[2,1024,512]{2,1,0:T(8,128)(2,1)}, bf16[2,...) custom-call(bf16[128,1024]{1,0:T(8,128)(2,1)} %copy-done.12, f32[16,8,128]{2,1,0:T(8,128)} %pad.4.gt_ref, ...), custom_call_target="tpu_custom_call" | custom-call | tf_op jit(solution)/shard_map/experts/pallas_call | solution.py:443
  231.0 5.9 bitcast_select_fusion
  237.0 4.0 stack.20
  241.0 3.3 copy.109
  244.2 4.0 stack.21
  248.2 3.2 copy.110
  251.4 3.9 copy.111
  255.3 6.6 %maximum_bitcast_fusion = bf16[2,4,3,1024,128]{4,3,2,1,0:T(8,128)(2,1)} fusion(bf16[2,1,1024,4,128]{4,2,1,3,0:T(8,128)(2,1)} %copy.111, bf16[2,1,1024,4,128]{4,2,1,3,0:T(8,128)(2,1)} %copy.110, bf16[2,1,1024,4,128]{4,2,1,3,0:T(8,128)(2,1)} %copy.109), kind=kLoop, calls=%fused_computation | loop fusion | flops 6291456 | bytes 12582912 | tf_op jit(solution)/shard_map/transpose | solution.py:643
  262.2 0.8 slice.59
  263.7 0.7 multiply_reduce_fusion.3
  265.2 1.4 convert_reduce_fusion
  266.5 2.4 multiply_reduce_fusion
  268.9 47.6 %reduce-scatter.20.cloned.1.call-done = bf16[1,128,1024]{2,1,0:T(8,128)(2,1)} async-done(((bf16[16,128,1024]{2,1,0:T(8,128)(2,1)}), bf16[1,128,1024]{2,1,0:T(8,128)(2,1)}) %reduce-scatter.20.cloned.1.call-update) | async-done | bytes 262160
  316.6 2.1 subtract_add_fusion
  318.7 0.8 convolution_convert_fusion
  319.7 3.8 fusion
  323.6 1.2 fusion.2
  324.8 0.8 fusion.6
  325.6 1.0 copy.133
  326.7 4.5 fusion.7
  331.1 2.3 copy.135
  333.5 3.9 reduce-scatter.12.cloned.1.call-done
  337.5 1.8 fusion.56
  339.9 2.8 fusion.47
  342.7 2.7 fusion.25
  345.4 15.7 %reduce-scatter.16.cloned.1.call-done = bf16[128,512]{1,0:T(8,128)(2,1)} async-done(((bf16[512,512]{1,0:T(8,128)(2,1)}), bf16[128,512]{1,0:T(8,128)(2,1)}) %reduce-scatter.16.cloned.1.call-update) | async-done | bytes 131088
  361.0 1.0 copy.134
  362.2 1.9 fusion.45
  364.0 21.1 %reduce-scatter.18.cloned.1.call-done = bf16[128,512]{1,0:T(8,128)(2,1)} async-done(((bf16[512,512]{1,0:T(8,128)(2,1)}), bf16[128,512]{1,0:T(8,128)(2,1)}) %reduce-scatter.18.cloned.1.call-update) | async-done | bytes 131088 | tf_op jit(solution)/shard_map/reshape | solution.py:703
  385.1 2.8 fusion.43
  387.9 1.6 copy-done.6
  389.5 0.8 fusion.55
  390.3 1.7 convolution_add_fusion.1
  392.7 68.5 %all-reduce.2 = (f32[1024]{0:T(1024)}, f32[1024]{0:T(1024)}, f32[32]{0:T(128)S(1)}) all-reduce(f32[1024]{0:T(1024)S(1)} %get-tuple-element.66, f32[1024]{0:T(1024)S(1)} %copy-done.40, f32[32]{0:T(128)S(1)} %copy-done.44), channel_id=1, replica_groups=mesh['dp'=32,'hid'=4] {'dp','hid'}, use_global_device_ids=true, to_apply=%region_21.22 | all-reduce | flops 2080 | bytes 16640 | tf_op jit(solution)/shard_map/psum | solution.py:721
  461.7 1.0 fusion.13
  462.7 1.3 convert_element_type.125
  464.0 1.1 slice_bitcast_fusion.3
  465.1 1.0 copy.112
  466.0 139.8 %all-reduce.6.cloned.1.call-done = (f32[1024,1024]{1,0:T(8,128)}, f32[1024,512]{1,0:T(8,128)}, f32[1024,512]{1,0:T(8,128)}, f32[1024,1024]{1,0:T(8,128)}, f32[1024,32]{0,1:T(8,128)}) async-done(((f32[1024,1024]{1,0:T(8,128)}, f32[1024,512]{1,0:T(8,128)}, f32[1024,512]{1,0:T(8,128)}, f32[1024,1024]{1,0:T(8,128)}, f32[1024,32]{0,1:T(8,128)}), (f32[1024,1024]{1,0:T(8,128)}, f32[1024,512]{1,0:T(8,128)}, ...) | async-done | bytes 12714000 | tf_op jit(solution)/shard_map/psum | solution.py:721
  605.8 4.9 copy.146
  610.8 1.3 copy.147
  612.1 1.3 copy.148
  613.4 1.1 copy-done.9
  614.5 2.0 copy.149
  (148 shorter events, 10.9 us)
Async XLA Ops:
  7.2 81.4 %copy-start = (bf16[1024,1024]{1,0:T(8,128)(2,1)S(1)}, bf16[1024,1024]{1,0:T(8,128)(2,1)}, u32[]{:S(2)}) copy-start(bf16[1024,1024]{1,0:T(8,128)(2,1)} %param.18) | copy-start | bytes 6291460
  7.2 47.2 %copy-start.4 = (bf16[128,1024]{1,0:T(8,128)(2,1)S(1)}, bf16[128,1024]{1,0:T(8,128)(2,1)}, u32[]{:S(2)}) copy-start(bf16[128,1024]{1,0:T(8,128)(2,1)} %param.14) | copy-start | bytes 786436
  7.2 48.4 %copy-start.28 = (f32[1024]{0:T(1024)S(1)}, f32[1024]{0:T(1024)}, u32[]{:S(2)}) copy-start(f32[1024]{0:T(1024)} %param.19) | copy-start | bytes 12292
  7.2 47.1 %all-gather.9.cloned.1.call-start = ((), (), s32[]{:S(2)}) async-start(), calls=%async_computation.8 | async-start | bytes 3932160 | tf_op jit(solution)/shard_map/all_gather | solution.py:629
  9.2 49.9 %copy-start.10 = (bf16[1024,512]{1,0:T(8,128)(2,1)S(1)}, bf16[1024,512]{1,0:T(8,128)(2,1)}, u32[]{:S(2)}) copy-start(bf16[1024,512]{1,0:T(8,128)(2,1)} %param.16) | copy-start | bytes 3145732
  11.4 97.5 %all-gather.7.cloned.1.call-start = ((), (), s32[]{:S(2)}) async-start(), calls=%async_computation.7 | async-start | bytes 4456448 | tf_op jit(solution)/shard_map/all_gather | solution.py:627
  12.1 0.6 copy-start.45
  14.5 115.6 %all-gather.11.cloned.1.call-start = ((), (), s32[]{:S(2)}) async-start(), calls=%async_computation.9 | async-start | bytes 9437184 | tf_op jit(solution)/shard_map/all_gather | solution.py:630
  54.4 262.2 %reduce-scatter.20.cloned.1.call-start = ((), (), s32[]{:S(2)}) async-start(), calls=%async_computation.12 | async-start | bytes 4456448
  55.1 0.5 copy-start.38
  58.9 25.0 %copy-start.5 = (bf16[1024,1024]{1,0:T(8,128)(2,1)S(1)}, bf16[1024,1024]{1,0:T(8,128)(2,1)}, u32[]{:S(2)}) copy-start(bf16[1024,1024]{1,0:T(8,128)(2,1)} %param.15) | copy-start | bytes 6291460
  59.1 27.4 %copy-start.25 = (f32[128,32]{0,1:T(8,128)}, f32[128,32]{0,1:T(8,128)S(1)}, u32[]{:S(2)}) copy-start(f32[128,32]{0,1:T(8,128)S(1)} %get-tuple-element.95) | copy-start | bytes 49156
  72.5 14.1 %copy-start.7 = (bf16[512,8,64]{0,2,1:T(8,128)(2,1)}, bf16[512,8,64]{0,2,1:T(8,128)(2,1)S(1)}, u32[]{:S(2)}) copy-start(bf16[512,8,64]{0,2,1:T(8,128)(2,1)S(1)} %all_gather.25) | copy-start | bytes 1572868
  83.7 3.8 copy-start.13
  85.7 0.9 copy-start.16
  85.7 0.9 copy-start.18
  86.5 2.0 copy-start.2
  87.4 1.7 copy-start.32
  87.5 2.7 copy-start.37
  87.5 2.8 copy-start.27
  87.5 3.0 copy-start.36
  88.6 1.1 copy-start.21
  89.7 0.5 copy-start.43
  90.3 24.5 %copy-start.12 = (bf16[128,1024]{1,0:T(8,128)(2,1)}, bf16[128,1024]{1,0:T(8,128)(2,1)S(1)}, u32[]{:S(2)}) copy-start(bf16[128,1024]{1,0:T(8,128)(2,1)S(1)} %multiply_convert_fusion.x_ref) | copy-start | bytes 786436
  90.6 24.3 %copy-start.30 = (f32[128,8]{0,1:T(8,128)}, f32[128,8]{0,1:T(8,128)S(1)}, u32[]{:S(2)}) copy-start(f32[128,8]{0,1:T(8,128)S(1)} %select_reduce_fusion.3) | copy-start | bytes 12292
  90.6 0.6 copy-start.41
  91.2 0.5 copy-start.42
  237.0 100.4 %reduce-scatter.12.cloned.1.call-start = ((), (), s32[]{:S(2)}) async-start(), calls=%async_computation.5 | async-start | bytes 9437184 | tf_op jit(solution)/shard_map/reduce_scatter | solution.py:644
  261.9 4.7 copy-start.24
  261.9 99.1 %reduce-scatter.16.cloned.1.call-start = ((), (), s32[]{:S(2)}) async-start(), calls=%async_computation.10 | async-start | bytes 655360
  266.5 2.4 copy-start.34
  268.9 50.8 %copy-start.33 = (f32[2,8,128]{2,1,0:T(8,128)S(1)}, f32[2,8,128]{2,1,0:T(8,128)}, u32[]{:S(2)}) copy-start(f32[2,8,128]{2,1,0:T(8,128)} %copy-done.32) | copy-start | bytes 24580
  319.7 3.8 copy-start.20
  319.7 3.8 copy-start.3
  323.5 1.2 copy-start.17
  323.5 1.2 copy-start.19
  326.6 10.8 %copy-start.35 = (bf16[128,32]{0,1:T(8,128)(2,1)S(1)}, bf16[128,32]{0,1:T(8,128)(2,1)}, u32[]{:S(2)}) copy-start(bf16[128,32]{0,1:T(8,128)(2,1)} %copy-done.34) | copy-start | bytes 24580
  326.6 12.6 %copy-start.8 = (bf16[512,8,64]{0,2,1:T(8,128)(2,1)S(1)}, bf16[512,8,64]{0,2,1:T(8,128)(2,1)}, u32[]{:S(2)}) copy-start(bf16[512,8,64]{0,2,1:T(8,128)(2,1)} %copy-done.7) | copy-start | bytes 1572868
  326.6 58.5 %reduce-scatter.18.cloned.1.call-start = ((), (), s32[]{:S(2)}) async-start(), calls=%async_computation.11 | async-start | bytes 655360 | tf_op jit(solution)/shard_map/reshape | solution.py:703
  331.1 8.6 %copy-start.26 = (f32[128,32]{0,1:T(8,128)S(1)}, f32[128,32]{0,1:T(8,128)}, u32[]{:S(2)}) copy-start(f32[128,32]{0,1:T(8,128)} %copy-done.25) | copy-start | bytes 49156
  333.4 6.4 %copy-start.29 = (f32[1024]{0:T(1024)S(1)}, f32[1024]{0:T(1024)}, u32[]{:S(2)}) copy-start(f32[1024]{0:T(1024)} %param.19) | copy-start | bytes 12292
  333.4 6.4 %copy-start.39 = (f32[128]{0:T(128)S(1)}, f32[128]{0:T(128)}, u32[]{:S(2)}) copy-start(f32[128]{0:T(128)} %copy-done.38) | copy-start | bytes 1540
  333.5 129.2 %reduce-scatter.14.cloned.1.call-start = ((), (), s32[]{:S(2)}) async-start(), calls=%async_computation.6 | async-start | bytes 3932160 | tf_op jit(solution)/shard_map/reduce_scatter | solution.py:645
  337.4 268.4 %all-reduce.6.cloned.1.call-start = ((), (), s32[]{:S(2)}) async-start(), calls=%async_computation.13 | async-start | bytes 25427968 | tf_op jit(solution)/shard_map/psum | solution.py:721
  339.2 3.4 copy-start.22
  387.9 1.6 copy-start.6
  389.5 2.6 copy-start.11
  389.5 2.6 copy-start.23
  389.5 3.2 copy-start.40
  389.5 3.2 copy-start.44
  389.5 72.2 %copy-start.46 = (f32[128]{0:T(128)S(1)}, f32[128]{0:T(128)}, u32[]{:S(2)}) copy-start(f32[128]{0:T(128)} %get-tuple-element.96) | copy-start | bytes 1540
  605.8 4.9 copy-start.15
  605.8 6.3 %copy-start.14 = (f32[1024,512]{1,0:T(8,128)S(1)}, f32[1024,512]{1,0:T(8,128)}, u32[]{:S(2)}) copy-start(f32[1024,512]{1,0:T(8,128)} %get-tuple-element.112) | copy-start | bytes 6291460
  610.8 3.7 copy-start.9
  612.1 5.1 copy-start.1
  614.5 2.0 copy-start.31
Sparse Core Ops, SparseCore 0:
  11.5 42.7 all-gather.8
  57.0 51.8 all-gather.6
  110.6 19.4 all-gather.10
  237.1 79.4 reduce-scatter.19
  318.9 18.3 reduce-scatter.11
  340.2 20.7 reduce-scatter.15
  364.0 21.1 reduce-scatter.17
  387.5 40.6 reduce-scatter.13
  435.4 170.4 all-reduce.5

commit v2 on v1

--- a/solution.py
+++ b/solution.py
@@ -1,5 +1,6 @@
 import jax
 import jax.numpy as jnp
+import numpy as np
 from jax import lax
 from jax.experimental import pallas as pl
 from jax.experimental.pallas import tpu as pltpu
@@ -494,6 +495,578 @@
     )(x, gt, u, wg, wu, wd)
 
 
+HALF = HEAD_DIM // 2
+SCALE = HEAD_DIM**-0.5
+
+
+def turn_tables():
+    inverse = 10000.0 ** (-np.arange(HALF, dtype=np.float32) / HALF)
+    phases = np.arange(4 * TOK, dtype=np.float32)[:, None] * inverse[None, :]
+    cosine = np.tile(np.cos(phases), (1, 4)).astype(np.float32)
+    sine = np.sin(phases)
+    sine = np.tile(np.concatenate([-sine, sine], axis=1), (1, 2)).astype(np.float32)
+    return cosine, sine
+
+
+def lanes(rows, width=128):
+    return lax.broadcasted_iota(jnp.int32, (rows, width), 1)
+
+
+def turn(chunk, cosine, sine):
+    front = lax.rem(lanes(chunk.shape[0]), HEAD_DIM) < HALF
+    swapped = jnp.where(front, pltpu.roll(chunk, 128 - HALF, 1), pltpu.roll(chunk, HALF, 1))
+    return chunk * cosine + swapped * sine
+
+
+def stack_heads(chunk, half):
+    low = lanes(chunk.shape[0]) < HEAD_DIM
+    rolled = pltpu.roll(chunk, HEAD_DIM, 1)
+    if half == 0:
+        pair = (jnp.where(low, chunk, 0.0), jnp.where(low, rolled, 0.0))
+    else:
+        pair = (jnp.where(low, 0.0, rolled), jnp.where(low, 0.0, chunk))
+    return jnp.concatenate(pair, axis=0).astype(BF)
+
+
+def unstack_heads(pair, half):
+    first, second = pair[:TOK], pair[TOK:]
+    low = lanes(TOK) < HEAD_DIM
+    if half == 0:
+        return jnp.where(low, first, pltpu.roll(second, HEAD_DIM, 1))
+    return jnp.where(low, pltpu.roll(first, HEAD_DIM, 1), second)
+
+
+def root(values):
+    return lax.rsqrt(jnp.mean(values * values, axis=1, keepdims=True) + 1e-06)
+
+
+def widen():
+    row = lax.broadcasted_iota(jnp.int32, (EXPERTS, TOK), 0)
+    lane = lax.broadcasted_iota(jnp.int32, (EXPERTS, TOK), 1)
+    return jnp.where(lane == lax.div(row, 2) * 8 + lax.rem(row, 2), 1.0, 0.0).astype(BF)
+
+
+def routed_mask(routes):
+    lane = lanes(TOK)
+    expert = jnp.where(lax.rem(lane, 8) < 2, lax.div(lane, 8) * 2 + lax.rem(lane, 8), -1)
+    hit = jnp.zeros((TOK, TOK), F32)
+    for k in range(TOP):
+        hit = hit + jnp.where(routes[:, k : k + 1] == expert, 1.0, 0.0)
+    return hit > 0
+
+
+class PlaneGather:
+    def __init__(self, net, spot, slabs, base):
+        self.net, self.spot, self.slabs, self.base = net, spot, slabs, base
+        p, q, y, core = spot
+        self.right, self.left = device(p + 1, q, y, core), device(p - 1, q, y, core)
+        self.up, self.down = device(p, q + 1, y, core), device(p, q - 1, y, core)
+
+    def slab(self, a, b):
+        return slab(self.slabs, self.spot[0] + a, self.spot[1] + b)
+
+    def send(self, ref, recv, to):
+        self.net.start(ref, ref, self.base + recv, to)
+
+    def arrived(self, ref, recv):
+        self.net.arrived(ref, self.base + recv)
+
+    def begin(self, own):
+        for recv, to in ((0, self.right), (1, self.left), (4, self.up), (8, self.down)):
+            self.net.start(own, self.slab(0, 0), self.base + recv, to)
+
+    def second(self):
+        s = self.slab(-1, 0)
+        self.arrived(s, 0)
+        self.send(s.at[0:64], 2, self.right)
+        self.send(s, 5, self.up)
+        s = self.slab(1, 0)
+        self.arrived(s, 1)
+        self.send(s.at[64:128], 3, self.left)
+        self.send(s, 10, self.down)
+
+    def third(self):
+        s = self.slab(0, -1)
+        self.arrived(s, 4)
+        self.send(s, 12, self.up)
+        s = self.slab(2, 0)
+        self.arrived(s.at[0:64], 2)
+        self.arrived(s.at[64:128], 3)
+        self.send(s, 11, self.down)
+        s = self.slab(-1, -1)
+        self.arrived(s, 5)
+        self.send(s, 13, self.up)
+        self.send(self.slab(1, 0), 6, self.up)
+        self.send(self.slab(2, 0), 7, self.up)
+        self.send(self.slab(-1, 0), 9, self.down)
+
+    def fourth(self):
+        for a, recv, far in ((1, 10, 14), (2, 11, 15)):
+            s = self.slab(a, 1)
+            self.arrived(s, recv)
+            self.send(s, far, self.down)
+
+    def finish(self):
+        for a, b, recv in (
+            (1, -1, 6), (2, -1, 7), (0, 1, 8), (-1, 1, 9),
+            (0, 2, 12), (-1, 2, 13), (1, 2, 14), (2, 2, 15),
+        ):
+            self.arrived(self.slab(a, b), recv)
+
+
+def front_kernel(
+    tok_ref, wq_hbm, wk_hbm, wv_hbm, wo_hbm, ga_ref, gm_ref, router_ref, cot_ref, routes_ref,
+    len_ref, cos_ref, sin_ref, wgs_hbm, wus_hbm, wds_hbm,
+    hidden_ref, x_ref, gt_ref, gates_ref, mixed_ref, query_ref, kv_ref, probs_hbm,
+    u_all, wg_all, wu_all, wd_all,
+    wq, wk, wv, wo, u_own, kv, probs, bias,
+    send_sem, recv_sem, local_sem,
+):
+    p, q, y, core = place()
+    spot = (p, q, y, core)
+    sibling = device(p, q, y, 1 - core)
+    sibling = (sibling[0] * 0 + chip_of(p, q, core) * 2 + 1 - core, y)
+    ahead, behind = device(p, q, y + 1, core), device(p, q, y - 1, core)
+    net = Sends(send_sem, recv_sem)
+    loads = {
+        name: pltpu.make_async_copy(src, dst, local_sem.at[i])
+        for i, (name, src, dst) in enumerate(
+            (("k", wk_hbm, wk), ("v", wv_hbm, wv), ("q", wq_hbm, wq), ("o", wo_hbm, wo))
+        )
+    }
+    for load in loads.values():
+        load.start()
+    gather = PlaneGather(net, spot, u_all, 0)
+    first = pl.multiple_of(y * TOK, TOK)
+    row = lax.broadcasted_iota(jnp.int32, (TOK, 1), 0) + y * TOK
+    length = len_ref[0]
+    u_own[...] = jnp.where(row < length, cot_ref[...].astype(F32), 0.0).astype(BF)
+    greet([gather.right, gather.left, gather.up, gather.down, ahead, behind, sibling])
+    gather.begin(u_own)
+    keep_own = pltpu.make_async_copy(u_own, gather.slab(0, 0), local_sem.at[4])
+    keep_own.start()
+
+    tokens = tok_ref[...].astype(F32)
+    normed = (tokens * root(tokens) * ga_ref[...]).astype(BF)
+    cosine, sine = cos_ref[pl.ds(first, TOK), :], sin_ref[pl.ds(first, TOK), :]
+    loads["k"].wait()
+    keys = jnp.dot(normed, wk[...], preferred_element_type=F32)
+    for c in range(4):
+        span = slice(c * 128, (c + 1) * 128)
+        kv[y, :, span] = turn(keys[:, span], cosine, sine).astype(BF)
+    loads["v"].wait()
+    kv[y, :, 512:1024] = jnp.dot(normed, wv[...], preferred_element_type=F32).astype(BF)
+    own = kv.at[y]
+    net.start(own, own, 16, ahead)
+    net.start(own, own, 17, behind)
+
+    def weight(a, e, yy, rows=None):
+        block = pl.ds(pl.multiple_of(wrap(yy) * TOK, TOK), TOK)
+        if a == 2:
+            return wd_all.at[e, block, :]
+        full = (wg_all, wu_all)[a]
+        return full.at[e, :, block] if rows is None else full.at[e, rows, block]
+
+    shards = (wgs_hbm.at[0], wus_hbm.at[0], wds_hbm.at[0])
+    top, bottom = pl.ds(0, 512), pl.ds(512, 512)
+    keep = []
+    for a in range(3):
+        net.start(shards[a], weight(a, core, y), 20 + a, ahead)
+        net.start(shards[a], weight(a, core, y), 23 + a, behind)
+        net.start(shards[a], weight(a, core, y), 30 + a, sibling)
+        keep.append(pltpu.make_async_copy(shards[a], weight(a, core, y), local_sem.at[5 + a]))
+        keep[-1].start()
+
+    loads["q"].wait()
+    queries = jnp.dot(normed, wq[...], preferred_element_type=F32)
+    for c in range(8):
+        span = slice(c * 128, (c + 1) * 128)
+        query_ref[:, span] = turn(queries[:, span], cosine, sine).astype(BF)
+    key_pos = lanes(TOK, 512)
+    bias[...] = jnp.where((key_pos <= row) & (key_pos < length), 0.0, -1e30)
+    gather.second()
+    s = kv.at[wrap(y - 1)]
+    net.arrived(s, 16)
+    net.start(s.at[0:64], s.at[0:64], 18, ahead)
+    s = kv.at[wrap(y + 1)]
+    net.arrived(s, 17)
+    net.start(s.at[64:128], s.at[64:128], 19, behind)
+    gather.third()
+    s = kv.at[wrap(y + 2)]
+    net.arrived(s.at[0:64], 18)
+    net.arrived(s.at[64:128], 19)
+
+    def attend(c, carry):
+        span = pl.ds(pl.multiple_of(c * 128, 128), 128)
+        keys = kv[:, :, span].reshape(512, 128)
+        values = kv[:, :, pl.ds(pl.multiple_of(512 + c * 128, 128), 128)].reshape(512, 128)
+        for half in range(2):
+            m = c * 2 + half
+            mine = pl.ds(pl.multiple_of(m * 128, 128), 128)
+            pair = stack_heads(query_ref[:, mine].astype(F32), half)
+            scores = lax.dot_general(
+                pair, keys, (((1,), (1,)), ((), ())), preferred_element_type=F32
+            )
+            scores = scores * SCALE + jnp.concatenate([bias[...], bias[...]], axis=0)
+            scores = jnp.exp(scores - jnp.max(scores, axis=1, keepdims=True))
+            low = (scores * (1.0 / jnp.sum(scores, axis=1, keepdims=True))).astype(BF)
+            probs[m] = low
+            out = jnp.dot(low, values, preferred_element_type=F32)
+            mixed_ref[:, mine] = unstack_heads(out, half).astype(BF)
+        return carry
+
+    lax.fori_loop(0, 2, attend, 0)
+    gather.fourth()
+    for a in range(3):
+        net.arrived(weight(a, core, y - 1), 20 + a)
+    net.start(weight(0, core, y - 1), weight(0, core, y - 1), 26, ahead)
+    net.start(weight(1, core, y - 1, top), weight(1, core, y - 1, top), 27, ahead)
+    for a in range(3):
+        net.arrived(weight(a, core, y + 1), 23 + a)
+    net.start(weight(1, core, y + 1, bottom), weight(1, core, y + 1, bottom), 28, behind)
+    net.start(weight(2, core, y + 1), weight(2, core, y + 1), 29, behind)
+    for a in range(3):
+        net.start(weight(a, core, y - 1), weight(a, core, y - 1), 33 + a, sibling)
+        net.start(weight(a, core, y + 1), weight(a, core, y + 1), 36 + a, sibling)
+    lax.fori_loop(2, 4, attend, 0)
+    keep_probs = pltpu.make_async_copy(probs, probs_hbm, local_sem.at[8])
+    keep_probs.start()
+    loads["o"].wait()
+    hidden = tokens + jnp.dot(mixed_ref[...], wo[...], preferred_element_type=F32)
+    hidden_ref[...] = hidden
+    x = (hidden * root(hidden) * gm_ref[...]).astype(BF)
+    x_ref[...] = x
+    wide = jnp.dot(router_ref[...], widen(), preferred_element_type=F32).astype(BF)
+    logits = jnp.dot(x, wide, preferred_element_type=F32)
+    routed = routed_mask(routes_ref[...])
+    logits = jnp.where(routed, logits, -1e30)
+    weights = jnp.where(routed, jnp.exp(logits - jnp.max(logits, axis=1, keepdims=True)), 0.0)
+    weights = weights * (1.0 / jnp.sum(weights, axis=1, keepdims=True))
+    gates_ref[...] = weights
+    gt_ref[...] = weights.T.reshape(16, 8, TOK)
+    kv_ref[...] = kv[...]
+
+    net.arrived(weight(0, core, y + 2), 26)
+    net.arrived(weight(1, core, y + 2, top), 27)
+    net.arrived(weight(1, core, y + 2, bottom), 28)
+    net.arrived(weight(2, core, y + 2), 29)
+    for a in range(3):
+        net.start(weight(a, core, y + 2), weight(a, core, y + 2), 39 + a, sibling)
+    gather.finish()
+    for i, step in enumerate((0, -1, 1, 2)):
+        for a in range(3):
+            net.arrived(weight(a, 1 - core, y + step), 30 + 3 * i + a)
+    net.drain()
+    keep_own.wait()
+    keep_probs.wait()
+    for copy in keep:
+        copy.wait()
+
+
+def front(tokens, wq, wk, wv, wo, ga, gm, router, cotangent, routes, lengths, wg, wu, wd):
+    cosine, sine = turn_tables()
+    any_space = pl.BlockSpec(memory_space=pl.ANY)
+    vmem = pl.BlockSpec(memory_space=pltpu.VMEM)
+    smem = pl.BlockSpec(memory_space=pltpu.SMEM)
+    shape = jax.ShapeDtypeStruct
+    dma = pltpu.SemaphoreType.DMA
+    return pl.pallas_call(
+        front_kernel,
+        out_shape=(
+            shape((TOK, D), F32),
+            shape((TOK, D), BF),
+            shape((16, 8, TOK), F32),
+            shape((TOK, TOK), F32),
+            shape((TOK, D), BF),
+            shape((TOK, D), BF),
+            shape((4, TOK, D), BF),
+            shape((8, 2 * TOK, 512), BF),
+            shape((16, TOK, D), BF),
+            shape((2, D, FF), BF),
+            shape((2, D, FF), BF),
+            shape((2, FF, D), BF),
+        ),
+        in_specs=[vmem] + [any_space] * 4 + [vmem] * 5 + [smem] + [vmem] * 2 + [any_space] * 3,
+        out_specs=(vmem,) * 7 + (any_space,) * 5,
+        scratch_shapes=[
+            pltpu.VMEM((D, D), BF),
+            pltpu.VMEM((D, 512), BF),
+            pltpu.VMEM((D, 512), BF),
+            pltpu.VMEM((D, D), BF),
+            pltpu.VMEM((TOK, D), BF),
+            pltpu.VMEM((4, TOK, D), BF),
+            pltpu.VMEM((8, 2 * TOK, 512), BF),
+            pltpu.VMEM((TOK, 512), F32),
+            dma((52,)),
+            dma((42,)),
+            dma((9,)),
+        ],
+        compiler_params=pltpu.CompilerParams(
+            collective_id=3, has_side_effects=True, vmem_limit_bytes=VMEM_BYTES
+        ),
+        name="front",
+    )(
+        tokens, wq, wk, wv, wo, ga.reshape(1, D), gm.reshape(1, D), router, cotangent, routes,
+        lengths, jnp.asarray(cosine), jnp.asarray(sine), wg, wu, wd,
+    )
+
+
+def total_kernel(
+    a_hbm, b_hbm, c_hbm, s_hbm, a_out, b_out, c_out, s_out,
+    mine, other, mine_s, other_s, from_low, from_high, from_low_s, from_high_s, bounced, bounced_s,
+    spread, spread_s, done, done_s,
+    sib_send, sib_recv, ring_send, ring_recv, plane_send, plane_recv, back_send, back_recv,
+    round_send, round_recv, last_send, last_recv, local_sem,
+):
+    dp, y = lax.axis_index("dp"), lax.axis_index("hid")
+    core = lax.rem(dp, 2)
+    here = (lax.div(dp, 8), y, lax.rem(lax.div(dp, 2), 4))
+
+    def at(spot, on=None):
+        spot = [wrap(v) for v in spot]
+        return (spot[0] * 8 + spot[2] * 2 + (core if on is None else on), spot[1])
+
+    def along(k, step):
+        return at([here[i] + (step if i == k else 0) for i in range(3)])
+
+    sibling = at(here, 1 - core)
+    ring = [(along(k, 1), along(k, -1)) for k in range(3)]
+    planes = [(1, 2), (0, 2), (0, 1)]
+    greeted = [sibling]
+    for dx in range(4):
+        for dy in range(4):
+            for dz in range(4):
+                if (dx or dy or dz) and not (dx and dy and dz):
+                    greeted.append(at([here[0] + dx, here[1] + dy, here[2] + dz]))
+    ins, results = (a_hbm, b_hbm, c_hbm, s_hbm), (a_out, b_out, c_out, s_out)
+    axes = (0, 1, 2, 0)
+    halves = [mine.at[k] for k in range(3)] + [mine_s]
+    theirs = [other.at[k] for k in range(3)] + [other_s]
+    lows = [from_low.at[k] for k in range(3)] + [from_low_s]
+    highs = [from_high.at[k] for k in range(3)] + [from_high_s]
+    hops = [bounced.at[k] for k in range(3)] + [bounced_s]
+    pieces = [spread.at[k] for k in range(3)] + [spread_s]
+    slabs = [done.at[k] for k in range(3)] + [done_s]
+    parts = range(4)
+    own_rows = pl.ds(pl.multiple_of(core * 512, 512), 512)
+    their_rows = pl.ds(pl.multiple_of((1 - core) * 512, 512), 512)
+
+    def remote(source, target, send, recv, to):
+        return pltpu.make_async_remote_copy(
+            src_ref=source, dst_ref=target, send_sem=send, recv_sem=recv,
+            device_id=to, device_id_type=MESH,
+        )
+
+    def arrived(ref, sem):
+        pltpu.make_async_copy(ref, ref, sem).wait()
+
+    loads = [
+        pltpu.make_async_copy(ins[k].at[own_rows], halves[k], local_sem.at[k]) for k in parts
+    ]
+    for load in loads:
+        load.start()
+    greet(greeted)
+    sent = []
+
+    def go(*copy):
+        copy = remote(*copy)
+        copy.start()
+        sent.append(copy)
+
+    for k in parts:
+        go(ins[k].at[their_rows], theirs[k], sib_send.at[k], sib_recv.at[k], sibling)
+
+    def rows_of(k, step):
+        start = pl.multiple_of(wrap(here[axes[k]] + step) * 128, 128)
+        return halves[k].at[pl.ds(start, 128)]
+
+    lo, hi = pl.ds(0, 64), pl.ds(64, 64)
+
+    def add(target, *terms):
+        total = target[...].astype(F32)
+        for term in terms:
+            total += term[...].astype(F32)
+        target[...] = total.astype(target.dtype)
+
+    def merge_rows(k, step):
+        start = pl.multiple_of(wrap(here[axes[k]] + step) * 128, 128)
+        span = pl.ds(start, 128)
+        add(halves[k].at[span], theirs[k].at[span])
+
+    for k in parts:
+        loads[k].wait()
+        arrived(theirs[k], sib_recv.at[k])
+        plus, minus = ring[axes[k]]
+        merge_rows(k, 2)
+        far = rows_of(k, 2)
+        go(far.at[lo], hops[k].at[lo], ring_send.at[k, 0], ring_recv.at[k, 0], plus)
+        go(far.at[hi], hops[k].at[hi], ring_send.at[k, 1], ring_recv.at[k, 1], minus)
+        merge_rows(k, 1)
+        go(rows_of(k, 1).at[hi], lows[k].at[hi], ring_send.at[k, 2], ring_recv.at[k, 2], plus)
+        merge_rows(k, -1)
+        go(rows_of(k, -1).at[lo], highs[k].at[lo], ring_send.at[k, 3], ring_recv.at[k, 3], minus)
+        merge_rows(k, 0)
+    for k in parts:
+        plus, minus = ring[axes[k]]
+        arrived(hops[k].at[lo], ring_recv.at[k, 0])
+        near = rows_of(k, 1).at[lo]
+        add(near, hops[k].at[lo])
+        go(near, lows[k].at[lo], ring_send.at[k, 4], ring_recv.at[k, 4], plus)
+        arrived(hops[k].at[hi], ring_recv.at[k, 1])
+        near = rows_of(k, -1).at[hi]
+        add(near, hops[k].at[hi])
+        go(near, highs[k].at[hi], ring_send.at[k, 5], ring_recv.at[k, 5], minus)
+
+    def piece(k, ref, u, v):
+        if k == 3:
+            return ref.at[pl.ds(pl.multiple_of((u * 4 + v) * 8, 8), 8)]
+        return ref.at[
+            pl.ds(pl.multiple_of(u * 32, 32), 32), pl.ds(pl.multiple_of(v * 256, 256), 256)
+        ]
+
+    def member(k, i):
+        u, v = planes[axes[k]]
+        spot = list(here)
+        spot[u] = wrap(here[u] + lax.div(i, 4))
+        spot[v] = wrap(here[v] + lax.rem(i, 4))
+        return spot[u], spot[v], at(spot)
+
+    def mirror(i):
+        return wrap(-lax.div(i, 4)) * 4 + wrap(-lax.rem(i, 4))
+
+    def piece_copy(k, i):
+        u, v, to = member(k, i)
+        return remote(
+            piece(k, rows_of(k, 0), u, v),
+            pieces[k].at[mirror(i)],
+            plane_send.at[k, i],
+            plane_recv.at[k, mirror(i)],
+            to,
+        )
+
+    def back_copy(k, i):
+        u, v = planes[axes[k]]
+        spot = piece(k, slabs[k], here[u], here[v])
+        return remote(spot, spot, back_send.at[k, i], back_recv.at[k, mirror(i)], member(k, i)[2])
+
+    def each(make, act):
+        def one(i, carry):
+            act(make(i))
+            return carry
+
+        lax.fori_loop(1, 16, one, 0)
+
+    for k in parts:
+        for i in (2, 4):
+            arrived(lows[k].at[hi if i == 2 else lo], ring_recv.at[k, i])
+        for i in (3, 5):
+            arrived(highs[k].at[lo if i == 3 else hi], ring_recv.at[k, i])
+        add(rows_of(k, 0), lows[k], highs[k])
+        each(lambda i: piece_copy(k, i), lambda copy: copy.start())
+    for k in parts:
+        u, v = planes[axes[k]]
+        pieces[k][0] = piece(k, rows_of(k, 0), here[u], here[v])[...]
+        each(
+            lambda i: pltpu.make_async_copy(pieces[k].at[0], pieces[k].at[0], plane_recv.at[k, i]),
+            lambda copy: copy.wait(),
+        )
+        total = jnp.sum(pieces[k][...].astype(F32), axis=0)
+        piece(k, slabs[k], here[u], here[v])[...] = total.astype(slabs[k].dtype)
+        each(lambda i: back_copy(k, i), lambda copy: copy.start())
+
+    def final(k, step, span=None):
+        start = pl.multiple_of(core * 512 + wrap(here[axes[k]] + step) * 128, 128)
+        if span is not None:
+            start, size = start + span, 64
+        else:
+            size = 128
+        return results[k].at[pl.ds(pl.multiple_of(start, 64), size)]
+
+    stores = []
+    for k in parts:
+        plus, minus = ring[axes[k]]
+        each(
+            lambda i: pltpu.make_async_copy(pieces[k].at[0], pieces[k].at[0], back_recv.at[k, i]),
+            lambda copy: copy.wait(),
+        )
+        go(slabs[k], final(k, 0), round_send.at[k, 0], round_recv.at[k, 0], plus)
+        go(slabs[k], final(k, 0), round_send.at[k, 1], round_recv.at[k, 1], minus)
+        go(slabs[k], final(k, 0), last_send.at[k, 0], last_recv.at[k, 0], sibling)
+        store = pltpu.make_async_copy(slabs[k], final(k, 0), local_sem.at[k])
+        store.start()
+        stores.append(store)
+    for k in parts:
+        plus, minus = ring[axes[k]]
+        arrived(final(k, -1), round_recv.at[k, 0])
+        spot = final(k, -1, 0)
+        go(spot, spot, round_send.at[k, 2], round_recv.at[k, 2], plus)
+        go(final(k, -1), final(k, -1), last_send.at[k, 1], last_recv.at[k, 1], sibling)
+        arrived(final(k, 1), round_recv.at[k, 1])
+        spot = final(k, 1, 64)
+        go(spot, spot, round_send.at[k, 3], round_recv.at[k, 3], minus)
+        go(final(k, 1), final(k, 1), last_send.at[k, 2], last_recv.at[k, 2], sibling)
+    for k in parts:
+        arrived(final(k, 2, 0), round_recv.at[k, 2])
+        arrived(final(k, 2, 64), round_recv.at[k, 3])
+        go(final(k, 2), final(k, 2), last_send.at[k, 3], last_recv.at[k, 3], sibling)
+    for k in parts:
+        for i in range(4):
+            arrived(final(k, 0), last_recv.at[k, i])
+    for copy in sent:
+        copy.wait_send()
+    for k in parts:
+        each(lambda i: piece_copy(k, i), lambda copy: copy.wait_send())
+        each(lambda i: back_copy(k, i), lambda copy: copy.wait_send())
+    for store in stores:
+        store.wait()
+
+
+def total(a, b, c, s):
+    any_space = pl.BlockSpec(memory_space=pl.ANY)
+    shape = jax.ShapeDtypeStruct
+    dma = pltpu.SemaphoreType.DMA
+    vmem = pltpu.VMEM
+    return pl.pallas_call(
+        total_kernel,
+        out_shape=(shape((D, D), BF),) * 3 + (shape((D, TOK), F32),),
+        in_specs=[any_space] * 4,
+        out_specs=(any_space,) * 4,
+        scratch_shapes=[
+            vmem((3, 512, D), BF),
+            vmem((3, 512, D), BF),
+            vmem((512, TOK), F32),
+            vmem((512, TOK), F32),
+            vmem((3, 128, D), BF),
+            vmem((3, 128, D), BF),
+            vmem((128, TOK), F32),
+            vmem((128, TOK), F32),
+            vmem((3, 128, D), BF),
+            vmem((128, TOK), F32),
+            vmem((3, 16, 32, 256), BF),
+            vmem((16, 8, TOK), F32),
+            vmem((3, 128, D), BF),
+            vmem((128, TOK), F32),
+            dma((4,)),
+            dma((4,)),
+            dma((4, 6)),
+            dma((4, 6)),
+            dma((4, 16)),
+            dma((4, 16)),
+            dma((4, 16)),
+            dma((4, 16)),
+            dma((4, 4)),
+            dma((4, 4)),
+            dma((4, 4)),
+            dma((4, 4)),
+            dma((4,)),
+        ],
+        compiler_params=pltpu.CompilerParams(
+            collective_id=2, has_side_effects=True, vmem_limit_bytes=VMEM_BYTES
+        ),
+        name="total",
+    )(a, b, c, s)
+
+
 def rms_forward(values, gain_vector):
     inverse_root = lax.rsqrt(jnp.mean(values * values, axis=-1, keepdims=True) + 1e-06)
     return (values * inverse_root * gain_vector, inverse_root)
@@ -566,55 +1139,26 @@
     normed, root_attn = rms_forward(inputs, gain_attn)
     normed_low = normed.astype(jnp.bfloat16)
     sine_table, cosine_table = rope_tables(first_pos, tok_count, HEAD_DIM)
-    query_raw = jnp.dot(normed_low, w_query, preferred_element_type=jnp.float32).reshape(
-        tok_count, HEADS, HEAD_DIM
-    )
-    key_raw = jnp.dot(normed_low, w_key, preferred_element_type=jnp.float32).reshape(
-        tok_count, KV_HEADS, HEAD_DIM
-    )
-    value_low = (
-        jnp.dot(normed_low, w_value, preferred_element_type=jnp.float32)
-        .astype(jnp.bfloat16)
-        .reshape(tok_count, KV_HEADS, HEAD_DIM)
-    )
-    query_low = rotate(query_raw, sine_table, cosine_table).astype(jnp.bfloat16)
-    key_low = rotate(key_raw, sine_table, cosine_table).astype(jnp.bfloat16)
-    keys_all, values_all = (
-        lax.all_gather(key_low, "hid", axis=0, tiled=True),
-        lax.all_gather(value_low, "hid", axis=0, tiled=True),
-    )
-    seq_count = keys_all.shape[0]
+    (
+        hidden, normed_two_low, gate_tiles, gates, mixed_low, query_low, kv, probs,
+        upstream_all, full_gate, full_up, full_down,
+    ) = front(
+        tokens, w_query, w_key, w_value, w_output, gain_attn, gain_moe, router, cotangent, routes,
+        lengths, w_gate, w_up, w_down,
+    )
+    root_moe = lax.rsqrt(jnp.mean(hidden * hidden, axis=-1, keepdims=True) + 1e-06)
+    route_onehot = (routes[:, :, None] == jnp.arange(EXPERTS, dtype=jnp.int32)).astype(jnp.float32)
+    kv = kv.reshape(512, D)
+    keys_all = kv[:, :512].reshape(512, KV_HEADS, HEAD_DIM)
+    values_all = kv[:, 512:].reshape(512, KV_HEADS, HEAD_DIM)
     grouped = query_low.reshape(tok_count, KV_HEADS, group_size, HEAD_DIM)
     query_pos = hid_pos * tok_count + jnp.arange(tok_count, dtype=jnp.int32)
-    key_pos = jnp.arange(seq_count, dtype=jnp.int32)
-    allowed = (key_pos[None, :] <= query_pos[:, None]) & (key_pos[None, :] < lengths[0])
-
-    def masked_scores():
-        raw_scores = (
-            jnp.einsum("tkgd,skd->kgts", grouped, keys_all, preferred_element_type=jnp.float32)
-            * score_scale
-        )
-        return jnp.where(allowed, raw_scores, -1e30)
-
-    masked = masked_scores()
-    top_score = jnp.max(masked, axis=-1, keepdims=True)
-    log_total = top_score + jnp.log(jnp.sum(jnp.exp(masked - top_score), axis=-1, keepdims=True))
-    softmaxed_low = jnp.exp(masked - log_total).astype(jnp.bfloat16)
-    mixed_low = jnp.einsum(
-        "kgts,skd->tkgd", softmaxed_low, values_all, preferred_element_type=jnp.float32
-    )
-    mixed_low = mixed_low.reshape(tok_count, HEADS * HEAD_DIM).astype(jnp.bfloat16)
-    hidden = inputs + jnp.dot(mixed_low, w_output, preferred_element_type=jnp.float32)
-    normed_two, root_moe = rms_forward(hidden, gain_moe)
-    normed_two_low = normed_two.astype(jnp.bfloat16)
-    logits = jnp.dot(normed_two_low, router, preferred_element_type=jnp.float32)
-    route_onehot = (routes[:, :, None] == jnp.arange(EXPERTS, dtype=jnp.int32)).astype(jnp.float32)
-    picked = jnp.sum(logits[:, None, :] * route_onehot, axis=-1)
-    gate_weights = jax.nn.softmax(picked, axis=-1)
+    score_scale = HEAD_DIM ** (-0.5)
+    softmaxed_low = probs.reshape(KV_HEADS, group_size, tok_count, 512)
+    softmaxed = softmaxed_low.astype(jnp.float32)
+    gate_weights = jnp.sum(gates.reshape(tok_count, 16, 8)[:, :, :2].reshape(tok_count, 1, EXPERTS) * route_onehot, axis=-1)
     core_groups = [[2 * i for i in range(16)], [2 * i + 1 for i in range(16)]]
     pair_groups = [[2 * i, 2 * i + 1] for i in range(16)]
-    dense_gates = jnp.sum(gate_weights[:, :, None] * route_onehot, axis=1)
-    gate_tiles = jnp.pad(dense_gates.T.reshape(16, 2, TOK), ((0, 0), (0, 6), (0, 0)))
     live_rows = (query_pos < lengths[0]).astype(jnp.float32)
     upstream_low = jnp.where(live_rows[:, None] > 0, cotangent, jnp.zeros_like(cotangent))
     upstream = upstream_low.astype(jnp.float32)
@@ -624,18 +1168,13 @@
         rows = rows.reshape(4, 4, TOK, D)
         return jnp.where(core == 0, rows, rows.transpose(1, 0, 2, 3)).reshape(16, TOK, D)
 
-    upstream_all = by_place(lax.all_gather(upstream_low, "dp", axis_index_groups=core_groups))
-    weights = jnp.stack([w_gate[0], w_up[0], w_down[0].T])
-    weights = lax.all_gather(weights, "hid")
-    weights = lax.all_gather(weights, "dp", axis_index_groups=pair_groups)
-    full = weights.transpose(0, 2, 3, 1, 4).reshape(2, 3, D, FF)
     grad_rows, out_parts, grad_gates_t, part_gate, part_up, part_down = moe(
         normed_two_low,
         gate_tiles,
         upstream_all,
-        full[:, 0],
-        full[:, 1],
-        full[:, 2].transpose(0, 2, 1),
+        full_gate,
+        full_up,
+        full_down,
     )
     moe_out = lax.psum_scatter(by_place(out_parts), "dp", axis_index_groups=core_groups)
     layer_out = (hidden + moe_out.astype(jnp.float32)).astype(jnp.bfloat16)
@@ -665,7 +1204,6 @@
         "td,fd->tf", grad_hidden_low, w_output, preferred_element_type=jnp.float32
     )
     grad_mixed = grad_mixed.astype(jnp.bfloat16).reshape(tok_count, KV_HEADS, group_size, HEAD_DIM)
-    softmaxed = jnp.exp(masked_scores() - log_total)
     grad_probs = jnp.einsum(
         "tkgd,skd->kgts", grad_mixed, values_all, preferred_element_type=jnp.float32
     )
@@ -718,34 +1256,37 @@
     grad_input_part, grad_gain_attn = rms_backward(inputs, root_attn, gain_attn, grad_normed)
     grad_input = grad_hidden + grad_input_part
     counts_local = jnp.sum(route_onehot, axis=(0, 1))
-    summed = lax.psum(
-        (
-            grad_w_query,
-            grad_w_key,
-            grad_w_value,
-            grad_w_output,
-            grad_gain_attn,
-            grad_gain_moe,
+    narrow = jnp.concatenate(
+        [
             grad_router,
-            counts_local,
-        ),
-        ("dp", "hid"),
-    )
-    counts = summed[7].astype(jnp.int32)
+            grad_gain_attn[:, None],
+            grad_gain_moe[:, None],
+            jnp.pad(counts_local, (0, D - EXPERTS))[:, None],
+            jnp.zeros((D, TOK - EXPERTS - 3), jnp.float32),
+        ],
+        axis=1,
+    )
+    sum_q, sum_o, sum_kv, narrow = total(
+        grad_w_query.astype(BF),
+        grad_w_output.astype(BF),
+        jnp.concatenate([grad_w_key, grad_w_value], axis=1).astype(BF),
+        narrow,
+    )
+    sum_kv = sum_kv.astype(jnp.float32)
     return (
         layer_out,
         grad_input,
-        summed[0],
-        summed[1],
-        summed[2],
-        summed[3],
-        summed[4],
-        summed[5],
-        summed[6],
+        sum_q.astype(jnp.float32),
+        sum_kv[:, :512],
+        sum_kv[:, 512:],
+        sum_o.astype(jnp.float32),
+        narrow[:, EXPERTS],
+        narrow[:, EXPERTS + 1],
+        narrow[:, :EXPERTS],
         grad_gate,
         grad_up,
         grad_down,
-        counts,
+        narrow[:EXPERTS, EXPERTS + 2].astype(jnp.int32),
     )
 
 

time: 625 us -> 401 us (0.64)
  waiting for transfers between devices: 300 us -> 85.8 us
  Pallas kernels: 78.7 us -> 203 us
  blocking collectives: 91.6 us -> 0 us
  local copies, waits for them, and re-layouts: 67.3 us -> 42.4 us
  matrix products: 35.8 us -> 22.8 us
    psum x1 -> x0, waiting for transfers between devices: 140 us -> none  [shards(): lax.psum((grad_w_query, grad_w_key, grad_w_value, grad_w_output, grad_gai...]
    pallas_call x0 -> x2, Pallas kernels: none -> 125 us  [the longest x1 72.8 us: total(): pl.pallas_call(total_kernel, out_shape=(shape((D, D), BF),) * 3 + (shape(...]
    all_gather x3 -> x0, waiting for transfers between devices: 71.6 us -> none  [the longest x1 39.8 us: shards(): weights = lax.all_gather(weights, 'hid')]
    psum x1 -> x0, blocking collectives: 68.5 us -> none  [shards(): lax.psum((grad_w_query, grad_w_key, grad_w_value, grad_w_output, grad_gai...]
    all_gather x2 -> x0, blocking collectives: 23.1 us -> none  [the longest x1 11.9 us: shards(): lax.all_gather(key_low, 'hid', axis=0, tiled=True)]
    unnamed x104 -> x59, local copies, waits for them, and re-layouts: 23 us -> 10.4 us
    slice x0 -> x6, local copies, waits for them, and re-layouts: none -> 8.76 us  [the longest x2 3.9 us: shards(): values_all = kv[:, 512:].reshape(512, KV_HEADS, HEAD_DIM)]
    all_gather x1 -> x0, local copies, waits for them, and re-layouts: 8.64 us -> none  [shards(): weights = lax.all_gather(weights, 'dp', axis_index_groups=pair_groups)]
  transfers between devices with their start and end apart: 9 -> 5, of which waited for: 8 -> 4; matrix products, arithmetic and copies ran while one was open for 14% -> 21% of each run, Pallas kernels for 0% -> 18%
where the time goes in v2:
time: 401 us; the launch traced here: 400 us
  Pallas kernels  203 us (51%)
  waiting for transfers between devices  85.8 us (21%)
  local copies, waits for them, and re-layouts  42.4 us (11%)
  other arithmetic  30.4 us (8%)
  matrix products  22.8 us (6%)
  between operations  14.8 us (4%)
    pallas_call x1, Pallas kernels, moe(): pl.pallas_call(moe_kernel, out_shape=(shape((TOK, D), F32), shape((16, TO...  77.5 us
    pallas_call x1, Pallas kernels, total(): pl.pallas_call(total_kernel, out_shape=(shape((D, D), BF),) * 3 + (shape(...  72.8 us
    unnamed x7, waiting for transfers between devices  60.5 us
    pallas_call x1, Pallas kernels, front(): pl.pallas_call(front_kernel, out_shape=(shape((TOK, D), F32), shape((TOK,...  52.7 us
    reshape x1, waiting for transfers between devices, shards(): grad_value.astype(jnp.bfloat16).reshape(tok_count, KV_HEADS * HEAD_DIM)  20.8 us
    another operation x5, local copies, waits for them, and re-layouts, shards(): jnp.stack([part_gate, part_up, part_down.transpose(0, 2, 1)], axis=1)  12.4 us
    unnamed x59, local copies, waits for them, and re-layouts  10.4 us
  transfers between devices with their start and end apart: 5, of which 4 were waited for; matrix products, arithmetic and copies ran while one was open for 21% of the time, Pallas kernels for 18%

profile of v2, /device:TPU:1, one launch (start us, length us, event | category | flops | bytes accessed | tf_op | source)
XLA Modules:
  0.0 399.6 jit_solution(12106952927006241522)
XLA Ops:
  7.9 1.7 copy.96.router_ref
  9.6 1.4 copy.97.routes_ref
  11.0 52.7 %front.1 = (f32[128,1024]{1,0:T(8,128)}, bf16[128,1024]{1,0:T(8,128)(2,1)}, f32[16,8,128]{2,1,0:T(8,128)}, f32[128,128]{1,0:T(8,128)}, bf16[128,1024]{1,0:T(8,12...) custom-call(bf16[128,1024]{1,0:T(8,128)(2,1)} %tok_ref.1, ...), custom_call_target="tpu_custom_call" | custom-call | tf_op jit(solution)/shard_map/front/pallas_call | solution.py:773
  63.6 77.5 %experts.1 = (f32[128,1024]{1,0:T(8,128)}, bf16[16,128,1024]{2,1,0:T(8,128)(2,1)}, f32[16,8,128]{2,1,0:T(8,128)}, bf16[2,1024,512]{2,1,0:T(8,128)(2,1)}, bf16[2,...) custom-call(bf16[128,1024]{1,0:T(8,128)(2,1)} %get-tuple-element.36.x_ref, f32[16,8,128]{2,1,0:T(8,128)} %get-tuple-element.37.gt_ref, ...), custom_call_target="tpu_custom_call" | custom-call | tf_op jit(solution)/shard_map/experts/pallas_call | solution.py:444
  141.2 5.9 %bitcast_select_fusion = bf16[4,4,128,1024]{3,2,1,0:T(8,128)(2,1)} fusion(bf16[4,4,128,1024]{3,2,1,0:T(8,128)(2,1)} %bitcast.116, pred[]{:T(512)S(6)} %eq.16), kind=kLoop, calls=%fused_computation.6 | loop fusion | flops 2097152 | bytes 8388609 | tf_op jit(solution)/shard_map/jit(_where)/select_n | solution.py:1169
  147.2 2.6 stack.12
  149.7 1.6 copy.113
  151.3 2.5 stack.13
  153.9 1.6 copy.114
  155.5 4.1 %copy.115 = bf16[2,1,1024,4,128]{4,2,1,3,0:T(8,128)(2,1)} copy(bf16[2,1,1024,4,128]{2,4,3,0,1:T(8,128)(2,1)} %bitcast.122) | data formatting | bytes 4194304 | tf_op jit(solution)/shard_map/stack | solution.py:1181
  159.6 5.5 %maximum_bitcast_fusion = bf16[2,4,3,1024,128]{4,3,2,1,0:T(8,128)(2,1)} fusion(bf16[2,1,1024,4,128]{4,2,1,3,0:T(8,128)(2,1)} %copy.115, bf16[2,1,1024,4,128]{4,2,1,3,0:T(8,128)(2,1)} %copy.114, bf16[2,1,1024,4,128]{4,2,1,3,0:T(8,128)(2,1)S(1)} %copy-done.5), kind=kLoop, calls=%fused_computation | loop fusion | flops 6291456 | bytes 12582912 | tf_op jit(solution)/shard_map/transpose | solution.py:1182
  165.1 0.2 reduce-scatter.16.cloned.1.call-start
  165.3 0.8 slice.59
  166.3 3.0 copy.101
  169.4 2.9 fusion.26
  172.3 1.0 copy.102
  173.3 1.8 copy.105
  175.2 0.1 convert_reduce_fusion
  175.3 0.1 multiply_reduce_fusion.2
  175.5 2.1 multiply_reduce_fusion
  177.6 48.5 %reduce-scatter.20.cloned.1.call-done = bf16[1,128,1024]{2,1,0:T(8,128)(2,1)} async-done(((bf16[16,128,1024]{2,1,0:T(8,128)(2,1)}), bf16[1,128,1024]{2,1,0:T(8,128)(2,1)}) %reduce-scatter.20.cloned.1.call-update) | async-done | bytes 262160
  226.1 2.2 subtract_add_fusion
  228.3 0.8 convolution_convert_fusion.4
  229.2 0.2 copy.103
  229.3 1.9 fusion
  231.2 2.3 fusion.1
  233.5 1.6 fusion.3
  235.1 2.0 copy.137
  237.2 3.2 fusion.4
  240.5 2.1 copy.139
  242.7 4.4 %reduce-scatter.12.cloned.1.call-done = bf16[1,4,3,1024,128]{4,3,2,1,0:T(8,128)(2,1)} async-done(((bf16[2,4,3,1024,128]{4,3,2,1,0:T(8,128)(2,1)}), bf16[1,4,3,1024,128]{4,3,2,1,0:T(8,128)(2,1)}) %reduce-scatter.12.cloned.1.call-update) | async-done | bytes 3145744 | tf_op jit(solution)/shard_map/reduce_scatter | solution.py:1183
  247.1 1.0 copy.100
  248.1 1.0 copy.111
  249.2 1.0 copy.112
  250.2 0.1 fusion.5
  250.4 0.6 multiply_multiply_fusion
  250.9 0.1 multiply_cosine_fusion
  251.1 2.0 fusion.28
  253.1 0.5 convolution_multiply_fusion
  253.8 2.1 convolution_convert_fusion.1.a_hbm
  255.9 0.8 fusion.27
  256.9 2.1 convolution_convert_fusion.b_hbm
  258.9 11.9 %reduce-scatter.16.cloned.1.call-done = bf16[128,512]{1,0:T(8,128)(2,1)} async-done(((bf16[512,512]{1,0:T(8,128)(2,1)}), bf16[128,512]{1,0:T(8,128)(2,1)}) %reduce-scatter.16.cloned.1.call-update) | async-done | bytes 131088
  270.9 1.0 copy.138
  271.9 0.8 add_convert_fusion.1
  272.7 1.3 convolution_add_fusion.1
  274.0 20.8 %reduce-scatter.18.cloned.1.call-done = bf16[128,512]{1,0:T(8,128)(2,1)} async-done(((bf16[512,512]{1,0:T(8,128)(2,1)}), bf16[128,512]{1,0:T(8,128)(2,1)}) %reduce-scatter.18.cloned.1.call-update) | async-done | bytes 131088 | tf_op jit(solution)/shard_map/reshape | solution.py:1241
  294.9 2.4 fusion.13
  297.3 0.2 copy.110
  297.6 1.6 concatenate.19.s_hbm
  299.2 0.5 convolution_convert_fusion.3
  299.7 1.4 convolution_convert_fusion.2
  301.2 1.6 pad_maximum_fusion.c_hbm
  302.8 72.8 %total.1 = (bf16[1024,1024]{1,0:T(8,128)(2,1)}, bf16[1024,1024]{1,0:T(8,128)(2,1)}, bf16[1024,1024]{1,0:T(8,128)(2,1)}, f32[1024,128]{1,0:T(8,128)}) custom-call(bf16[1024,1024]{1,0:T(8,128)(2,1)} %convolution_convert_fusion.1.a_hbm, bf16[1024,1024]{1,0:T(8,128)(2,1)} %convolution_convert_fusion.b_hbm, bf16[1024,1024]{1,0:T(8,128)(2,1)} %pad_maximum_fusion.c_hbm, ...), custom_call_target="tpu_custom_call" | custom-call | tf_op jit(solution)/shard_map/total/pallas_call | solution.py:1029
  375.6 4.2 %convert_element_type.124 = f32[1024,1024]{1,0:T(8,128)} convert(bf16[1024,1024]{1,0:T(8,128)(2,1)} %get-tuple-element.50) | non-fusion elementwise | flops 1048576 | bytes 6291456 | tf_op jit(solution)/shard_map/convert_element_type | solution.py:1279
  379.8 2.5 convert_element_type.126
  382.3 0.8 copy.116
  383.1 0.7 convert_reduce_fusion.1
  383.8 1.2 slice_reduce_fusion
  385.0 2.1 fusion.8
  387.1 2.6 fusion.25
  389.7 1.2 convert_element_type.127
  391.0 1.1 slice_bitcast_fusion
  392.0 1.0 copy.117
  (80 shorter events, 0.9 us)
Async XLA Ops:
  7.2 218.9 %reduce-scatter.20.cloned.1.call-start = ((), (), s32[]{:S(2)}) async-start(), calls=%async_computation.9 | async-start | bytes 4456448
  147.1 100.0 %reduce-scatter.12.cloned.1.call-start = ((), (), s32[]{:S(2)}) async-start(), calls=%async_computation.5 | async-start | bytes 9437184 | tf_op jit(solution)/shard_map/reduce_scatter | solution.py:1183
  155.5 4.1 %copy-start.5 = (bf16[2,1,1024,4,128]{4,2,1,3,0:T(8,128)(2,1)S(1)}, bf16[2,1,1024,4,128]{4,2,1,3,0:T(8,128)(2,1)}, u32[]{:S(2)}) copy-start(bf16[2,1,1024,4,128]{4,2,1,3,0:T(8,128)(2,1)} %copy.113) | copy-start | bytes 6291460
  165.1 1.1 copy-start.22
  165.1 105.8 %reduce-scatter.16.cloned.1.call-start = ((), (), s32[]{:S(2)}) async-start(), calls=%async_computation.7 | async-start | bytes 655360
  169.3 60.0 %copy-start = (bf16[8,2,128,512]{2,3,1,0:T(8,128)(2,1)}, bf16[8,2,128,512]{2,3,1,0:T(8,128)(2,1)S(1)}, u32[]{:S(2)}) copy-start(bf16[8,2,128,512]{2,3,1,0:T(8,128)(2,1)S(1)} %copy.101) | copy-start | bytes 6291460
  169.4 5.8 %copy-start.23 = (s32[128,8]{0,1:T(8,128)S(1)}, s32[128,8]{0,1:T(8,128)}, u32[]{:S(2)}) copy-start(s32[128,8]{0,1:T(8,128)} %param.28) | copy-start | bytes 12292
  169.4 6.0 %copy-start.7 = (f32[128,1024]{1,0:T(8,128)S(1)}, f32[128,1024]{1,0:T(8,128)}, u32[]{:S(2)}) copy-start(f32[128,1024]{1,0:T(8,128)} %get-tuple-element.35) | copy-start | bytes 1572868
  169.4 6.1 %copy-start.17 = (bf16[1024,32]{0,1:T(8,128)(2,1)S(1)}, bf16[1024,32]{0,1:T(8,128)(2,1)}, u32[]{:S(2)}) copy-start(bf16[1024,32]{0,1:T(8,128)(2,1)} %param.23) | copy-start | bytes 196612
  169.4 6.1 %copy-start.24 = (f32[1024]{0:T(1024)S(1)}, f32[1024]{0:T(1024)}, u32[]{:S(2)}) copy-start(f32[1024]{0:T(1024)} %param.22) | copy-start | bytes 12292
  226.1 2.2 copy-start.2
  231.2 2.3 copy-start.16
  237.2 57.7 %reduce-scatter.18.cloned.1.call-start = ((), (), s32[]{:S(2)}) async-start(), calls=%async_computation.8 | async-start | bytes 655360 | tf_op jit(solution)/shard_map/reshape | solution.py:1241
  242.6 4.5 %copy-start.11 = (bf16[512,512]{1,0:T(8,128)(2,1)S(1)}, bf16[512,512]{1,0:T(8,128)(2,1)}, u32[]{:S(2)}) copy-start(bf16[512,512]{1,0:T(8,128)(2,1)} %get-tuple-element.123) | copy-start | bytes 1572868
  242.6 147.1 %reduce-scatter.14.cloned.1.call-start = ((), (), s32[]{:S(2)}) async-start(), calls=%async_computation.6 | async-start | bytes 3932160 | tf_op jit(solution)/shard_map/reduce_scatter | solution.py:1184
  247.1 3.1 copy-start.1
  248.1 4.9 %copy-start.15 = (bf16[512,512]{0,1:T(8,128)(2,1)S(1)}, bf16[512,512]{0,1:T(8,128)(2,1)}, u32[]{:S(2)}) copy-start(bf16[512,512]{0,1:T(8,128)(2,1)} %copy.100) | copy-start | bytes 1572868
  251.1 2.6 copy-start.20
  251.1 2.6 copy-start.21
  253.1 0.7 copy-start.19
  253.6 2.3 copy-start.3
  255.9 1.0 copy-start.18
  256.9 15.9 %copy-start.8 = (bf16[1024,512]{1,0:T(8,128)(2,1)S(1)}, bf16[1024,512]{1,0:T(8,128)(2,1)}, u32[]{:S(2)}) copy-start(bf16[1024,512]{1,0:T(8,128)(2,1)} %wk_hbm.1) | copy-start | bytes 3145732
  258.9 35.9 %copy-start.9 = (bf16[1024,512]{1,0:T(8,128)(2,1)S(1)}, bf16[1024,512]{1,0:T(8,128)(2,1)}, u32[]{:S(2)}) copy-start(bf16[1024,512]{1,0:T(8,128)(2,1)} %wv_hbm.1) | copy-start | bytes 3145732
  274.0 23.6 %copy-start.12 = (f32[1024,1]{1,0:T(8,128)S(1)}, f32[1024,1]{1,0:T(8,128)}, u32[]{:S(2)}) copy-start(f32[1024,1]{1,0:T(8,128)} %copy.111) | copy-start | bytes 12292
  274.0 23.6 %copy-start.13 = (f32[1024,1]{1,0:T(8,128)S(1)}, f32[1024,1]{1,0:T(8,128)}, u32[]{:S(2)}) copy-start(f32[1024,1]{1,0:T(8,128)} %copy.112) | copy-start | bytes 12292
  274.0 23.6 %copy-start.14 = (f32[1024,32]{1,0:T(8,128)S(1)}, f32[1024,32]{1,0:T(8,128)}, u32[]{:S(2)}) copy-start(f32[1024,32]{1,0:T(8,128)} %fusion.28) | copy-start | bytes 393220
  375.6 4.2 %copy-start.10 = (bf16[1024,1024]{1,0:T(8,128)(2,1)S(1)}, bf16[1024,1024]{1,0:T(8,128)(2,1)}, u32[]{:S(2)}) copy-start(bf16[1024,1024]{1,0:T(8,128)(2,1)} %get-tuple-element.52) | copy-start | bytes 6291460
  379.8 2.5 copy-start.6
  379.8 5.2 %copy-start.25 = (f32[128]{0:T(128)S(1)}, f32[128]{0:T(128)}, u32[]{:S(2)}) copy-start(f32[128]{0:T(128)} %get-tuple-element.132) | copy-start | bytes 1540
  382.3 4.8 %copy-start.4 = (bf16[1024,1024]{1,0:T(8,128)(2,1)S(1)}, bf16[1024,1024]{1,0:T(8,128)(2,1)}, u32[]{:S(2)}) copy-start(bf16[1024,1024]{1,0:T(8,128)(2,1)} %get-tuple-element.51) | copy-start | bytes 6291460
Sparse Core Ops, SparseCore 0:
  147.2 78.8 reduce-scatter.19
  228.6 18.4 reduce-scatter.11
  250.1 20.7 reduce-scatter.15
  273.7 21.1 reduce-scatter.17
  297.1 64.5 reduce-scatter.13

commit v3 on v2

--- a/solution.py
+++ b/solution.py
@@ -811,6 +811,379 @@
     )
 
 
+def accumulate(target, *terms):
+    total = target[...].astype(F32)
+    for term in terms:
+        total += term[...].astype(F32)
+    target[...] = total.astype(target.dtype)
+
+
+class PlaneReduce:
+    OFF = (0, -1, 1, 2)
+
+    def __init__(self, net, spot, slabs, rb, rc, rd, re, base):
+        self.net, self.spot, self.slabs, self.base = net, spot, slabs, base
+        self.rb, self.rc, self.rd, self.re = rb, rc, rd, re
+        p, q, y, core = spot
+        self.right, self.left = device(p + 1, q, y, core), device(p - 1, q, y, core)
+        self.up, self.down = device(p, q + 1, y, core), device(p, q - 1, y, core)
+
+    def slab(self, a, b):
+        return slab(self.slabs, self.spot[0] + a, self.spot[1] + b)
+
+    def send(self, source, target, recv, to):
+        self.net.start(source, target, self.base + recv, to)
+
+    def arrived(self, ref, recv):
+        self.net.arrived(ref, self.base + recv)
+
+    def bounce(self):
+        for j in range(4):
+            to = self.up if j < 2 else self.down
+            self.send(self.slab(self.OFF[j], 2), self.rb.at[j], j, to)
+
+    def to_up(self, j):
+        self.send(self.slab(self.OFF[j], 1), self.rc.at[j], 4 + j, self.up)
+
+    def to_down(self, j):
+        self.send(self.slab(self.OFF[j], -1), self.rc.at[4 + j], 8 + j, self.down)
+
+    def begin(self):
+        self.bounce()
+        for j in (3, 2):
+            self.to_up(j)
+        for j in (0, 1):
+            self.to_down(j)
+
+    def middle(self):
+        for j in (3, 1, 2, 0):
+            self.arrived(self.rb.at[j], j)
+            accumulate(self.slab(self.OFF[j], 1 if j < 2 else -1), self.rb.at[j])
+            (self.to_up if j < 2 else self.to_down)(j)
+
+    def column(self, j):
+        self.arrived(self.rc.at[j], 4 + j)
+        self.arrived(self.rc.at[4 + j], 8 + j)
+        accumulate(self.slab(self.OFF[j], 0), self.rc.at[j], self.rc.at[4 + j])
+
+    def third(self):
+        lo, hi = pl.ds(0, 64), pl.ds(64, 64)
+        rd, re = self.rd, self.re
+        self.column(3)
+        self.send(self.slab(2, 0).at[lo], rd.at[lo], 12, self.right)
+        self.send(self.slab(2, 0).at[hi], rd.at[hi], 13, self.left)
+        self.column(2)
+        self.send(self.slab(1, 0).at[hi], re.at[0, hi], 14, self.right)
+        self.column(1)
+        self.send(self.slab(-1, 0).at[lo], re.at[1, lo], 15, self.left)
+
+    def fourth(self):
+        lo, hi = pl.ds(0, 64), pl.ds(64, 64)
+        rd, re = self.rd, self.re
+        self.arrived(rd.at[lo], 12)
+        accumulate(self.slab(1, 0).at[lo], rd.at[lo])
+        self.send(self.slab(1, 0).at[lo], re.at[0, lo], 16, self.right)
+        self.arrived(rd.at[hi], 13)
+        accumulate(self.slab(-1, 0).at[hi], rd.at[hi])
+        self.send(self.slab(-1, 0).at[hi], re.at[1, hi], 17, self.left)
+        self.column(0)
+
+    def finish(self):
+        lo, hi = pl.ds(0, 64), pl.ds(64, 64)
+        re = self.re
+        self.arrived(re.at[0, hi], 14)
+        self.arrived(re.at[1, lo], 15)
+        self.arrived(re.at[0, lo], 16)
+        self.arrived(re.at[1, hi], 17)
+        return self.slab(0, 0)[...].astype(F32) + re[0].astype(F32) + re[1].astype(F32)
+
+
+class RingReduce:
+    def __init__(self, net, base, ahead, behind, portion, hops, lows, highs):
+        self.net, self.base, self.ahead, self.behind = net, base, ahead, behind
+        self.portion, self.hops, self.lows, self.highs = portion, hops, lows, highs
+        self.n = len(hops[0])
+
+    def send(self, sources, targets, group, to):
+        for i, (source, target) in enumerate(zip(sources, targets)):
+            self.net.start(source, target, self.base + group * self.n + i, to)
+
+    def arrived(self, refs, group):
+        for i, ref in enumerate(refs):
+            self.net.arrived(ref, self.base + group * self.n + i)
+
+    def begin(self):
+        self.send(self.portion(2, 0), self.hops[0], 0, self.ahead)
+        self.send(self.portion(2, 1), self.hops[1], 1, self.behind)
+
+    def direct(self):
+        self.send(self.portion(1, 1), self.lows[1], 2, self.ahead)
+        self.send(self.portion(-1, 0), self.highs[0], 3, self.behind)
+
+    def middle(self):
+        for which, step, targets, to in (
+            (0, 1, self.lows[0], self.ahead),
+            (1, -1, self.highs[1], self.behind),
+        ):
+            self.arrived(self.hops[which], which)
+            refs = self.portion(step, which)
+            for ref, hop in zip(refs, self.hops[which]):
+                accumulate(ref, hop)
+            self.send(refs, targets, 4 + which, to)
+
+    def finish(self):
+        self.arrived(self.lows[1], 2)
+        self.arrived(self.highs[0], 3)
+        self.arrived(self.lows[0], 4)
+        self.arrived(self.highs[1], 5)
+
+
+def back_kernel(
+    rows_ref, gg_ref, x_ref, gates_ref, hidden_ref, gm_ref, ga_ref, router_ref, cot_ref, tok_ref,
+    mixed_ref, query_ref, kv_ref, cos_ref, sin_ref, routes_ref, len_ref,
+    probs_hbm, wo_hbm, wq_hbm, wk_hbm, wv_hbm, o_hbm, pg_hbm, pu_hbm, pd_hbm,
+    layer_ref, input_ref, dq_out, do_out, dkv_out, narrow_ref, gate_out, up_out, down_out,
+    probs, wo, wq, wk, wv, o_buf, rb, rc, rd, re,
+    pg, pu, pd, sg, su, sd, hop_g, hop_ua, hop_ub, hop_d, low_g, low_u, low_d, high_g, high_u, high_d,
+    grad_mixed, grad_query, grad_kv, kv_hops, kv_low, kv_high,
+    send_sem, recv_sem, local_sem,
+):
+    p, q, y, core = place()
+    spot = (p, q, y, core)
+    sibling = (chip_of(p, q, core) * 2 + 1 - core, y)
+    ahead, behind = device(p, q, y + 1, core), device(p, q, y - 1, core)
+    net = Sends(send_sem, recv_sem)
+    pairs = (
+        (o_hbm, o_buf), (wo_hbm, wo), (probs_hbm, probs), (wq_hbm, wq), (wk_hbm, wk), (wv_hbm, wv),
+        (pg_hbm.at[core], pg), (pu_hbm.at[core], pu), (pd_hbm.at[core], pd),
+    )
+    loads = [pltpu.make_async_copy(s, d, local_sem.at[i]) for i, (s, d) in enumerate(pairs)]
+    for load in loads:
+        load.start()
+    plane = PlaneReduce(net, spot, o_buf, rb, rc, rd, re, 0)
+    greet([plane.right, plane.left, plane.up, plane.down, ahead, behind, sibling])
+    loads[0].wait()
+    plane.begin()
+    for i, (source, target) in enumerate(((pg_hbm, sg), (pu_hbm, su), (pd_hbm, sd))):
+        net.start(source.at[1 - core], target, 18 + i, sibling)
+
+    first = pl.multiple_of(y * TOK, TOK)
+    row = lax.broadcasted_iota(jnp.int32, (TOK, 1), 0) + y * TOK
+    upstream = jnp.where(row < len_ref[0], cot_ref[...].astype(F32), 0.0)
+    gates = gates_ref[...]
+    grad_gates = gg_ref[...].reshape(TOK, TOK).T
+    grad_logits = gates * (grad_gates - jnp.sum(gates * grad_gates, axis=1, keepdims=True))
+    grad_logits = grad_logits.astype(BF)
+    wide = jnp.dot(router_ref[...], widen(), preferred_element_type=F32).astype(BF)
+    by_row = (((0,), (0,)), ((), ()))
+    by_col = (((1,), (1,)), ((), ()))
+    grad_normed = rows_ref[...] + lax.dot_general(
+        grad_logits, wide, by_col, preferred_element_type=F32
+    )
+    hidden = hidden_ref[...]
+    scale = root(hidden)
+    grad_gain_moe = jnp.sum(grad_normed * hidden * scale, axis=0, keepdims=True)
+    scaled = grad_normed * gm_ref[...]
+    pull = jnp.mean(scaled * hidden, axis=1, keepdims=True)
+    grad_hidden = upstream + scale * scaled - hidden * (scale * scale * scale) * pull
+    input_ref[...] = grad_hidden
+    low = grad_hidden.astype(BF)
+    loads[1].wait()
+    grad_mixed[...] = lax.dot_general(low, wo[...], by_col, preferred_element_type=F32).astype(BF)
+    narrow_ref[...] = lax.dot_general(grad_logits, x_ref[...], by_row, preferred_element_type=F32)
+    counts = jnp.sum(jnp.where(routed_mask(routes_ref[...]), 1.0, 0.0), axis=0, keepdims=True)
+    narrow_ref[3:4, :] = grad_gain_moe
+    narrow_ref[4:5, :] = jnp.zeros((1, D), F32)
+    narrow_ref[4:5, 0:TOK] = counts
+    plane.middle()
+
+    def block(ref, step, rows=None):
+        span = pl.ds(pl.multiple_of(wrap(y + step) * TOK, TOK), TOK)
+        return ref.at[:, span] if rows is None else ref.at[rows, span]
+
+    def down_block(ref, step):
+        return ref.at[pl.ds(pl.multiple_of(wrap(y + step) * TOK, TOK), TOK)]
+
+    top, bottom = pl.ds(0, 512), pl.ds(512, 512)
+
+    def weight_portion(step, which):
+        if which == 0:
+            return [block(pg, step), block(pu, step, top)]
+        return [block(pu, step, bottom), down_block(pd, step)]
+
+    def weight_merge(step):
+        accumulate(block(pg, step), block(sg, step))
+        accumulate(block(pu, step), block(su, step))
+        accumulate(down_block(pd, step), down_block(sd, step))
+
+    weights = RingReduce(
+        net, 24, ahead, behind, weight_portion,
+        ([hop_g, hop_ua], [hop_ub, hop_d]),
+        ([low_g, low_u.at[top]], [low_u.at[bottom], low_d]),
+        ([high_g, high_u.at[top]], [high_u.at[bottom], high_d]),
+    )
+    for load in loads[6:]:
+        load.wait()
+    for i, ref in enumerate((sg, su, sd)):
+        net.arrived(ref, 18 + i)
+    weight_merge(2)
+    weights.begin()
+
+    cosine, sine = cos_ref[pl.ds(first, TOK), :], sin_ref[pl.ds(first, TOK), :]
+    loads[2].wait()
+
+    def attend(c, carry):
+        span = pl.ds(pl.multiple_of(c * 128, 128), 128)
+        value_span = pl.ds(pl.multiple_of(512 + c * 128, 128), 128)
+        keys = kv_ref[:, :, span].reshape(512, 128)
+        values = kv_ref[:, :, value_span].reshape(512, 128)
+        grad_keys = jnp.zeros((512, 128), F32)
+        grad_values = jnp.zeros((512, 128), F32)
+        for half in range(2):
+            m = c * 2 + half
+            mine = pl.ds(pl.multiple_of(m * 128, 128), 128)
+            pair = stack_heads(query_ref[:, mine].astype(F32), half)
+            grad_pair = stack_heads(grad_mixed[:, mine].astype(F32), half)
+            grad_probs = lax.dot_general(grad_pair, values, by_col, preferred_element_type=F32)
+            prob = probs[m]
+            wide_prob = prob.astype(F32)
+            middle = jnp.sum(wide_prob * grad_probs, axis=1, keepdims=True)
+            grad_scores = (wide_prob * (grad_probs - middle)).astype(BF)
+            back = jnp.dot(grad_scores, keys, preferred_element_type=F32) * SCALE
+            grad_query[:, mine] = turn(unstack_heads(back, half), cosine, -sine).astype(BF)
+            grad_keys += lax.dot_general(grad_scores, pair, by_row, preferred_element_type=F32)
+            grad_values += lax.dot_general(prob, grad_pair, by_row, preferred_element_type=F32)
+        grad_kv[:, :, span] = (grad_keys * SCALE).astype(BF).reshape(4, TOK, 128)
+        grad_kv[:, :, value_span] = grad_values.astype(BF).reshape(4, TOK, 128)
+        return carry
+
+    lax.fori_loop(0, 4, attend, 0)
+    lo, hi = pl.ds(0, 64), pl.ds(64, 64)
+    sums = RingReduce(
+        net, 36, ahead, behind,
+        lambda step, which: [grad_kv.at[wrap(y + step), hi if which else lo]],
+        ([kv_hops.at[0]], [kv_hops.at[1]]),
+        ([kv_low.at[lo]], [kv_low.at[hi]]),
+        ([kv_high.at[lo]], [kv_high.at[hi]]),
+    )
+    sums.begin()
+    sums.direct()
+    plane.third()
+    do_out[...] = lax.dot_general(
+        mixed_ref[...], low, by_row, preferred_element_type=F32
+    ).astype(BF)
+    sums.middle()
+    plane.fourth()
+    tokens = tok_ref[...].astype(F32)
+    scale = root(tokens)
+    normed = (tokens * scale * ga_ref[...]).astype(BF)
+    dq_out[...] = lax.dot_general(
+        normed, grad_query[...], by_row, preferred_element_type=F32
+    ).astype(BF)
+    for load in loads[3:6]:
+        load.wait()
+    grad_normed = lax.dot_general(grad_query[...], wq[...], by_col, preferred_element_type=F32)
+    weight_merge(1)
+    weight_merge(-1)
+    weights.direct()
+    weights.middle()
+    weight_merge(0)
+    sums.finish()
+    both = grad_kv[y].astype(F32) + kv_low[...].astype(F32) + kv_high[...].astype(F32)
+    grad_key = jnp.concatenate(
+        [turn(both[:, c * 128 : (c + 1) * 128], cosine, -sine) for c in range(4)], axis=1
+    ).astype(BF)
+    grad_value = both[:, 512:].astype(BF)
+    dkv_out[:, 0:512] = lax.dot_general(
+        normed, grad_key, by_row, preferred_element_type=F32
+    ).astype(BF)
+    dkv_out[:, 512:1024] = lax.dot_general(
+        normed, grad_value, by_row, preferred_element_type=F32
+    ).astype(BF)
+    grad_normed += lax.dot_general(grad_key, wk[...], by_col, preferred_element_type=F32)
+    grad_normed += lax.dot_general(grad_value, wv[...], by_col, preferred_element_type=F32)
+    narrow_ref[2:3, :] = jnp.sum(grad_normed * tokens * scale, axis=0, keepdims=True)
+    scaled = grad_normed * ga_ref[...]
+    pull = jnp.mean(scaled * tokens, axis=1, keepdims=True)
+    input_ref[...] += scale * scaled - tokens * (scale * scale * scale) * pull
+    layer_ref[...] = (hidden_ref[...] + plane.finish()).astype(BF)
+    weights.finish()
+    gate_out[...] = (
+        block(pg, 0)[...].astype(F32) + low_g[...].astype(F32) + high_g[...].astype(F32)
+    )
+    up_out[...] = block(pu, 0)[...].astype(F32) + low_u[...].astype(F32) + high_u[...].astype(F32)
+    down_out[...] = (
+        down_block(pd, 0)[...].astype(F32) + low_d[...].astype(F32) + high_d[...].astype(F32)
+    )
+    net.drain()
+
+
+def back(operands, arrays):
+    any_space = pl.BlockSpec(memory_space=pl.ANY)
+    vmem = pl.BlockSpec(memory_space=pltpu.VMEM)
+    smem = pl.BlockSpec(memory_space=pltpu.SMEM)
+    shape = jax.ShapeDtypeStruct
+    dma = pltpu.SemaphoreType.DMA
+    low = lambda *size: pltpu.VMEM(size, BF)
+    return pl.pallas_call(
+        back_kernel,
+        out_shape=(
+            shape((TOK, D), BF),
+            shape((TOK, D), F32),
+            shape((D, D), BF),
+            shape((D, D), BF),
+            shape((D, D), BF),
+            shape((TOK, D), F32),
+            shape((D, TOK), F32),
+            shape((D, TOK), F32),
+            shape((TOK, D), F32),
+        ),
+        in_specs=[vmem] * 16 + [smem] + [any_space] * 9,
+        out_specs=(vmem,) * 9,
+        scratch_shapes=[
+            low(8, 2 * TOK, 512),
+            low(D, D),
+            low(D, D),
+            low(D, 512),
+            low(D, 512),
+            low(16, TOK, D),
+            low(4, TOK, D),
+            low(8, TOK, D),
+            low(TOK, D),
+            low(2, TOK, D),
+            low(D, FF),
+            low(D, FF),
+            low(FF, D),
+            low(D, FF),
+            low(D, FF),
+            low(FF, D),
+            low(D, TOK),
+            low(512, TOK),
+            low(512, TOK),
+            low(TOK, D),
+            low(D, TOK),
+            low(D, TOK),
+            low(TOK, D),
+            low(D, TOK),
+            low(D, TOK),
+            low(TOK, D),
+            low(TOK, D),
+            low(TOK, D),
+            low(4, TOK, D),
+            low(2, 64, D),
+            low(TOK, D),
+            low(TOK, D),
+            dma((48,)),
+            dma((42,)),
+            dma((9,)),
+        ],
+        compiler_params=pltpu.CompilerParams(
+            collective_id=4, has_side_effects=True, vmem_limit_bytes=VMEM_BYTES
+        ),
+        name="back",
+    )(*operands, *arrays)
+
+
 def total_kernel(
     a_hbm, b_hbm, c_hbm, s_hbm, a_out, b_out, c_out, s_out,
     mine, other, mine_s, other_s, from_low, from_high, from_low_s, from_high_s, bounced, bounced_s,
@@ -848,8 +1221,11 @@
     pieces = [spread.at[k] for k in range(3)] + [spread_s]
     slabs = [done.at[k] for k in range(3)] + [done_s]
     parts = range(4)
-    own_rows = pl.ds(pl.multiple_of(core * 512, 512), 512)
-    their_rows = pl.ds(pl.multiple_of((1 - core) * 512, 512), 512)
+    sizes = (128, 128, 128, 16)
+
+    def half_of(k, which):
+        return ins[k].at[pl.ds(pl.multiple_of(which * sizes[k] * 4, sizes[k] * 4), sizes[k] * 4)]
+
 
     def remote(source, target, send, recv, to):
         return pltpu.make_async_remote_copy(
@@ -861,7 +1237,7 @@
         pltpu.make_async_copy(ref, ref, sem).wait()
 
     loads = [
-        pltpu.make_async_copy(ins[k].at[own_rows], halves[k], local_sem.at[k]) for k in parts
+        pltpu.make_async_copy(half_of(k, core), halves[k], local_sem.at[k]) for k in parts
     ]
     for load in loads:
         load.start()
@@ -874,13 +1250,14 @@
         sent.append(copy)
 
     for k in parts:
-        go(ins[k].at[their_rows], theirs[k], sib_send.at[k], sib_recv.at[k], sibling)
+        go(half_of(k, 1 - core), theirs[k], sib_send.at[k], sib_recv.at[k], sibling)
 
     def rows_of(k, step):
-        start = pl.multiple_of(wrap(here[axes[k]] + step) * 128, 128)
-        return halves[k].at[pl.ds(start, 128)]
-
-    lo, hi = pl.ds(0, 64), pl.ds(64, 64)
+        start = pl.multiple_of(wrap(here[axes[k]] + step) * sizes[k], sizes[k])
+        return halves[k].at[pl.ds(start, sizes[k])]
+
+    los = [pl.ds(0, size // 2) for size in sizes]
+    his = [pl.ds(size // 2, size // 2) for size in sizes]
 
     def add(target, *terms):
         total = target[...].astype(F32)
@@ -889,11 +1266,12 @@
         target[...] = total.astype(target.dtype)
 
     def merge_rows(k, step):
-        start = pl.multiple_of(wrap(here[axes[k]] + step) * 128, 128)
-        span = pl.ds(start, 128)
+        start = pl.multiple_of(wrap(here[axes[k]] + step) * sizes[k], sizes[k])
+        span = pl.ds(start, sizes[k])
         add(halves[k].at[span], theirs[k].at[span])
 
     for k in parts:
+        lo, hi = los[k], his[k]
         loads[k].wait()
         arrived(theirs[k], sib_recv.at[k])
         plus, minus = ring[axes[k]]
@@ -907,6 +1285,7 @@
         go(rows_of(k, -1).at[lo], highs[k].at[lo], ring_send.at[k, 3], ring_recv.at[k, 3], minus)
         merge_rows(k, 0)
     for k in parts:
+        lo, hi = los[k], his[k]
         plus, minus = ring[axes[k]]
         arrived(hops[k].at[lo], ring_recv.at[k, 0])
         near = rows_of(k, 1).at[lo]
@@ -919,7 +1298,8 @@
 
     def piece(k, ref, u, v):
         if k == 3:
-            return ref.at[pl.ds(pl.multiple_of((u * 4 + v) * 8, 8), 8)]
+            row, lane = lax.div(u, 2) * 8, (lax.rem(u, 2) * 4 + v) * 128
+            return ref.at[pl.ds(pl.multiple_of(row, 8), 8), pl.ds(pl.multiple_of(lane, 128), 128)]
         return ref.at[
             pl.ds(pl.multiple_of(u * 32, 32), 32), pl.ds(pl.multiple_of(v * 256, 256), 256)
         ]
@@ -957,6 +1337,7 @@
         lax.fori_loop(1, 16, one, 0)
 
     for k in parts:
+        lo, hi = los[k], his[k]
         for i in (2, 4):
             arrived(lows[k].at[hi if i == 2 else lo], ring_recv.at[k, i])
         for i in (3, 5):
@@ -975,12 +1356,12 @@
         each(lambda i: back_copy(k, i), lambda copy: copy.start())
 
     def final(k, step, span=None):
-        start = pl.multiple_of(core * 512 + wrap(here[axes[k]] + step) * 128, 128)
+        size = sizes[k]
+        start = core * size * 4 + wrap(here[axes[k]] + step) * size
         if span is not None:
-            start, size = start + span, 64
-        else:
-            size = 128
-        return results[k].at[pl.ds(pl.multiple_of(start, 64), size)]
+            size = size // 2
+            start += span * size
+        return results[k].at[pl.ds(pl.multiple_of(start, size), size)]
 
     stores = []
     for k in parts:
@@ -1002,12 +1383,12 @@
         go(spot, spot, round_send.at[k, 2], round_recv.at[k, 2], plus)
         go(final(k, -1), final(k, -1), last_send.at[k, 1], last_recv.at[k, 1], sibling)
         arrived(final(k, 1), round_recv.at[k, 1])
-        spot = final(k, 1, 64)
+        spot = final(k, 1, 1)
         go(spot, spot, round_send.at[k, 3], round_recv.at[k, 3], minus)
         go(final(k, 1), final(k, 1), last_send.at[k, 2], last_recv.at[k, 2], sibling)
     for k in parts:
         arrived(final(k, 2, 0), round_recv.at[k, 2])
-        arrived(final(k, 2, 64), round_recv.at[k, 3])
+        arrived(final(k, 2, 1), round_recv.at[k, 3])
         go(final(k, 2), final(k, 2), last_send.at[k, 3], last_recv.at[k, 3], sibling)
     for k in parts:
         for i in range(4):
@@ -1028,24 +1409,24 @@
     vmem = pltpu.VMEM
     return pl.pallas_call(
         total_kernel,
-        out_shape=(shape((D, D), BF),) * 3 + (shape((D, TOK), F32),),
+        out_shape=(shape((D, D), BF),) * 3 + (shape((TOK, D), F32),),
         in_specs=[any_space] * 4,
         out_specs=(any_space,) * 4,
         scratch_shapes=[
             vmem((3, 512, D), BF),
             vmem((3, 512, D), BF),
-            vmem((512, TOK), F32),
-            vmem((512, TOK), F32),
+            vmem((64, D), F32),
+            vmem((64, D), F32),
             vmem((3, 128, D), BF),
             vmem((3, 128, D), BF),
-            vmem((128, TOK), F32),
-            vmem((128, TOK), F32),
+            vmem((16, D), F32),
+            vmem((16, D), F32),
             vmem((3, 128, D), BF),
-            vmem((128, TOK), F32),
+            vmem((16, D), F32),
             vmem((3, 16, 32, 256), BF),
             vmem((16, 8, TOK), F32),
             vmem((3, 128, D), BF),
-            vmem((128, TOK), F32),
+            vmem((16, D), F32),
             dma((4,)),
             dma((4,)),
             dma((4, 6)),
@@ -1067,53 +1448,6 @@
     )(a, b, c, s)
 
 
-def rms_forward(values, gain_vector):
-    inverse_root = lax.rsqrt(jnp.mean(values * values, axis=-1, keepdims=True) + 1e-06)
-    return (values * inverse_root * gain_vector, inverse_root)
-
-
-def rms_backward(values, inverse_root, gain_vector, upstream):
-    scaled = upstream * gain_vector
-    grad_gain = jnp.sum(upstream * values * inverse_root, axis=0)
-    grad_values = inverse_root * scaled - values * inverse_root**3 * jnp.mean(
-        scaled * values, axis=-1, keepdims=True
-    )
-    return (grad_values, grad_gain)
-
-
-def rope_tables(first_pos, row_count, head_width):
-    half_dim = head_width // 2
-    inverse = 10000.0 ** (-jnp.arange(half_dim, dtype=jnp.float32) / half_dim)
-    phases = (first_pos + jnp.arange(row_count, dtype=jnp.float32))[:, None] * inverse[None, :]
-    return (jnp.sin(phases)[:, None, :], jnp.cos(phases)[:, None, :])
-
-
-def rotate(values, sine_table, cosine_table):
-    half_dim = values.shape[-1] // 2
-    front_half = values[..., :half_dim]
-    back_half = values[..., half_dim:]
-    return jnp.concatenate(
-        [
-            front_half * cosine_table - back_half * sine_table,
-            back_half * cosine_table + front_half * sine_table,
-        ],
-        axis=-1,
-    )
-
-
-def unrotate(grad_values, sine_table, cosine_table):
-    half_dim = grad_values.shape[-1] // 2
-    front_half = grad_values[..., :half_dim]
-    back_half = grad_values[..., half_dim:]
-    return jnp.concatenate(
-        [
-            front_half * cosine_table + back_half * sine_table,
-            back_half * cosine_table - front_half * sine_table,
-        ],
-        axis=-1,
-    )
-
-
 def shards(
     tokens,
     w_query,
@@ -1130,163 +1464,43 @@
     routes,
     lengths,
 ):
-    tok_count = tokens.shape[0]
-    hid_pos = lax.axis_index("hid")
-    first_pos = (hid_pos * tok_count).astype(jnp.float32)
-    group_size = HEADS // KV_HEADS
-    score_scale = HEAD_DIM ** (-0.5)
-    inputs = tokens.astype(jnp.float32)
-    normed, root_attn = rms_forward(inputs, gain_attn)
-    normed_low = normed.astype(jnp.bfloat16)
-    sine_table, cosine_table = rope_tables(first_pos, tok_count, HEAD_DIM)
     (
-        hidden, normed_two_low, gate_tiles, gates, mixed_low, query_low, kv, probs,
-        upstream_all, full_gate, full_up, full_down,
+        hidden, x, gate_tiles, gates, mixed, query, kv, probs, upstream_all, full_gate, full_up,
+        full_down,
     ) = front(
         tokens, w_query, w_key, w_value, w_output, gain_attn, gain_moe, router, cotangent, routes,
         lengths, w_gate, w_up, w_down,
     )
-    root_moe = lax.rsqrt(jnp.mean(hidden * hidden, axis=-1, keepdims=True) + 1e-06)
-    route_onehot = (routes[:, :, None] == jnp.arange(EXPERTS, dtype=jnp.int32)).astype(jnp.float32)
-    kv = kv.reshape(512, D)
-    keys_all = kv[:, :512].reshape(512, KV_HEADS, HEAD_DIM)
-    values_all = kv[:, 512:].reshape(512, KV_HEADS, HEAD_DIM)
-    grouped = query_low.reshape(tok_count, KV_HEADS, group_size, HEAD_DIM)
-    query_pos = hid_pos * tok_count + jnp.arange(tok_count, dtype=jnp.int32)
-    score_scale = HEAD_DIM ** (-0.5)
-    softmaxed_low = probs.reshape(KV_HEADS, group_size, tok_count, 512)
-    softmaxed = softmaxed_low.astype(jnp.float32)
-    gate_weights = jnp.sum(gates.reshape(tok_count, 16, 8)[:, :, :2].reshape(tok_count, 1, EXPERTS) * route_onehot, axis=-1)
-    core_groups = [[2 * i for i in range(16)], [2 * i + 1 for i in range(16)]]
-    pair_groups = [[2 * i, 2 * i + 1] for i in range(16)]
-    live_rows = (query_pos < lengths[0]).astype(jnp.float32)
-    upstream_low = jnp.where(live_rows[:, None] > 0, cotangent, jnp.zeros_like(cotangent))
-    upstream = upstream_low.astype(jnp.float32)
-    core = lax.rem(lax.axis_index("dp"), 2)
-
-    def by_place(rows):
-        rows = rows.reshape(4, 4, TOK, D)
-        return jnp.where(core == 0, rows, rows.transpose(1, 0, 2, 3)).reshape(16, TOK, D)
-
-    grad_rows, out_parts, grad_gates_t, part_gate, part_up, part_down = moe(
-        normed_two_low,
-        gate_tiles,
-        upstream_all,
-        full_gate,
-        full_up,
-        full_down,
+    grad_rows, out_parts, grad_gates, part_gate, part_up, part_down = moe(
+        x, gate_tiles, upstream_all, full_gate, full_up, full_down
     )
-    moe_out = lax.psum_scatter(by_place(out_parts), "dp", axis_index_groups=core_groups)
-    layer_out = (hidden + moe_out.astype(jnp.float32)).astype(jnp.bfloat16)
-    parts = jnp.stack([part_gate, part_up, part_down.transpose(0, 2, 1)], axis=1)
-    parts = parts.reshape(2, 3, D, 4, TOK).transpose(0, 3, 1, 2, 4)
-    parts = lax.psum_scatter(parts, "dp", axis_index_groups=pair_groups)
-    parts = lax.psum_scatter(parts, "hid").astype(jnp.float32)
-    grad_gate, grad_up, grad_down = parts[0][None], parts[1][None], parts[2].T[None]
-    grad_gates = jnp.einsum("et,tke->tk", grad_gates_t[:, :2].reshape(EXPERTS, TOK), route_onehot, precision=lax.Precision.HIGHEST)
-    grad_picked = gate_weights * (
-        grad_gates - jnp.sum(gate_weights * grad_gates, axis=-1, keepdims=True)
+    cosine, sine = turn_tables()
+    layer_out, grad_input, sum_q, sum_o, sum_kv, narrow, grad_gate, grad_up, grad_down = back(
+        (
+            grad_rows, grad_gates, x, gates, hidden, gain_moe.reshape(1, D),
+            gain_attn.reshape(1, D), router, cotangent, tokens, mixed, query, kv,
+            jnp.asarray(cosine), jnp.asarray(sine), routes, lengths,
+        ),
+        (
+            probs, w_output, w_query, w_key, w_value, out_parts, part_gate, part_up, part_down,
+        ),
     )
-    grad_logits = jnp.sum(grad_picked[:, :, None] * route_onehot, axis=1).astype(jnp.bfloat16)
-    grad_router = jnp.einsum(
-        "td,te->de", normed_two_low, grad_logits, preferred_element_type=jnp.float32
-    )
-    grad_normed_two = grad_rows + jnp.einsum(
-        "te,de->td", grad_logits, router, preferred_element_type=jnp.float32
-    )
-    grad_hidden_part, grad_gain_moe = rms_backward(hidden, root_moe, gain_moe, grad_normed_two)
-    grad_hidden = upstream + grad_hidden_part
-    grad_hidden_low = grad_hidden.astype(jnp.bfloat16)
-    grad_w_output = jnp.einsum(
-        "tf,td->fd", mixed_low, grad_hidden_low, preferred_element_type=jnp.float32
-    )
-    grad_mixed = jnp.einsum(
-        "td,fd->tf", grad_hidden_low, w_output, preferred_element_type=jnp.float32
-    )
-    grad_mixed = grad_mixed.astype(jnp.bfloat16).reshape(tok_count, KV_HEADS, group_size, HEAD_DIM)
-    grad_probs = jnp.einsum(
-        "tkgd,skd->kgts", grad_mixed, values_all, preferred_element_type=jnp.float32
-    )
-    grad_scores = (
-        softmaxed * (grad_probs - jnp.sum(softmaxed * grad_probs, axis=-1, keepdims=True))
-    ).astype(jnp.bfloat16)
-    grad_query = (
-        jnp.einsum("kgts,skd->tkgd", grad_scores, keys_all, preferred_element_type=jnp.float32)
-        * score_scale
-    )
-    grad_key_part = (
-        jnp.einsum("kgts,tkgd->skd", grad_scores, grouped, preferred_element_type=jnp.float32)
-        * score_scale
-    )
-    grad_value_part = jnp.einsum(
-        "kgts,tkgd->skd", softmaxed_low, grad_mixed, preferred_element_type=jnp.float32
-    )
-    grad_key, grad_value = (
-        lax.psum_scatter(
-            grad_key_part.astype(jnp.bfloat16), "hid", scatter_dimension=0, tiled=True
-        ).astype(jnp.float32),
-        lax.psum_scatter(
-            grad_value_part.astype(jnp.bfloat16), "hid", scatter_dimension=0, tiled=True
-        ).astype(jnp.float32),
-    )
-    grad_query_low = unrotate(
-        grad_query.reshape(tok_count, HEADS, HEAD_DIM), sine_table, cosine_table
-    )
-    grad_query_low = grad_query_low.astype(jnp.bfloat16).reshape(tok_count, HEADS * HEAD_DIM)
-    grad_key_low = (
-        unrotate(grad_key, sine_table, cosine_table)
-        .astype(jnp.bfloat16)
-        .reshape(tok_count, KV_HEADS * HEAD_DIM)
-    )
-    grad_value_low = grad_value.astype(jnp.bfloat16).reshape(tok_count, KV_HEADS * HEAD_DIM)
-    grad_w_query = jnp.einsum(
-        "td,tf->df", normed_low, grad_query_low, preferred_element_type=jnp.float32
-    )
-    grad_w_key = jnp.einsum(
-        "td,tf->df", normed_low, grad_key_low, preferred_element_type=jnp.float32
-    )
-    grad_w_value = jnp.einsum(
-        "td,tf->df", normed_low, grad_value_low, preferred_element_type=jnp.float32
-    )
-    grad_normed = (
-        jnp.einsum("tf,df->td", grad_query_low, w_query, preferred_element_type=jnp.float32)
-        + jnp.einsum("tf,df->td", grad_key_low, w_key, preferred_element_type=jnp.float32)
-        + jnp.einsum("tf,df->td", grad_value_low, w_value, preferred_element_type=jnp.float32)
-    )
-    grad_input_part, grad_gain_attn = rms_backward(inputs, root_attn, gain_attn, grad_normed)
-    grad_input = grad_hidden + grad_input_part
-    counts_local = jnp.sum(route_onehot, axis=(0, 1))
-    narrow = jnp.concatenate(
-        [
-            grad_router,
-            grad_gain_attn[:, None],
-            grad_gain_moe[:, None],
-            jnp.pad(counts_local, (0, D - EXPERTS))[:, None],
-            jnp.zeros((D, TOK - EXPERTS - 3), jnp.float32),
-        ],
-        axis=1,
-    )
-    sum_q, sum_o, sum_kv, narrow = total(
-        grad_w_query.astype(BF),
-        grad_w_output.astype(BF),
-        jnp.concatenate([grad_w_key, grad_w_value], axis=1).astype(BF),
-        narrow,
-    )
-    sum_kv = sum_kv.astype(jnp.float32)
+    sum_q, sum_o, sum_kv, narrow = total(sum_q, sum_o, sum_kv, narrow)
+    sum_kv = sum_kv.astype(F32)
     return (
         layer_out,
         grad_input,
-        sum_q.astype(jnp.float32),
+        sum_q.astype(F32),
         sum_kv[:, :512],
         sum_kv[:, 512:],
-        sum_o.astype(jnp.float32),
-        narrow[:, EXPERTS],
-        narrow[:, EXPERTS + 1],
-        narrow[:, :EXPERTS],
-        grad_gate,
-        grad_up,
-        grad_down,
-        narrow[:EXPERTS, EXPERTS + 2].astype(jnp.int32),
+        sum_o.astype(F32),
+        narrow[2],
+        narrow[3],
+        narrow.reshape(16, 8, D)[:, :2].reshape(EXPERTS, D).T,
+        grad_gate[None],
+        grad_up[None],
+        grad_down[None],
+        narrow[4, :TOK].reshape(16, 8)[:, :2].reshape(EXPERTS).astype(jnp.int32),
     )
 
 

time: 401 us -> 263 us (0.66)
  waiting for transfers between devices: 85.8 us -> 0 us
  Pallas kernels: 203 us -> 241 us
  local copies, waits for them, and re-layouts: 42.4 us -> 14.2 us
  other arithmetic: 30.4 us -> 6.7 us
  matrix products: 22.8 us -> 0 us
  between operations: 14.8 us -> 1.35 us
    unnamed x7 -> x0, waiting for transfers between devices: 60.5 us -> none
    pallas_call x0 -> x1, Pallas kernels: none -> 56.2 us  [back(): pl.pallas_call(back_kernel, out_shape=(shape((TOK, D), BF), shape((TOK, D...]
    dot_general x14 -> x0, matrix products: 22.8 us -> none  [the longest x1 3.24 us: shards(): jnp.einsum('kgts,tkgd->skd', softmaxed_low, grad_mixed, preferred_element...]
    reshape x1 -> x0, waiting for transfers between devices: 20.8 us -> none  [shards(): grad_value.astype(jnp.bfloat16).reshape(tok_count, KV_HEADS * HEAD_DIM)]
    pallas_call x1, Pallas kernels: 72.8 us -> 54.5 us  [total(): pl.pallas_call(total_kernel, out_shape=(shape((D, D), BF),) * 3 + (shape(...]
    another operation x5 -> x1, local copies, waits for them, and re-layouts: 12.4 us -> 0.08 us  [shards(): narrow[4, :TOK].reshape(16, 8)[:, :2].reshape(EXPERTS).astype(jnp.int32)]
    select_n x1 -> x0, other arithmetic: 5.92 us -> none  [by_place(): jnp.where(core == 0, rows, rows.transpose(1, 0, 2, 3)).reshape(16, TOK, D)]
    transpose x1 -> x0, other arithmetic: 5.52 us -> none  [shards(): parts = parts.reshape(2, 3, D, 4, TOK).transpose(0, 3, 1, 2, 4)]
  transfers between devices with their start and end apart: 5 -> 0, of which waited for: 4 -> 0; matrix products, arithmetic and copies ran while one was open for 21% -> 0% of each run, Pallas kernels for 18% -> 0%
where the time goes in v3:
time: 263 us
  Pallas kernels  241 us (92%)
  local copies, waits for them, and re-layouts  14.2 us (5%)
  other arithmetic  6.7 us (3%)
    pallas_call x1, Pallas kernels, moe(): pl.pallas_call(moe_kernel, out_shape=(shape((TOK, D), F32), shape((16, TO...  77.5 us
    pallas_call x1, Pallas kernels, back(): pl.pallas_call(back_kernel, out_shape=(shape((TOK, D), BF), shape((TOK, D...  56.2 us
    pallas_call x1, Pallas kernels, total(): pl.pallas_call(total_kernel, out_shape=(shape((D, D), BF),) * 3 + (shape(...  54.5 us
    pallas_call x1, Pallas kernels, front(): pl.pallas_call(front_kernel, out_shape=(shape((TOK, D), F32), shape((TOK,...  52.6 us
    unnamed x21, local copies, waits for them, and re-layouts  7 us

profile of v3, /device:TPU:1, one launch (start us, length us, event | category | flops | bytes accessed | tf_op | source)
XLA Modules:
  0.0 263.0 jit_solution(13176015554785429853)
XLA Ops:
  1.3 1.4 copy.36.routes_ref
  2.7 1.7 copy.35.router_ref
  4.4 52.6 %front.1 = (f32[128,1024]{1,0:T(8,128)}, bf16[128,1024]{1,0:T(8,128)(2,1)}, f32[16,8,128]{2,1,0:T(8,128)}, f32[128,128]{1,0:T(8,128)}, bf16[128,1024]{1,0:T(8,12...) custom-call(bf16[128,1024]{1,0:T(8,128)(2,1)} %tok_ref.3, ...), custom_call_target="tpu_custom_call" | custom-call | tf_op jit(solution)/shard_map/front/pallas_call | solution.py:773
  57.0 77.5 %experts.1 = (f32[128,1024]{1,0:T(8,128)}, bf16[16,128,1024]{2,1,0:T(8,128)(2,1)}, f32[16,8,128]{2,1,0:T(8,128)}, bf16[2,1024,512]{2,1,0:T(8,128)(2,1)}, bf16[2,...) custom-call(bf16[128,1024]{1,0:T(8,128)(2,1)} %get-tuple-element.44.x_ref, f32[16,8,128]{2,1,0:T(8,128)} %get-tuple-element.45.gt_ref, ...), custom_call_target="tpu_custom_call" | custom-call | tf_op jit(solution)/shard_map/experts/pallas_call | solution.py:444
  134.4 56.2 %back.1 = (bf16[128,1024]{1,0:T(8,128)(2,1)}, f32[128,1024]{1,0:T(8,128)}, bf16[1024,1024]{1,0:T(8,128)(2,1)}, bf16[1024,1024]{1,0:T(8,128)(2,1)}, bf16[1024,102...) custom-call(f32[128,1024]{1,0:T(8,128)} %get-tuple-element.50.rows_r, ...), custom_call_target="tpu_custom_call" | custom-call | tf_op jit(solution)/shard_map/back/pallas_call | solution.py:1128
  190.7 54.5 %total.1 = (bf16[1024,1024]{1,0:T(8,128)(2,1)}, bf16[1024,1024]{1,0:T(8,128)(2,1)}, bf16[1024,1024]{1,0:T(8,128)(2,1)}, f32[128,1024]{1,0:T(8,128)}) custom-call(bf16[1024,1024]{1,0:T(8,128)(2,1)} %get-tuple-element.64.a_hbm, bf16[1024,1024]{1,0:T(8,128)(2,1)} %get-tuple-element.65.b_hbm, bf16[1024,1024]{1,0:T(8,128)(2,1)} %get-tuple-element.66.c_hbm, ...), custom_call_target="tpu_custom_call" | custom-call | tf_op jit(solution)/shard_map/total/pallas_call | solution.py:1410
  245.1 0.7 slice_reduce_fusion
  245.8 0.1 reshape_squeeze.3
  245.9 0.6 convert_element_type.19
  246.5 1.4 fusion.1
  248.0 1.1 slice.30
  249.0 0.7 reshape.45
  249.8 0.0 copy-start.1
  249.8 4.2 %convert_element_type.15 = f32[1024,1024]{1,0:T(8,128)} convert(bf16[1024,1024]{1,0:T(8,128)(2,1)} %get-tuple-element.68) | non-fusion elementwise | flops 1048576 | bytes 6291456 | tf_op jit(solution)/shard_map/convert_element_type | solution.py:1493
  254.0 0.0 copy-done.1
  254.0 0.0 copy-start
  254.0 2.5 convert_element_type.17
  256.5 0.0 copy-done
  256.5 0.0 copy-start.6
  256.5 0.0 copy-start.5
  256.5 0.0 copy-start.4
  256.5 2.6 fusion
  259.1 0.0 copy-start.3
  259.1 0.0 copy-start.2
  259.1 0.0 copy-done.6
  259.1 0.7 copy.45
  259.8 0.0 copy-done.5
  259.8 0.8 copy.46
  260.6 0.0 copy-done.4
  260.6 0.8 copy.47
  261.4 0.0 copy-done.3
  261.4 0.8 copy.48
  262.2 0.0 copy-done.2
  262.2 0.8 copy.49
  (1 shorter events, 0.0 us)
Async XLA Ops:
  249.8 4.2 %copy-start.1 = (bf16[1024,1024]{1,0:T(8,128)(2,1)S(1)}, bf16[1024,1024]{1,0:T(8,128)(2,1)}, u32[]{:S(2)}) copy-start(bf16[1024,1024]{1,0:T(8,128)(2,1)} %get-tuple-element.70) | copy-start | bytes 6291460
  254.0 2.5 copy-start
  256.5 2.6 copy-start.6
  256.5 3.3 %copy-start.5 = (f32[128,1024]{1,0:T(8,128)S(1)}, f32[128,1024]{1,0:T(8,128)}, u32[]{:S(2)}) copy-start(f32[128,1024]{1,0:T(8,128)} %get-tuple-element.93) | copy-start | bytes 1572868
  256.5 4.1 %copy-start.4 = (f32[1024,128]{1,0:T(8,128)S(1)}, f32[1024,128]{1,0:T(8,128)}, u32[]{:S(2)}) copy-start(f32[1024,128]{1,0:T(8,128)} %get-tuple-element.72) | copy-start | bytes 1572868
  259.1 2.3 copy-start.3
  259.1 3.1 %copy-start.2 = (f32[128,1024]{1,0:T(8,128)S(1)}, f32[128,1024]{1,0:T(8,128)}, u32[]{:S(2)}) copy-start(f32[128,1024]{1,0:T(8,128)} %get-tuple-element.74) | copy-start | bytes 1572868

commit v4 on v3

--- a/solution.py
+++ b/solution.py
@@ -81,418 +81,6 @@
 
 def slab(buffer, p, q):
     return buffer.at[wrap(p) * 4 + wrap(q)]
-
-
-def moe_kernel(
-    x_ref, gt_ref, u_hbm, wg_hbm, wu_hbm, wd_hbm,
-    grad_out, o_hbm, gg_out, dwg_hbm, dwu_hbm, dwd_hbm,
-    xs, us, wg, wu, wd, gin, rank, ggo, picks, rows, rows_up, slot_grads, acts, gparts, uparts,
-    outs, pairs, o_buf, p_buf, rb, rc, rd, re, dwg, dwu, dwd,
-    send_sem, recv_sem, g_send, g_recv, gg_send, gg_recv, local_sem,
-):
-    p, q, y, core = place()
-    me = device(p, q, y, core)
-    right, left = device(p + 1, q, y, core), device(p - 1, q, y, core)
-    up, down = device(p, q + 1, y, core), device(p, q - 1, y, core)
-    others = [device(p + a, q + b, y, core) for a in range(4) for b in range(4) if a or b]
-    loads = [
-        pltpu.make_async_copy(src, dst, local_sem.at[i])
-        for i, (src, dst) in enumerate(((u_hbm, us), (wg_hbm, wg), (wu_hbm, wu), (wd_hbm, wd)))
-    ]
-    for load in loads:
-        load.start()
-    greet(others)
-    net = Sends(send_sem, recv_sem)
-    my_chip = chip_of(p, q, core)
-
-    own = slab(xs, p, q)
-    net.start(x_ref, own, 0, right)
-    net.start(x_ref, own, 1, left)
-    net.start(x_ref, own, 4, up)
-    net.start(x_ref, own, 8, down)
-
-    def gate_copy(i):
-        a, b = lax.div(i, 4), lax.rem(i, 4)
-        return pltpu.make_async_remote_copy(
-            src_ref=gt_ref.at[chip_of(p + a, q + b, core)],
-            dst_ref=gin.at[p * 4 + q],
-            send_sem=g_send.at[i],
-            recv_sem=g_recv.at[wrap(-a) * 4 + wrap(-b)],
-            device_id=device(p + a, q + b, y, core),
-            device_id_type=MESH,
-        )
-
-    def start_gate(i, _):
-        gate_copy(i).start()
-        return 0
-
-    lax.fori_loop(1, 16, start_gate, 0)
-    gin[p * 4 + q] = gt_ref[my_chip]
-    own[...] = x_ref[...]
-
-    s = slab(xs, p - 1, q)
-    net.arrived(s, 0)
-    net.start(s.at[0:64], s.at[0:64], 2, right)
-    net.start(s, s, 5, up)
-    s = slab(xs, p + 1, q)
-    net.arrived(s, 1)
-    net.start(s.at[64:128], s.at[64:128], 3, left)
-    net.start(s, s, 10, down)
-    s = slab(xs, p, q - 1)
-    net.arrived(s, 4)
-    net.start(s, s, 12, up)
-    s = slab(xs, p + 2, q)
-    net.arrived(s.at[0:64], 2)
-    net.arrived(s.at[64:128], 3)
-    net.start(s, s, 11, down)
-    s = slab(xs, p - 1, q - 1)
-    net.arrived(s, 5)
-    net.start(s, s, 13, up)
-    s = slab(xs, p + 1, q)
-    net.start(s, s, 6, up)
-    s = slab(xs, p + 2, q)
-    net.start(s, s, 7, up)
-    s = slab(xs, p - 1, q)
-    net.start(s, s, 9, down)
-
-    def take_gate(i, _):
-        pltpu.make_async_copy(gin.at[0], gin.at[0], g_recv.at[i]).wait()
-        return 0
-
-    lax.fori_loop(1, 16, take_gate, 0)
-    ids = lax.broadcasted_iota(jnp.int32, (TOK, TOK), 0)
-    cols = lax.broadcasted_iota(jnp.int32, (TOK, TOK), 1)
-    before = jnp.where(ids < cols, 1.0, 0.0).astype(BF)
-    routed = jnp.where(gin[...].reshape(TOK, TOK) > 0, 1.0, 0.0).astype(BF)
-    rank[...] = jnp.dot(routed, before, preferred_element_type=F32).reshape(16, 8, TOK)
-    for load in loads:
-        load.wait()
-    ggo[...] = jnp.zeros_like(ggo)
-    slot_ids = lax.broadcasted_iota(jnp.int32, (SLOTS, TOK), 0).astype(F32)
-
-    def source_of(g, j):
-        b = jnp.where(g == 0, 0, jnp.where(g == 1, 2, jnp.where(g == 2, 3, 1)))
-        a = jnp.where(j == 0, 0, jnp.where(j == 1, 3, jnp.where(j == 2, 1, 2)))
-        return wrap(p + a) * 4 + wrap(q + b)
-
-    def pick_source(g, j):
-        src = source_of(g, j)
-        token_rows, up_rows = xs[src], us[src]
-        base = pl.multiple_of(g * 4 * SLOTS + j * SLOTS, 16)
-        for e in range(2):
-            gate_row = gin[src, e : e + 1, :]
-            hit = (rank[src, e : e + 1, :] == slot_ids) & (gate_row > 0)
-            pick = jnp.where(hit, 1.0, 0.0)
-            pick_low = pick.astype(BF)
-            picks[src, e * SLOTS : (e + 1) * SLOTS, :] = pick_low
-            gate_col = jnp.sum(pick * gate_row, axis=1, keepdims=True)
-            rows[e, pl.ds(base, SLOTS), :] = jnp.dot(
-                pick_low, token_rows, preferred_element_type=F32
-            ).astype(BF)
-            picked = jnp.dot(pick_low, up_rows, preferred_element_type=F32)
-            rows_up[e, pl.ds(pl.multiple_of(j * SLOTS, 16), SLOTS), :] = picked.astype(BF)
-            slot_grads[e, pl.ds(base, SLOTS), :] = (picked * gate_col).astype(BF)
-
-    def run_expert(g, e):
-        base = pl.multiple_of(g * 4 * SLOTS, 16)
-        span = pl.ds(base, 4 * SLOTS)
-        taken = rows[e, span, :]
-        gate = jnp.dot(taken, wg[e], preferred_element_type=F32)
-        upv = jnp.dot(taken, wu[e], preferred_element_type=F32)
-        sig = 1.0 / (1.0 + jnp.exp(-gate))
-        silu = gate * sig
-        act = (silu * upv).astype(BF)
-        acts[e, span, :] = act
-        out = jnp.dot(act, wd[e], preferred_element_type=F32).astype(BF)
-        outs[e] = out
-        gg_col = jnp.sum(out.astype(F32) * rows_up[e].astype(F32), axis=1, keepdims=True)
-        for j in range(4):
-            src = source_of(g, j)
-            pick = picks[src, pl.ds(pl.multiple_of(e * SLOTS, 16), SLOTS), :].astype(F32)
-            part = gg_col[j * SLOTS : (j + 1) * SLOTS]
-            ggo[src, pl.ds(e, 1), :] = jnp.sum(pick * part, axis=0, keepdims=True)
-        grad_act = lax.dot_general(
-            slot_grads[e, span, :], wd[e], (((1,), (1,)), ((), ())), preferred_element_type=F32
-        )
-        ggp = (grad_act * upv * sig * (1.0 + gate * (1.0 - sig))).astype(BF)
-        gup = (grad_act * silu).astype(BF)
-        gparts[e, span, :] = ggp
-        uparts[e, span, :] = gup
-        pair = lax.dot_general(ggp, wg[e], (((1,), (1,)), ((), ())), preferred_element_type=F32)
-        pair += lax.dot_general(gup, wu[e], (((1,), (1,)), ((), ())), preferred_element_type=F32)
-        pairs[e] = pair.astype(BF)
-
-    def spread(g, j):
-        src = source_of(g, j)
-        pick = picks[src]
-        span = pl.ds(pl.multiple_of(j * SLOTS, 16), SLOTS)
-        gates = jnp.concatenate(
-            [
-                pick[e * SLOTS : (e + 1) * SLOTS].astype(F32) * gin[src, e : e + 1, :]
-                for e in range(2)
-            ],
-            axis=0,
-        ).astype(BF)
-        both = jnp.concatenate([outs[0, span, :], outs[1, span, :]], axis=0)
-        o_buf[src] = lax.dot_general(
-            gates, both, (((0,), (0,)), ((), ())), preferred_element_type=F32
-        ).astype(BF)
-        both = jnp.concatenate([pairs[0, span, :], pairs[1, span, :]], axis=0)
-        p_buf[src] = lax.dot_general(
-            pick, both, (((0,), (0,)), ((), ())), preferred_element_type=F32
-        ).astype(BF)
-
-    def chunk(g):
-        lax.fori_loop(0, 4, lambda j, c: (pick_source(g, j), c)[1], 0)
-        lax.fori_loop(0, 2, lambda e, c: (run_expert(g, e), c)[1], 0)
-        lax.fori_loop(0, 4, lambda j, c: (spread(g, j), c)[1], 0)
-
-    OFF = (0, -1, 1, 2)
-    R = 16
-
-    def make(source, target, recv, to, index):
-        return pltpu.make_async_remote_copy(
-            src_ref=source,
-            dst_ref=target,
-            send_sem=send_sem.at[index],
-            recv_sem=recv_sem.at[recv],
-            device_id=to,
-            device_id_type=MESH,
-        )
-
-    first = len(net.made)
-    far = [
-        lambda: make(slab(xs, p + 1, q + 1), slab(xs, p + 1, q + 1), 14, down, first),
-        lambda: make(slab(xs, p + 2, q + 1), slab(xs, p + 2, q + 1), 15, down, first + 1),
-    ]
-    bounce = [
-        (lambda j=j: make(slab(p_buf, p + OFF[j], q + 2), rb.at[j], R + j, up if j < 2 else down, first + 2 + j))
-        for j in range(4)
-    ]
-    to_down = [
-        (lambda j=j: make(slab(p_buf, p + OFF[j], q - 1), rc.at[4 + j], R + 8 + j, down, first + 6 + j))
-        for j in range(4)
-    ]
-    to_up = [
-        (lambda j=j: make(slab(p_buf, p + OFF[j], q + 1), rc.at[j], R + 4 + j, up, first + 10 + j))
-        for j in range(4)
-    ]
-
-    def add_bounce(j):
-        net.arrived(rb.at[j], R + j)
-        target = slab(p_buf, p + OFF[j], q + 1 if j < 2 else q - 1)
-        target[...] = (target[...].astype(F32) + rb[j].astype(F32)).astype(BF)
-
-    def step(g, carry):
-        @pl.when(g == 1)
-        def _():
-            net.arrived(slab(xs, p + 1, q + 1), 10)
-            far[0]().start()
-            net.arrived(slab(xs, p + 2, q + 1), 11)
-            far[1]().start()
-            net.arrived(slab(xs, p, q + 2), 12)
-            net.arrived(slab(xs, p - 1, q + 2), 13)
-            net.arrived(slab(xs, p + 1, q + 2), 14)
-            net.arrived(slab(xs, p + 2, q + 2), 15)
-
-        @pl.when(g == 2)
-        def _():
-            net.arrived(slab(xs, p + 1, q - 1), 6)
-            net.arrived(slab(xs, p + 2, q - 1), 7)
-
-        @pl.when(g == 3)
-        def _():
-            net.arrived(slab(xs, p, q + 1), 8)
-            net.arrived(slab(xs, p - 1, q + 1), 9)
-
-        chunk(g)
-
-        @pl.when(g == 1)
-        def _():
-            for j in range(4):
-                bounce[j]().start()
-
-        @pl.when(g == 2)
-        def _():
-            to_down[0]().start()
-            to_down[1]().start()
-            for j in (3, 2):
-                add_bounce(j)
-                to_down[j]().start()
-
-        @pl.when(g == 3)
-        def _():
-            to_up[3]().start()
-            to_up[2]().start()
-            for j in (1, 0):
-                add_bounce(j)
-                to_up[j]().start()
-
-        return carry
-
-    lax.fori_loop(0, 4, step, 0)
-
-    def gg_copy(i):
-        a, b = lax.div(i, 4), lax.rem(i, 4)
-        return pltpu.make_async_remote_copy(
-            src_ref=ggo.at[wrap(p + a) * 4 + wrap(q + b)],
-            dst_ref=gg_out.at[my_chip],
-            send_sem=gg_send.at[i],
-            recv_sem=gg_recv.at[wrap(-a) * 4 + wrap(-b)],
-            device_id=device(p + a, q + b, y, core),
-            device_id_type=MESH,
-        )
-
-    def start_gg(i, _):
-        gg_copy(i).start()
-        return 0
-
-    lax.fori_loop(1, 16, start_gg, 0)
-    gg_out[my_chip] = ggo[p * 4 + q]
-    o_store = pltpu.make_async_copy(o_buf, o_hbm, local_sem.at[4])
-    o_store.start()
-
-    def weight_tile(e, t):
-        cols = pl.ds(pl.multiple_of(t * 256, 256), 256)
-        dims = (((0,), (0,)), ((), ()))
-        lhs = rows[e, :, cols]
-        dwg[e, cols, :] = lax.dot_general(lhs, gparts[e], dims, preferred_element_type=F32).astype(BF)
-        dwu[e, cols, :] = lax.dot_general(lhs, uparts[e], dims, preferred_element_type=F32).astype(BF)
-        dwd[e, :, cols] = lax.dot_general(
-            acts[e], slot_grads[e, :, cols], dims, preferred_element_type=F32
-        ).astype(BF)
-
-    def weight_grads(e):
-        lax.fori_loop(0, 4, lambda t, c: (weight_tile(e, t), c)[1], 0)
-
-    weight_grads(0)
-
-    def gather_sum(j):
-        net.arrived(rc.at[j], R + 4 + j)
-        net.arrived(rc.at[4 + j], R + 8 + j)
-        target = slab(p_buf, p + OFF[j], q)
-        target[...] = (
-            target[...].astype(F32) + rc[j].astype(F32) + rc[4 + j].astype(F32)
-        ).astype(BF)
-
-    last = first + 14
-    lo, hi = pl.ds(0, 64), pl.ds(64, 64)
-    far_slab, next_slab, prev_slab = slab(p_buf, p + 2, q), slab(p_buf, p + 1, q), slab(p_buf, p - 1, q)
-    tail = [
-        make(far_slab.at[lo], rd.at[lo], R + 12, right, last),
-        make(far_slab.at[hi], rd.at[hi], R + 13, left, last + 1),
-        make(next_slab.at[hi], re.at[0, hi], R + 14, right, last + 2),
-        make(prev_slab.at[lo], re.at[1, lo], R + 15, left, last + 3),
-        make(next_slab.at[lo], re.at[0, lo], R + 16, right, last + 4),
-        make(prev_slab.at[hi], re.at[1, hi], R + 17, left, last + 5),
-    ]
-    gather_sum(3)
-    tail[0].start()
-    tail[1].start()
-    gather_sum(2)
-    tail[2].start()
-    gather_sum(1)
-    tail[3].start()
-    net.arrived(rd.at[lo], R + 12)
-    next_slab[lo] = (next_slab[lo].astype(F32) + rd[lo].astype(F32)).astype(BF)
-    tail[4].start()
-    net.arrived(rd.at[hi], R + 13)
-    prev_slab[hi] = (prev_slab[hi].astype(F32) + rd[hi].astype(F32)).astype(BF)
-    tail[5].start()
-    gather_sum(0)
-    weight_grads(1)
-    stores = [
-        pltpu.make_async_copy(src, dst, local_sem.at[i])
-        for i, (src, dst) in enumerate(((dwg, dwg_hbm), (dwu, dwu_hbm), (dwd, dwd_hbm)))
-    ]
-    for store in stores:
-        store.start()
-    net.arrived(re.at[0, hi], R + 14)
-    net.arrived(re.at[1, lo], R + 15)
-    net.arrived(re.at[0, lo], R + 16)
-    net.arrived(re.at[1, hi], R + 17)
-    grad_out[...] = slab(p_buf, p, q)[...].astype(F32) + re[0].astype(F32) + re[1].astype(F32)
-
-    def take_gg(i, _):
-        pltpu.make_async_copy(ggo.at[0], ggo.at[0], gg_recv.at[i]).wait()
-        return 0
-
-    lax.fori_loop(1, 16, take_gg, 0)
-    net.drain()
-    for copy in far + bounce + to_down + to_up:
-        copy().wait_send()
-    for copy in tail:
-        copy.wait_send()
-
-    def drain_small(i, _):
-        gate_copy(i).wait_send()
-        gg_copy(i).wait_send()
-        return 0
-
-    lax.fori_loop(1, 16, drain_small, 0)
-    o_store.wait()
-    for store in stores:
-        store.wait()
-
-
-def moe(x, gt, u, wg, wu, wd):
-    any_space = pl.BlockSpec(memory_space=pl.ANY)
-    vmem = pl.BlockSpec(memory_space=pltpu.VMEM)
-    shape = jax.ShapeDtypeStruct
-    slots = 16 * SLOTS
-    dma = pltpu.SemaphoreType.DMA
-    return pl.pallas_call(
-        moe_kernel,
-        out_shape=(
-            shape((TOK, D), F32),
-            shape((16, TOK, D), BF),
-            shape((16, 8, TOK), F32),
-            shape((2, D, FF), BF),
-            shape((2, D, FF), BF),
-            shape((2, FF, D), BF),
-        ),
-        in_specs=[vmem, vmem, any_space, any_space, any_space, any_space],
-        out_specs=(vmem, any_space, vmem, any_space, any_space, any_space),
-        scratch_shapes=[
-            pltpu.VMEM((16, TOK, D), BF),
-            pltpu.VMEM((16, TOK, D), BF),
-            pltpu.VMEM((2, D, FF), BF),
-            pltpu.VMEM((2, D, FF), BF),
-            pltpu.VMEM((2, FF, D), BF),
-            pltpu.VMEM((16, 8, TOK), F32),
-            pltpu.VMEM((16, 8, TOK), F32),
-            pltpu.VMEM((16, 8, TOK), F32),
-            pltpu.VMEM((16, 2 * SLOTS, TOK), BF),
-            pltpu.VMEM((2, slots, D), BF),
-            pltpu.VMEM((2, 4 * SLOTS, D), BF),
-            pltpu.VMEM((2, slots, D), BF),
-            pltpu.VMEM((2, slots, FF), BF),
-            pltpu.VMEM((2, slots, FF), BF),
-            pltpu.VMEM((2, slots, FF), BF),
-            pltpu.VMEM((2, 4 * SLOTS, D), BF),
-            pltpu.VMEM((2, 4 * SLOTS, D), BF),
-            pltpu.VMEM((16, TOK, D), BF),
-            pltpu.VMEM((16, TOK, D), BF),
-            pltpu.VMEM((4, TOK, D), BF),
-            pltpu.VMEM((8, TOK, D), BF),
-            pltpu.VMEM((TOK, D), BF),
-            pltpu.VMEM((2, TOK, D), BF),
-            pltpu.VMEM((2, D, FF), BF),
-            pltpu.VMEM((2, D, FF), BF),
-            pltpu.VMEM((2, FF, D), BF),
-            dma((40,)),
-            dma((34,)),
-            dma((16,)),
-            dma((16,)),
-            dma((16,)),
-            dma((16,)),
-            dma((5,)),
-        ],
-        compiler_params=pltpu.CompilerParams(
-            collective_id=1, has_side_effects=True, vmem_limit_bytes=VMEM_BYTES
-        ),
-        name="experts",
-    )(x, gt, u, wg, wu, wd)
 
 
 HALF = HEAD_DIM // 2
@@ -600,11 +188,11 @@
         self.send(self.slab(2, 0), 7, self.up)
         self.send(self.slab(-1, 0), 9, self.down)
 
-    def fourth(self):
-        for a, recv, far in ((1, 10, 14), (2, 11, 15)):
-            s = self.slab(a, 1)
-            self.arrived(s, recv)
-            self.send(s, far, self.down)
+    def fourth(self, which):
+        a, recv, far = ((1, 10, 14), (2, 11, 15))[which]
+        s = self.slab(a, 1)
+        self.arrived(s, recv)
+        self.send(s, far, self.down)
 
     def finish(self):
         for a, b, recv in (
@@ -614,20 +202,26 @@
             self.arrived(self.slab(a, b), recv)
 
 
-def front_kernel(
+def main_kernel(
     tok_ref, wq_hbm, wk_hbm, wv_hbm, wo_hbm, ga_ref, gm_ref, router_ref, cot_ref, routes_ref,
     len_ref, cos_ref, sin_ref, wgs_hbm, wus_hbm, wds_hbm,
-    hidden_ref, x_ref, gt_ref, gates_ref, mixed_ref, query_ref, kv_ref, probs_hbm,
-    u_all, wg_all, wu_all, wd_all,
-    wq, wk, wv, wo, u_own, kv, probs, bias,
-    send_sem, recv_sem, local_sem,
+    hidden_ref, x_ref, gates_ref, mixed_ref, query_ref, kv_ref, grad_out, gg_out,
+    probs_hbm, o_hbm, dwg_hbm, dwu_hbm, dwd_hbm,
+    wqo, wk, wv, u_own, kv, probs, bias, gt,
+    xs, us, wg, wu, wd, gin, rank, ggo, picks, rows, slot_grads, acts, gparts, uparts,
+    outs, pairs, o_buf, p_buf, rb, rc, rd, re, dwg, dwu,
+    send_sem, recv_sem, g_send, g_recv, gg_send, gg_recv, local_sem,
 ):
     p, q, y, core = place()
     spot = (p, q, y, core)
-    sibling = device(p, q, y, 1 - core)
-    sibling = (sibling[0] * 0 + chip_of(p, q, core) * 2 + 1 - core, y)
+    sibling = (chip_of(p, q, core) * 2 + 1 - core, y)
     ahead, behind = device(p, q, y + 1, core), device(p, q, y - 1, core)
+    up, down = device(p, q + 1, y, core), device(p, q - 1, y, core)
+    right, left = device(p + 1, q, y, core), device(p - 1, q, y, core)
+    others = [device(p + a, q + b, y, core) for a in range(4) for b in range(4) if a or b]
+    my_chip = chip_of(p, q, core)
     net = Sends(send_sem, recv_sem)
+    wq, wo = wqo.at[0], wqo.at[1]
     loads = {
         name: pltpu.make_async_copy(src, dst, local_sem.at[i])
         for i, (name, src, dst) in enumerate(
@@ -636,16 +230,53 @@
     }
     for load in loads.values():
         load.start()
-    gather = PlaneGather(net, spot, u_all, 0)
+    gather = PlaneGather(net, spot, us, 0)
+    tokens_in = PlaneGather(net, spot, xs, 42)
     first = pl.multiple_of(y * TOK, TOK)
     row = lax.broadcasted_iota(jnp.int32, (TOK, 1), 0) + y * TOK
     length = len_ref[0]
     u_own[...] = jnp.where(row < length, cot_ref[...].astype(F32), 0.0).astype(BF)
-    greet([gather.right, gather.left, gather.up, gather.down, ahead, behind, sibling])
+    greet(others + [ahead, behind, sibling])
     gather.begin(u_own)
     keep_own = pltpu.make_async_copy(u_own, gather.slab(0, 0), local_sem.at[4])
     keep_own.start()
 
+    def weight(a, e, yy, rows=None):
+        block = pl.ds(pl.multiple_of(wrap(yy) * TOK, TOK), TOK)
+        if a == 2:
+            return wd.at[e, block, :]
+        full = (wg, wu)[a]
+        return full.at[e, :, block] if rows is None else full.at[e, rows, block]
+
+    shards = (wgs_hbm.at[0], wus_hbm.at[0], wds_hbm.at[0])
+    top, bottom = pl.ds(0, 512), pl.ds(512, 512)
+    keep = []
+
+    def send_weight(a):
+        net.start(shards[a], weight(a, core, y), 20 + a, ahead)
+        net.start(shards[a], weight(a, core, y), 23 + a, behind)
+        net.start(shards[a], weight(a, core, y), 30 + a, sibling)
+        keep.append(pltpu.make_async_copy(shards[a], weight(a, core, y), local_sem.at[5 + a]))
+        keep[-1].start()
+
+    def pass_weight(a):
+        before, after = weight(a, core, y - 1), weight(a, core, y + 1)
+        net.arrived(before, 20 + a)
+        if a == 0:
+            net.start(before, before, 26, ahead)
+        if a == 1:
+            spot = weight(1, core, y - 1, top)
+            net.start(spot, spot, 27, ahead)
+        net.start(before, before, 33 + a, sibling)
+        net.arrived(after, 23 + a)
+        if a == 1:
+            spot = weight(1, core, y + 1, bottom)
+            net.start(spot, spot, 28, behind)
+        if a == 2:
+            net.start(after, after, 29, behind)
+        net.start(after, after, 36 + a, sibling)
+
+    send_weight(0)
     tokens = tok_ref[...].astype(F32)
     normed = (tokens * root(tokens) * ga_ref[...]).astype(BF)
     cosine, sine = cos_ref[pl.ds(first, TOK), :], sin_ref[pl.ds(first, TOK), :]
@@ -659,23 +290,6 @@
     own = kv.at[y]
     net.start(own, own, 16, ahead)
     net.start(own, own, 17, behind)
-
-    def weight(a, e, yy, rows=None):
-        block = pl.ds(pl.multiple_of(wrap(yy) * TOK, TOK), TOK)
-        if a == 2:
-            return wd_all.at[e, block, :]
-        full = (wg_all, wu_all)[a]
-        return full.at[e, :, block] if rows is None else full.at[e, rows, block]
-
-    shards = (wgs_hbm.at[0], wus_hbm.at[0], wds_hbm.at[0])
-    top, bottom = pl.ds(0, 512), pl.ds(512, 512)
-    keep = []
-    for a in range(3):
-        net.start(shards[a], weight(a, core, y), 20 + a, ahead)
-        net.start(shards[a], weight(a, core, y), 23 + a, behind)
-        net.start(shards[a], weight(a, core, y), 30 + a, sibling)
-        keep.append(pltpu.make_async_copy(shards[a], weight(a, core, y), local_sem.at[5 + a]))
-        keep[-1].start()
 
     loads["q"].wait()
     queries = jnp.dot(normed, wq[...], preferred_element_type=F32)
@@ -695,6 +309,10 @@
     s = kv.at[wrap(y + 2)]
     net.arrived(s.at[0:64], 18)
     net.arrived(s.at[64:128], 19)
+    send_weight(1)
+    send_weight(2)
+    pass_weight(0)
+    gather.fourth(0)
 
     def attend(c, carry):
         span = pl.ds(pl.multiple_of(c * 128, 128), 128)
@@ -715,20 +333,8 @@
             mixed_ref[:, mine] = unstack_heads(out, half).astype(BF)
         return carry
 
-    lax.fori_loop(0, 2, attend, 0)
-    gather.fourth()
-    for a in range(3):
-        net.arrived(weight(a, core, y - 1), 20 + a)
-    net.start(weight(0, core, y - 1), weight(0, core, y - 1), 26, ahead)
-    net.start(weight(1, core, y - 1, top), weight(1, core, y - 1, top), 27, ahead)
-    for a in range(3):
-        net.arrived(weight(a, core, y + 1), 23 + a)
-    net.start(weight(1, core, y + 1, bottom), weight(1, core, y + 1, bottom), 28, behind)
-    net.start(weight(2, core, y + 1), weight(2, core, y + 1), 29, behind)
-    for a in range(3):
-        net.start(weight(a, core, y - 1), weight(a, core, y - 1), 33 + a, sibling)
-        net.start(weight(a, core, y + 1), weight(a, core, y + 1), 36 + a, sibling)
-    lax.fori_loop(2, 4, attend, 0)
+    lax.fori_loop(0, 4, attend, 0)
+    gather.fourth(1)
     keep_probs = pltpu.make_async_copy(probs, probs_hbm, local_sem.at[8])
     keep_probs.start()
     loads["o"].wait()
@@ -736,6 +342,8 @@
     hidden_ref[...] = hidden
     x = (hidden * root(hidden) * gm_ref[...]).astype(BF)
     x_ref[...] = x
+    tokens_in.begin(x_ref)
+    tokens_in.slab(0, 0)[...] = x
     wide = jnp.dot(router_ref[...], widen(), preferred_element_type=F32).astype(BF)
     logits = jnp.dot(x, wide, preferred_element_type=F32)
     routed = routed_mask(routes_ref[...])
@@ -743,68 +351,401 @@
     weights = jnp.where(routed, jnp.exp(logits - jnp.max(logits, axis=1, keepdims=True)), 0.0)
     weights = weights * (1.0 / jnp.sum(weights, axis=1, keepdims=True))
     gates_ref[...] = weights
-    gt_ref[...] = weights.T.reshape(16, 8, TOK)
+    gt[...] = weights.T.reshape(16, 8, TOK)
+
+    def gate_copy(i):
+        a, b = lax.div(i, 4), lax.rem(i, 4)
+        return pltpu.make_async_remote_copy(
+            src_ref=gt.at[chip_of(p + a, q + b, core)],
+            dst_ref=gin.at[p * 4 + q],
+            send_sem=g_send.at[i],
+            recv_sem=g_recv.at[wrap(-a) * 4 + wrap(-b)],
+            device_id=device(p + a, q + b, y, core),
+            device_id_type=MESH,
+        )
+
+    def start_gate(i, _):
+        gate_copy(i).start()
+        return 0
+
+    lax.fori_loop(1, 16, start_gate, 0)
+    gin[p * 4 + q] = gt[my_chip]
+
     kv_ref[...] = kv[...]
-
+    tokens_in.second()
+    pass_weight(1)
+    tokens_in.third()
+    pass_weight(2)
+
+    def take_gate(i, _):
+        pltpu.make_async_copy(gin.at[0], gin.at[0], g_recv.at[i]).wait()
+        return 0
+
+    lax.fori_loop(1, 16, take_gate, 0)
+    ids = lax.broadcasted_iota(jnp.int32, (TOK, TOK), 0)
+    cols = lax.broadcasted_iota(jnp.int32, (TOK, TOK), 1)
+    before = jnp.where(ids < cols, 1.0, 0.0).astype(BF)
+    routed = jnp.where(gin[...].reshape(TOK, TOK) > 0, 1.0, 0.0).astype(BF)
+    rank[...] = jnp.dot(routed, before, preferred_element_type=F32).reshape(16, 8, TOK)
+    gather.finish()
+    ggo[...] = jnp.zeros_like(ggo)
+    slot_ids = lax.broadcasted_iota(jnp.int32, (SLOTS, TOK), 0).astype(F32)
+
+    def source_of(g, j):
+        side = jnp.where((j < 2) == (g == 1), 3, 1)
+        b = jnp.where(g == 0, 0, jnp.where(g == 2, 2, side))
+        a = jnp.where(j == 0, 0, jnp.where(j == 1, 3, jnp.where(j == 2, 1, 2)))
+        return wrap(p + a) * 4 + wrap(q + b)
+
+    def pick_source(g, j):
+        src = source_of(g, j)
+        token_rows, up_rows = xs[src], us[src]
+        base = pl.multiple_of(g * 4 * SLOTS + j * SLOTS, 16)
+        for e in range(2):
+            gate_row = gin[src, e : e + 1, :]
+            hit = (rank[src, e : e + 1, :] == slot_ids) & (gate_row > 0)
+            pick = jnp.where(hit, 1.0, 0.0)
+            pick_low = pick.astype(BF)
+            picks[src, e * SLOTS : (e + 1) * SLOTS, :] = pick_low
+            gate_col = jnp.sum(pick * gate_row, axis=1, keepdims=True)
+            rows[e, pl.ds(base, SLOTS), :] = jnp.dot(
+                pick_low, token_rows, preferred_element_type=F32
+            ).astype(BF)
+            picked = jnp.dot(pick_low, up_rows, preferred_element_type=F32)
+            wqo[e, pl.ds(base, SLOTS), :] = picked.astype(BF)
+            slot_grads[e, pl.ds(base, SLOTS), :] = (picked * gate_col).astype(BF)
+
+    def run_expert(g, e):
+        base = pl.multiple_of(g * 4 * SLOTS, 16)
+        span = pl.ds(base, 4 * SLOTS)
+        taken = rows[e, span, :]
+        gate = jnp.dot(taken, wg[e], preferred_element_type=F32)
+        upv = jnp.dot(taken, wu[e], preferred_element_type=F32)
+        sig = 1.0 / (1.0 + jnp.exp(-gate))
+        silu = gate * sig
+        act = (silu * upv).astype(BF)
+        acts[e, span, :] = act
+        grad_act = lax.dot_general(
+            slot_grads[e, span, :], wd[e], (((1,), (1,)), ((), ())), preferred_element_type=F32
+        )
+        ggp = (grad_act * upv * sig * (1.0 + gate * (1.0 - sig))).astype(BF)
+        gup = (grad_act * silu).astype(BF)
+        gparts[e, span, :] = ggp
+        uparts[e, span, :] = gup
+        pair = lax.dot_general(ggp, wg[e], (((1,), (1,)), ((), ())), preferred_element_type=F32)
+        pair += lax.dot_general(gup, wu[e], (((1,), (1,)), ((), ())), preferred_element_type=F32)
+        pairs[e] = pair.astype(BF)
+
+    def spread(g, j):
+        src = source_of(g, j)
+        span = pl.ds(pl.multiple_of(j * SLOTS, 16), SLOTS)
+        both = jnp.concatenate([pairs[0, span, :], pairs[1, span, :]], axis=0)
+        p_buf[src] = lax.dot_general(
+            picks[src], both, (((0,), (0,)), ((), ())), preferred_element_type=F32
+        ).astype(BF)
+
+    def run_output(g, e):
+        span = pl.ds(pl.multiple_of(g * 4 * SLOTS, 16), 4 * SLOTS)
+        out = jnp.dot(acts[e, span, :], wd[e], preferred_element_type=F32).astype(BF)
+        outs[e] = out
+        gg_col = jnp.sum(out.astype(F32) * wqo[e, span, :].astype(F32), axis=1, keepdims=True)
+        for j in range(4):
+            src = source_of(g, j)
+            pick = picks[src, pl.ds(pl.multiple_of(e * SLOTS, 16), SLOTS), :].astype(F32)
+            part = gg_col[j * SLOTS : (j + 1) * SLOTS]
+            ggo[src, pl.ds(e, 1), :] = jnp.sum(pick * part, axis=0, keepdims=True)
+
+    def spread_output(g, j):
+        src = source_of(g, j)
+        pick = picks[src]
+        span = pl.ds(pl.multiple_of(j * SLOTS, 16), SLOTS)
+        gates = jnp.concatenate(
+            [
+                pick[e * SLOTS : (e + 1) * SLOTS].astype(F32) * gin[src, e : e + 1, :]
+                for e in range(2)
+            ],
+            axis=0,
+        ).astype(BF)
+        both = jnp.concatenate([outs[0, span, :], outs[1, span, :]], axis=0)
+        o_buf[src] = lax.dot_general(
+            gates, both, (((0,), (0,)), ((), ())), preferred_element_type=F32
+        ).astype(BF)
+
+    def output(g, carry):
+        lax.fori_loop(0, 2, lambda e, c: (run_output(g, e), c)[1], 0)
+        lax.fori_loop(0, 4, lambda j, c: (spread_output(g, j), c)[1], 0)
+        return carry
+
+    def pick(g):
+        lax.fori_loop(0, 4, lambda j, c: (pick_source(g, j), c)[1], 0)
+
+    OFF = (0, -1, 1, 2)
+    R = 58
+
+    def make(source, target, recv, to, index):
+        return pltpu.make_async_remote_copy(
+            src_ref=source,
+            dst_ref=target,
+            send_sem=send_sem.at[index],
+            recv_sem=recv_sem.at[recv],
+            device_id=to,
+            device_id_type=MESH,
+        )
+
+    first = 80
+    bounce = [
+        (lambda j=j: make(slab(p_buf, p + OFF[j], q + 2), rb.at[j], R + j, up if j < 2 else down, first + j))
+        for j in range(4)
+    ]
+    to_down = [
+        (lambda j=j: make(slab(p_buf, p + OFF[j], q - 1), rc.at[4 + j], R + 8 + j, down, first + 4 + j))
+        for j in range(4)
+    ]
+    to_up = [
+        (lambda j=j: make(slab(p_buf, p + OFF[j], q + 1), rc.at[j], R + 4 + j, up, first + 8 + j))
+        for j in range(4)
+    ]
+
+    def add_bounce(j):
+        net.arrived(rb.at[j], R + j)
+        target = slab(p_buf, p + OFF[j], q + 1 if j < 2 else q - 1)
+        target[...] = (target[...].astype(F32) + rb[j].astype(F32)).astype(BF)
+
+    def step(g, carry):
+        @pl.when(g == 2)
+        def _():
+            for j in range(4):
+                tokens_in.arrived(slab(xs, p + OFF[j], q + 2), 12 + j)
+
+        @pl.when(g == 3)
+        def _():
+            tokens_in.arrived(slab(xs, p + 1, q - 1), 6)
+            tokens_in.arrived(slab(xs, p + 2, q - 1), 7)
+            tokens_in.arrived(slab(xs, p, q + 1), 8)
+            tokens_in.arrived(slab(xs, p - 1, q + 1), 9)
+            for j in range(2):
+                to_down[j]().start()
+                to_up[3 - j]().start()
+
+        @pl.when(g >= 2)
+        def _():
+            pick(g)
+
+        lax.fori_loop(0, 2, lambda e, c: (run_expert(g, e), c)[1], 0)
+        lax.fori_loop(0, 4, lambda j, c: (spread(g, j), c)[1], 0)
+
+        @pl.when(g == 2)
+        def _():
+            for j in range(4):
+                bounce[j]().start()
+
+        @pl.when(g == 3)
+        def _():
+            for j in (3, 1, 2, 0):
+                add_bounce(j)
+                (to_up if j < 2 else to_down)[j]().start()
+
+        return carry
+
+    keep_own.wait()
+    pick(0)
+    tokens_in.fourth(0)
+    tokens_in.fourth(1)
+    pick(1)
     net.arrived(weight(0, core, y + 2), 26)
     net.arrived(weight(1, core, y + 2, top), 27)
     net.arrived(weight(1, core, y + 2, bottom), 28)
     net.arrived(weight(2, core, y + 2), 29)
     for a in range(3):
         net.start(weight(a, core, y + 2), weight(a, core, y + 2), 39 + a, sibling)
-    gather.finish()
-    for i, step in enumerate((0, -1, 1, 2)):
+    for i, ahead_by in enumerate((0, -1, 1, 2)):
         for a in range(3):
-            net.arrived(weight(a, 1 - core, y + step), 30 + 3 * i + a)
-    net.drain()
-    keep_own.wait()
-    keep_probs.wait()
+            net.arrived(weight(a, 1 - core, y + ahead_by), 30 + 3 * i + a)
     for copy in keep:
         copy.wait()
-
-
-def front(tokens, wq, wk, wv, wo, ga, gm, router, cotangent, routes, lengths, wg, wu, wd):
+    lax.fori_loop(0, 4, step, 0)
+    lax.fori_loop(0, 2, output, 0)
+
+    def weight_tile(e, t):
+        cols = pl.ds(pl.multiple_of(t * 256, 256), 256)
+        dims = (((0,), (0,)), ((), ()))
+        lhs = rows[e, :, cols]
+        dwg[e, cols, :] = lax.dot_general(lhs, gparts[e], dims, preferred_element_type=F32).astype(BF)
+        dwu[e, cols, :] = lax.dot_general(lhs, uparts[e], dims, preferred_element_type=F32).astype(BF)
+        us[4 * e : 4 * e + 4, :, cols] = (
+            lax.dot_general(acts[e], slot_grads[e, :, cols], dims, preferred_element_type=F32)
+            .astype(BF)
+            .reshape(4, TOK, 256)
+        )
+
+    def weight_grads(e):
+        lax.fori_loop(0, 4, lambda t, c: (weight_tile(e, t), c)[1], 0)
+
+    net.drain()
+    weight_grads(0)
+
+    def gather_sum(j):
+        net.arrived(rc.at[j], R + 4 + j)
+        net.arrived(rc.at[4 + j], R + 8 + j)
+        target = slab(p_buf, p + OFF[j], q)
+        target[...] = (
+            target[...].astype(F32) + rc[j].astype(F32) + rc[4 + j].astype(F32)
+        ).astype(BF)
+
+    last = first + 12
+    lo, hi = pl.ds(0, 64), pl.ds(64, 64)
+    far_slab, next_slab, prev_slab = slab(p_buf, p + 2, q), slab(p_buf, p + 1, q), slab(p_buf, p - 1, q)
+    tail = [
+        make(far_slab.at[lo], rd.at[lo], R + 12, right, last),
+        make(far_slab.at[hi], rd.at[hi], R + 13, left, last + 1),
+        make(next_slab.at[hi], re.at[0, hi], R + 14, right, last + 2),
+        make(prev_slab.at[lo], re.at[1, lo], R + 15, left, last + 3),
+        make(next_slab.at[lo], re.at[0, lo], R + 16, right, last + 4),
+        make(prev_slab.at[hi], re.at[1, hi], R + 17, left, last + 5),
+    ]
+    gather_sum(3)
+    tail[0].start()
+    tail[1].start()
+    gather_sum(2)
+    tail[2].start()
+    gather_sum(1)
+    tail[3].start()
+    lax.fori_loop(2, 4, output, 0)
+
+    def gg_copy(i):
+        a, b = lax.div(i, 4), lax.rem(i, 4)
+        return pltpu.make_async_remote_copy(
+            src_ref=ggo.at[wrap(p + a) * 4 + wrap(q + b)],
+            dst_ref=gg_out.at[my_chip],
+            send_sem=gg_send.at[i],
+            recv_sem=gg_recv.at[wrap(-a) * 4 + wrap(-b)],
+            device_id=device(p + a, q + b, y, core),
+            device_id_type=MESH,
+        )
+
+    def start_gg(i, _):
+        gg_copy(i).start()
+        return 0
+
+    lax.fori_loop(1, 16, start_gg, 0)
+    gg_out[my_chip] = ggo[p * 4 + q]
+    o_store = pltpu.make_async_copy(o_buf, o_hbm, local_sem.at[9])
+    o_store.start()
+    net.arrived(rd.at[lo], R + 12)
+    next_slab[lo] = (next_slab[lo].astype(F32) + rd[lo].astype(F32)).astype(BF)
+    tail[4].start()
+    net.arrived(rd.at[hi], R + 13)
+    prev_slab[hi] = (prev_slab[hi].astype(F32) + rd[hi].astype(F32)).astype(BF)
+    tail[5].start()
+    gather_sum(0)
+    weight_grads(1)
+    stores = [
+        pltpu.make_async_copy(src, dst, local_sem.at[10 + i])
+        for i, (src, dst) in enumerate(((dwg, dwg_hbm), (dwu, dwu_hbm), (us.at[0:8], dwd_hbm)))
+    ]
+    for store in stores:
+        store.start()
+    net.arrived(re.at[0, hi], R + 14)
+    net.arrived(re.at[1, lo], R + 15)
+    net.arrived(re.at[0, lo], R + 16)
+    net.arrived(re.at[1, hi], R + 17)
+    grad_out[...] = slab(p_buf, p, q)[...].astype(F32) + re[0].astype(F32) + re[1].astype(F32)
+
+    def take_gg(i, _):
+        pltpu.make_async_copy(ggo.at[0], ggo.at[0], gg_recv.at[i]).wait()
+        return 0
+
+    lax.fori_loop(1, 16, take_gg, 0)
+    for copy in bounce + to_down + to_up:
+        copy().wait_send()
+    for copy in tail:
+        copy.wait_send()
+
+    def drain_small(i, _):
+        gate_copy(i).wait_send()
+        gg_copy(i).wait_send()
+        return 0
+
+    lax.fori_loop(1, 16, drain_small, 0)
+    o_store.wait()
+    for store in stores:
+        store.wait()
+    keep_probs.wait()
+
+
+def main(tokens, wq, wk, wv, wo, ga, gm, router, cotangent, routes, lengths, wg, wu, wd):
     cosine, sine = turn_tables()
     any_space = pl.BlockSpec(memory_space=pl.ANY)
     vmem = pl.BlockSpec(memory_space=pltpu.VMEM)
     smem = pl.BlockSpec(memory_space=pltpu.SMEM)
     shape = jax.ShapeDtypeStruct
     dma = pltpu.SemaphoreType.DMA
+    slots = 16 * SLOTS
+    low = lambda *size: pltpu.VMEM(size, BF)
     return pl.pallas_call(
-        front_kernel,
+        main_kernel,
         out_shape=(
             shape((TOK, D), F32),
             shape((TOK, D), BF),
-            shape((16, 8, TOK), F32),
             shape((TOK, TOK), F32),
             shape((TOK, D), BF),
             shape((TOK, D), BF),
             shape((4, TOK, D), BF),
+            shape((TOK, D), F32),
+            shape((16, 8, TOK), F32),
             shape((8, 2 * TOK, 512), BF),
             shape((16, TOK, D), BF),
             shape((2, D, FF), BF),
             shape((2, D, FF), BF),
-            shape((2, FF, D), BF),
+            shape((8, TOK, D), BF),
         ),
         in_specs=[vmem] + [any_space] * 4 + [vmem] * 5 + [smem] + [vmem] * 2 + [any_space] * 3,
-        out_specs=(vmem,) * 7 + (any_space,) * 5,
+        out_specs=(vmem,) * 8 + (any_space,) * 5,
         scratch_shapes=[
-            pltpu.VMEM((D, D), BF),
-            pltpu.VMEM((D, 512), BF),
-            pltpu.VMEM((D, 512), BF),
-            pltpu.VMEM((D, D), BF),
-            pltpu.VMEM((TOK, D), BF),
-            pltpu.VMEM((4, TOK, D), BF),
-            pltpu.VMEM((8, 2 * TOK, 512), BF),
+            low(2, D, D),
+            low(D, 512),
+            low(D, 512),
+            low(TOK, D),
+            low(4, TOK, D),
+            low(8, 2 * TOK, 512),
             pltpu.VMEM((TOK, 512), F32),
-            dma((52,)),
-            dma((42,)),
-            dma((9,)),
+            pltpu.VMEM((16, 8, TOK), F32),
+            low(16, TOK, D),
+            low(16, TOK, D),
+            low(2, D, FF),
+            low(2, D, FF),
+            low(2, FF, D),
+            pltpu.VMEM((16, 8, TOK), F32),
+            pltpu.VMEM((16, 8, TOK), F32),
+            pltpu.VMEM((16, 8, TOK), F32),
+            low(16, 2 * SLOTS, TOK),
+            low(2, slots, D),
+            low(2, slots, D),
+            low(2, slots, FF),
+            low(2, slots, FF),
+            low(2, slots, FF),
+            low(2, 4 * SLOTS, D),
+            low(2, 4 * SLOTS, D),
+            low(16, TOK, D),
+            low(16, TOK, D),
+            low(4, TOK, D),
+            low(8, TOK, D),
+            low(TOK, D),
+            low(2, TOK, D),
+            low(2, D, FF),
+            low(2, D, FF),
+            dma((100,)),
+            dma((76,)),
+            dma((16,)),
+            dma((16,)),
+            dma((16,)),
+            dma((16,)),
+            dma((13,)),
         ],
         compiler_params=pltpu.CompilerParams(
-            collective_id=3, has_side_effects=True, vmem_limit_bytes=VMEM_BYTES
+            collective_id=1, has_side_effects=True, vmem_limit_bytes=VMEM_BYTES
         ),
-        name="front",
+        name="main",
     )(
         tokens, wq, wk, wv, wo, ga.reshape(1, D), gm.reshape(1, D), router, cotangent, routes,
         lengths, jnp.asarray(cosine), jnp.asarray(sine), wg, wu, wd,
@@ -1465,14 +1406,11 @@
     lengths,
 ):
     (
-        hidden, x, gate_tiles, gates, mixed, query, kv, probs, upstream_all, full_gate, full_up,
-        full_down,
-    ) = front(
+        hidden, x, gates, mixed, query, kv, grad_rows, grad_gates, probs, out_parts, part_gate,
+        part_up, part_down,
+    ) = main(
         tokens, w_query, w_key, w_value, w_output, gain_attn, gain_moe, router, cotangent, routes,
         lengths, w_gate, w_up, w_down,
-    )
-    grad_rows, out_parts, grad_gates, part_gate, part_up, part_down = moe(
-        x, gate_tiles, upstream_all, full_gate, full_up, full_down
     )
     cosine, sine = turn_tables()
     layer_out, grad_input, sum_q, sum_o, sum_kv, narrow, grad_gate, grad_up, grad_down = back(
@@ -1482,7 +1420,8 @@
             jnp.asarray(cosine), jnp.asarray(sine), routes, lengths,
         ),
         (
-            probs, w_output, w_query, w_key, w_value, out_parts, part_gate, part_up, part_down,
+            probs, w_output, w_query, w_key, w_value, out_parts, part_gate, part_up,
+            part_down.reshape(2, FF, D),
         ),
     )
     sum_q, sum_o, sum_kv, narrow = total(sum_q, sum_o, sum_kv, narrow)

time: 263 us -> 237 us (0.901)
  Pallas kernels: 241 us -> 214 us
    pallas_call x2 -> x1, Pallas kernels: 130 us -> 104 us  [main(): pl.pallas_call(main_kernel, out_shape=(shape((TOK, D), F32), shape((TOK,...]
where the time goes in v4:
time: 237 us
  Pallas kernels  214 us (90%)
  local copies, waits for them, and re-layouts  14.2 us (6%)
  other arithmetic  6.7 us (3%)
    pallas_call x1, Pallas kernels, main(): pl.pallas_call(main_kernel, out_shape=(shape((TOK, D), F32), shape((TOK,...  104 us
    pallas_call x1, Pallas kernels, back(): pl.pallas_call(back_kernel, out_shape=(shape((TOK, D), BF), shape((TOK, D...  55.9 us
    pallas_call x1, Pallas kernels, total(): pl.pallas_call(total_kernel, out_shape=(shape((D, D), BF),) * 3 + (shape(...  54.8 us
    unnamed x21, local copies, waits for them, and re-layouts  7 us

profile of v4, /device:TPU:1, one launch (start us, length us, event | category | flops | bytes accessed | tf_op | source)
XLA Modules:
  0.0 236.7 jit_solution(1564945904210690762)
XLA Ops:
  1.3 1.4 copy.36.routes_ref
  2.7 1.7 copy.35.router_ref
  4.4 103.7 %main.1 = (f32[128,1024]{1,0:T(8,128)}, bf16[128,1024]{1,0:T(8,128)(2,1)}, f32[128,128]{1,0:T(8,128)}, bf16[128,1024]{1,0:T(8,128)(2,1)}, bf16[128,1024]{1,0:T(8...) custom-call(bf16[128,1024]{1,0:T(8,128)(2,1)} %tok_ref.3, ...), custom_call_target="tpu_custom_call" | custom-call | tf_op jit(solution)/shard_map/main/pallas_call | solution.py:685
  108.1 55.9 %back.1 = (bf16[128,1024]{1,0:T(8,128)(2,1)}, f32[128,1024]{1,0:T(8,128)}, bf16[1024,1024]{1,0:T(8,128)(2,1)}, bf16[1024,1024]{1,0:T(8,128)(2,1)}, bf16[1024,102...) custom-call(f32[128,1024]{1,0:T(8,128)} %get-tuple-element.39.rows_r, ...), custom_call_target="tpu_custom_call" | custom-call | tf_op jit(solution)/shard_map/back/pallas_call | solution.py:1069
  164.0 54.8 %total.1 = (bf16[1024,1024]{1,0:T(8,128)(2,1)}, bf16[1024,1024]{1,0:T(8,128)(2,1)}, bf16[1024,1024]{1,0:T(8,128)(2,1)}, f32[128,1024]{1,0:T(8,128)}) custom-call(bf16[1024,1024]{1,0:T(8,128)(2,1)} %get-tuple-element.54.a_hbm, bf16[1024,1024]{1,0:T(8,128)(2,1)} %get-tuple-element.55.b_hbm, bf16[1024,1024]{1,0:T(8,128)(2,1)} %get-tuple-element.56.c_hbm, ...), custom_call_target="tpu_custom_call" | custom-call | tf_op jit(solution)/shard_map/total/pallas_call | solution.py:1351
  218.8 0.7 slice_reduce_fusion
  219.5 0.1 reshape_squeeze.3
  219.6 0.6 convert_element_type.19
  220.2 1.4 fusion.1
  221.7 1.1 slice.30
  222.8 0.7 reshape.49
  223.5 0.0 copy-start.1
  223.5 4.2 %convert_element_type.15 = f32[1024,1024]{1,0:T(8,128)} convert(bf16[1024,1024]{1,0:T(8,128)(2,1)} %get-tuple-element.58) | non-fusion elementwise | flops 1048576 | bytes 6291456 | tf_op jit(solution)/shard_map/convert_element_type | solution.py:1432
  227.7 0.0 copy-done.1
  227.7 0.0 copy-start
  227.7 2.5 %convert_element_type.17 = f32[1024,1024]{1,0:T(8,128)} convert(bf16[1024,1024]{1,0:T(8,128)(2,1)S(1)} %copy-done.1) | non-fusion elementwise | flops 1048576 | bytes 6291456 | tf_op jit(solution)/shard_map/convert_element_type | solution.py:1435
  230.2 0.0 copy-done
  230.2 0.0 copy-start.6
  230.2 0.0 copy-start.5
  230.2 0.0 copy-start.4
  230.2 2.6 %fusion = (f32[1024,512]{1,0:T(8,128)}, f32[1024,512]{1,0:T(8,128)}) fusion(bf16[1024,1024]{1,0:T(8,128)(2,1)S(1)} %copy-done), kind=kLoop, calls=%fused_computation.2 | loop fusion | bytes 8388608 | tf_op jit(solution)/shard_map/slice | solution.py:1434
  232.8 0.0 copy-start.3
  232.8 0.0 copy-start.2
  232.8 0.0 copy-done.6
  232.8 0.7 copy.45
  233.5 0.0 copy-done.5
  233.5 0.8 copy.46
  234.3 0.0 copy-done.4
  234.3 0.8 copy.47
  235.1 0.0 copy-done.3
  235.1 0.8 copy.48
  235.9 0.0 copy-done.2
  235.9 0.8 copy.49
  (1 shorter events, 0.0 us)
Async XLA Ops:
  223.5 4.2 %copy-start.1 = (bf16[1024,1024]{1,0:T(8,128)(2,1)S(1)}, bf16[1024,1024]{1,0:T(8,128)(2,1)}, u32[]{:S(2)}) copy-start(bf16[1024,1024]{1,0:T(8,128)(2,1)} %get-tuple-element.60) | copy-start | bytes 6291460
  227.7 2.5 %copy-start = (bf16[1024,1024]{1,0:T(8,128)(2,1)S(1)}, bf16[1024,1024]{1,0:T(8,128)(2,1)}, u32[]{:S(2)}) copy-start(bf16[1024,1024]{1,0:T(8,128)(2,1)} %get-tuple-element.59) | copy-start | bytes 6291460
  230.2 2.6 %copy-start.6 = (bf16[128,1024]{1,0:T(8,128)(2,1)S(1)}, bf16[128,1024]{1,0:T(8,128)(2,1)}, u32[]{:S(2)}) copy-start(bf16[128,1024]{1,0:T(8,128)(2,1)} %get-tuple-element.82) | copy-start | bytes 786436
  230.2 3.3 %copy-start.5 = (f32[128,1024]{1,0:T(8,128)S(1)}, f32[128,1024]{1,0:T(8,128)}, u32[]{:S(2)}) copy-start(f32[128,1024]{1,0:T(8,128)} %get-tuple-element.83) | copy-start | bytes 1572868
  230.2 4.1 %copy-start.4 = (f32[1024,128]{1,0:T(8,128)S(1)}, f32[1024,128]{1,0:T(8,128)}, u32[]{:S(2)}) copy-start(f32[1024,128]{1,0:T(8,128)} %get-tuple-element.62) | copy-start | bytes 1572868
  232.8 2.3 copy-start.3
  232.8 3.1 %copy-start.2 = (f32[128,1024]{1,0:T(8,128)S(1)}, f32[128,1024]{1,0:T(8,128)}, u32[]{:S(2)}) copy-start(f32[128,1024]{1,0:T(8,128)} %get-tuple-element.64) | copy-start | bytes 1572868

commit v5 on v4

--- a/solution.py
+++ b/solution.py
@@ -59,11 +59,14 @@
         self.send_sem, self.recv_sem, self.made = send_sem, recv_sem, []
 
     def start(self, source, target, recv, to):
+        self.put(source, target, self.recv_sem.at[recv], to)
+
+    def put(self, source, target, sem, to):
         copy = pltpu.make_async_remote_copy(
             src_ref=source,
             dst_ref=target,
             send_sem=self.send_sem.at[len(self.made)],
-            recv_sem=self.recv_sem.at[recv],
+            recv_sem=sem,
             device_id=to,
             device_id_type=MESH,
         )
@@ -134,13 +137,16 @@
     return jnp.where(lane == lax.div(row, 2) * 8 + lax.rem(row, 2), 1.0, 0.0).astype(BF)
 
 
-def routed_mask(routes):
-    lane = lanes(TOK)
-    expert = jnp.where(lax.rem(lane, 8) < 2, lax.div(lane, 8) * 2 + lax.rem(lane, 8), -1)
+def routed_mask(routes, expert):
     hit = jnp.zeros((TOK, TOK), F32)
     for k in range(TOP):
-        hit = hit + jnp.where(routes[:, k : k + 1] == expert, 1.0, 0.0)
-    return hit > 0
+        hit = hit + jnp.where(routes[k : k + 1, :] == expert, 1.0, 0.0)
+    return hit
+
+
+def wide_experts():
+    row = lax.broadcasted_iota(jnp.int32, (TOK, 1), 0)
+    return jnp.where(lax.rem(row, 8) < 2, lax.div(row, 8) * 2 + lax.rem(row, 8), -1)
 
 
 class PlaneGather:
@@ -344,9 +350,11 @@
     x_ref[...] = x
     tokens_in.begin(x_ref)
     tokens_in.slab(0, 0)[...] = x
-    wide = jnp.dot(router_ref[...], widen(), preferred_element_type=F32).astype(BF)
-    logits = jnp.dot(x, wide, preferred_element_type=F32)
-    routed = routed_mask(routes_ref[...])
+    wide = lax.dot_general(
+        widen(), router_ref[...], (((0,), (0,)), ((), ())), preferred_element_type=F32
+    ).astype(BF)
+    logits = lax.dot_general(x, wide, (((1,), (1,)), ((), ())), preferred_element_type=F32)
+    routed = routed_mask(routes_ref[...], wide_experts()).T > 0
     logits = jnp.where(routed, logits, -1e30)
     weights = jnp.where(routed, jnp.exp(logits - jnp.max(logits, axis=1, keepdims=True)), 0.0)
     weights = weights * (1.0 / jnp.sum(weights, axis=1, keepdims=True))
@@ -879,15 +887,194 @@
         self.arrived(self.highs[1], 5)
 
 
+class Total:
+    def __init__(self, net, axis, source, result, span, rows, first, piece, buffers, sems):
+        self.net, self.axis, self.source, self.result = net, axis, source, result
+        self.span, self.rows, self.first, self.piece_size = span, rows, first, piece
+        self.theirs, self.low, self.high, self.hop, self.pieces, self.done = buffers
+        self.recv, self.plane_send, self.plane_recv, self.back_send, self.back_recv = sems
+        dp, y = lax.axis_index("dp"), lax.axis_index("hid")
+        self.core = lax.rem(dp, 2)
+        self.here = (lax.div(dp, 8), y, lax.rem(lax.div(dp, 2), 4))
+        self.sibling = self.at(self.here, 1 - self.core)
+        self.plus, self.minus = self.along(1), self.along(-1)
+        self.plane = [i for i in range(3) if i != axis]
+        self.slab_rows = rows // 4
+        half = self.slab_rows // 2
+        self.lo, self.hi = pl.ds(0, half), pl.ds(half, half)
+
+    def at(self, spot, on=None):
+        spot = [wrap(v) for v in spot]
+        return (spot[0] * 8 + spot[2] * 2 + (self.core if on is None else on), spot[1])
+
+    def along(self, step):
+        return self.at([self.here[i] + (step if i == self.axis else 0) for i in range(3)])
+
+    def arrived(self, ref, i):
+        pltpu.make_async_copy(ref, ref, self.recv.at[i]).wait()
+
+    def put(self, source, target, i, to):
+        self.net.put(source, target, self.recv.at[i], to)
+
+    def block(self, ref, step, part=None):
+        size = self.slab_rows
+        start = self.core * self.span + self.first + wrap(self.here[self.axis] + step) * size
+        if part is not None:
+            size = size // 2
+            start += part * size
+        return ref.at[pl.ds(pl.multiple_of(start, size), size)]
+
+    def own(self, step):
+        return self.block(self.source, step)
+
+    def begin(self):
+        start = (1 - self.core) * self.span + self.first
+        theirs = self.source.at[pl.ds(pl.multiple_of(start, self.rows), self.rows)]
+        self.put(theirs, self.theirs, 0, self.sibling)
+
+    def merge(self, step):
+        size = self.slab_rows
+        start = wrap(self.here[self.axis] + step) * size
+        accumulate(self.own(step), self.theirs.at[pl.ds(pl.multiple_of(start, size), size)])
+
+    def second(self):
+        lo, hi = self.lo, self.hi
+        self.arrived(self.theirs, 0)
+        self.merge(2)
+        far = self.own(2)
+        self.put(far.at[lo], self.hop.at[lo], 1, self.plus)
+        self.put(far.at[hi], self.hop.at[hi], 2, self.minus)
+        self.merge(1)
+        self.put(self.own(1).at[hi], self.low.at[hi], 3, self.plus)
+        self.merge(-1)
+        self.put(self.own(-1).at[lo], self.high.at[lo], 4, self.minus)
+        self.merge(0)
+
+    def third(self):
+        lo, hi = self.lo, self.hi
+        self.arrived(self.hop.at[lo], 1)
+        near = self.own(1).at[lo]
+        accumulate(near, self.hop.at[lo])
+        self.put(near, self.low.at[lo], 5, self.plus)
+        self.arrived(self.hop.at[hi], 2)
+        near = self.own(-1).at[hi]
+        accumulate(near, self.hop.at[hi])
+        self.put(near, self.high.at[hi], 6, self.minus)
+
+    def piece(self, ref, u, v):
+        rows, cols = self.piece_size
+        if self.slab_rows == 4 * rows:
+            row, col = u * rows, v * cols
+        else:
+            row, col = lax.div(u, 2) * rows, (lax.rem(u, 2) * 4 + v) * cols
+        return ref.at[
+            pl.ds(pl.multiple_of(row, rows), rows), pl.ds(pl.multiple_of(col, cols), cols)
+        ]
+
+    def member(self, i):
+        u, v = self.plane
+        spot = list(self.here)
+        spot[u] = wrap(spot[u] + lax.div(i, 4))
+        spot[v] = wrap(spot[v] + lax.rem(i, 4))
+        return spot[u], spot[v], self.at(spot)
+
+    def mirror(self, i):
+        return wrap(-lax.div(i, 4)) * 4 + wrap(-lax.rem(i, 4))
+
+    def mine(self):
+        return self.here[self.plane[0]], self.here[self.plane[1]]
+
+    def remote(self, source, target, send, recv, to):
+        return pltpu.make_async_remote_copy(
+            src_ref=source, dst_ref=target, send_sem=send, recv_sem=recv,
+            device_id=to, device_id_type=MESH,
+        )
+
+    def piece_copy(self, i):
+        u, v, to = self.member(i)
+        there = self.mirror(i)
+        return self.remote(
+            self.piece(self.own(0), u, v),
+            self.pieces.at[there],
+            self.plane_send.at[i],
+            self.plane_recv.at[there],
+            to,
+        )
+
+    def back_copy(self, i):
+        spot = self.piece(self.done, *self.mine())
+        return self.remote(
+            spot, spot, self.back_send.at[i], self.back_recv.at[self.mirror(i)], self.member(i)[2]
+        )
+
+    def each(self, act):
+        lax.fori_loop(1, 16, lambda i, carry: (act(i), carry)[1], 0)
+
+    def take(self, sems):
+        spot = self.pieces
+        self.each(lambda i: pltpu.make_async_copy(spot.at[0], spot.at[0], sems.at[i]).wait())
+
+    def fourth(self):
+        lo, hi = self.lo, self.hi
+        self.arrived(self.low.at[hi], 3)
+        self.arrived(self.high.at[lo], 4)
+        self.arrived(self.low.at[lo], 5)
+        self.arrived(self.high.at[hi], 6)
+        accumulate(self.own(0), self.low, self.high)
+        self.each(lambda i: self.piece_copy(i).start())
+        self.pieces[0] = self.piece(self.own(0), *self.mine())[...]
+
+    def fifth(self):
+        self.take(self.plane_recv)
+        total = jnp.sum(self.pieces[...].astype(F32), axis=0)
+        self.piece(self.done, *self.mine())[...] = total.astype(self.done.dtype)
+        self.each(lambda i: self.back_copy(i).start())
+
+    def sixth(self, sem):
+        self.take(self.back_recv)
+        spot = self.block(self.result, 0)
+        self.put(self.done, spot, 7, self.plus)
+        self.put(self.done, spot, 8, self.minus)
+        self.put(self.done, spot, 11, self.sibling)
+        self.store = pltpu.make_async_copy(self.done, spot, sem)
+        self.store.start()
+
+    def seventh(self):
+        whole, spot = self.block(self.result, -1), self.block(self.result, -1, 0)
+        self.arrived(whole, 7)
+        self.put(spot, spot, 9, self.plus)
+        self.put(whole, whole, 12, self.sibling)
+        whole, spot = self.block(self.result, 1), self.block(self.result, 1, 1)
+        self.arrived(whole, 8)
+        self.put(spot, spot, 10, self.minus)
+        self.put(whole, whole, 13, self.sibling)
+
+    def eighth(self):
+        whole = self.block(self.result, 2)
+        self.arrived(self.block(self.result, 2, 0), 9)
+        self.arrived(self.block(self.result, 2, 1), 10)
+        self.put(whole, whole, 14, self.sibling)
+
+    def finish(self):
+        for i in range(11, 15):
+            self.arrived(self.block(self.result, 0), i)
+        self.each(lambda i: self.piece_copy(i).wait_send())
+        self.each(lambda i: self.back_copy(i).wait_send())
+        self.store.wait()
+
+
 def back_kernel(
     rows_ref, gg_ref, x_ref, gates_ref, hidden_ref, gm_ref, ga_ref, router_ref, cot_ref, tok_ref,
     mixed_ref, query_ref, kv_ref, cos_ref, sin_ref, routes_ref, len_ref,
     probs_hbm, wo_hbm, wq_hbm, wk_hbm, wv_hbm, o_hbm, pg_hbm, pu_hbm, pd_hbm,
-    layer_ref, input_ref, dq_out, do_out, dkv_out, narrow_ref, gate_out, up_out, down_out,
+    layer_ref, input_ref, gate_out, up_out, down_out, q_hbm, o_sum_hbm, kv_hbm, narrow_hbm,
     probs, wo, wq, wk, wv, o_buf, rb, rc, rd, re,
     pg, pu, pd, sg, su, sd, hop_g, hop_ua, hop_ub, hop_d, low_g, low_u, low_d, high_g, high_u, high_d,
     grad_mixed, grad_query, grad_kv, kv_hops, kv_low, kv_high,
-    send_sem, recv_sem, local_sem,
+    dq_out, do_out, dkv_out, narrow_ref,
+    their_a, their_b, their_c, their_n, low_a, low_b, low_c, low_n, high_a, high_b, high_c, high_n,
+    hop_a, hop_b, hop_c, hop_n, piece_a, piece_b, piece_c, piece_n, done_a, done_b, done_c, done_n,
+    send_sem, recv_sem, local_sem, t_recv, plane_send, plane_recv, back_send, back_recv,
 ):
     p, q, y, core = place()
     spot = (p, q, y, core)
@@ -902,7 +1089,39 @@
     for load in loads:
         load.start()
     plane = PlaneReduce(net, spot, o_buf, rb, rc, rd, re, 0)
-    greet([plane.right, plane.left, plane.up, plane.down, ahead, behind, sibling])
+
+    def unit(k, axis, source, result, span, rows, first, piece, *buffers):
+        sems = [ref.at[k] for ref in (t_recv, plane_send, plane_recv, back_send, back_recv)]
+        return Total(net, axis, source, result, span, rows, first, piece, buffers, sems)
+
+    sum_o = unit(
+        0, 2, do_out, o_sum_hbm, 512, 512, 0, (32, 256), their_a, low_a, high_a, hop_a, piece_a, done_a
+    )
+    sum_q = unit(
+        1, 0, dq_out, q_hbm, 512, 512, 0, (32, 256), their_b, low_b, high_b, hop_b, piece_b, done_b
+    )
+    sum_kv = [
+        unit(
+            2 + h, 2 * h, dkv_out, kv_hbm, 512, 256, 256 * h, (16, 256),
+            *[ref.at[h] for ref in (their_c, low_c, high_c, hop_c, piece_c, done_c)],
+        )
+        for h in range(2)
+    ]
+    sum_n = unit(
+        4, 1, narrow_ref, narrow_hbm, 64, 64, 0, (8, 128),
+        their_n, low_n, high_n, hop_n, piece_n, done_n,
+    )
+    late = [*sum_kv, sum_n]
+    everyone = [sum_o, sum_q, *late]
+    here = sum_o.here
+    partners = [
+        sum_o.at([here[0] + i, here[1] + j, here[2] + k])
+        for i in range(4)
+        for j in range(4)
+        for k in range(4)
+        if (i or j or k) and not (i and j and k)
+    ]
+    greet(partners + [sibling])
     loads[0].wait()
     plane.begin()
     for i, (source, target) in enumerate(((pg_hbm, sg), (pu_hbm, su), (pd_hbm, sd))):
@@ -915,12 +1134,12 @@
     grad_gates = gg_ref[...].reshape(TOK, TOK).T
     grad_logits = gates * (grad_gates - jnp.sum(gates * grad_gates, axis=1, keepdims=True))
     grad_logits = grad_logits.astype(BF)
-    wide = jnp.dot(router_ref[...], widen(), preferred_element_type=F32).astype(BF)
+    wide = lax.dot_general(
+        widen(), router_ref[...], (((0,), (0,)), ((), ())), preferred_element_type=F32
+    ).astype(BF)
     by_row = (((0,), (0,)), ((), ()))
     by_col = (((1,), (1,)), ((), ()))
-    grad_normed = rows_ref[...] + lax.dot_general(
-        grad_logits, wide, by_col, preferred_element_type=F32
-    )
+    grad_normed = rows_ref[...] + jnp.dot(grad_logits, wide, preferred_element_type=F32)
     hidden = hidden_ref[...]
     scale = root(hidden)
     grad_gain_moe = jnp.sum(grad_normed * hidden * scale, axis=0, keepdims=True)
@@ -932,10 +1151,15 @@
     loads[1].wait()
     grad_mixed[...] = lax.dot_general(low, wo[...], by_col, preferred_element_type=F32).astype(BF)
     narrow_ref[...] = lax.dot_general(grad_logits, x_ref[...], by_row, preferred_element_type=F32)
-    counts = jnp.sum(jnp.where(routed_mask(routes_ref[...]), 1.0, 0.0), axis=0, keepdims=True)
+    named = routed_mask(routes_ref[...], lax.broadcasted_iota(jnp.int32, (TOK, 1), 0))
+    counts = jnp.sum(named.T, axis=0, keepdims=True)
     narrow_ref[3:4, :] = grad_gain_moe
     narrow_ref[4:5, :] = jnp.zeros((1, D), F32)
     narrow_ref[4:5, 0:TOK] = counts
+    do_out[...] = lax.dot_general(
+        mixed_ref[...], low, by_row, preferred_element_type=F32
+    ).astype(BF)
+    sum_o.begin()
     plane.middle()
 
     def block(ref, step, rows=None):
@@ -969,6 +1193,7 @@
         net.arrived(ref, 18 + i)
     weight_merge(2)
     weights.begin()
+    sum_o.second()
 
     cosine, sine = cos_ref[pl.ds(first, TOK), :], sin_ref[pl.ds(first, TOK), :]
     loads[2].wait()
@@ -1010,26 +1235,26 @@
     sums.begin()
     sums.direct()
     plane.third()
-    do_out[...] = lax.dot_general(
-        mixed_ref[...], low, by_row, preferred_element_type=F32
-    ).astype(BF)
-    sums.middle()
-    plane.fourth()
+    sum_o.third()
     tokens = tok_ref[...].astype(F32)
     scale = root(tokens)
     normed = (tokens * scale * ga_ref[...]).astype(BF)
     dq_out[...] = lax.dot_general(
         normed, grad_query[...], by_row, preferred_element_type=F32
     ).astype(BF)
+    sum_q.begin()
+    sums.middle()
+    plane.fourth()
+    sum_q.second()
     for load in loads[3:6]:
         load.wait()
     grad_normed = lax.dot_general(grad_query[...], wq[...], by_col, preferred_element_type=F32)
     weight_merge(1)
     weight_merge(-1)
+    weight_merge(0)
+    sum_o.fourth()
+    sums.finish()
     weights.direct()
-    weights.middle()
-    weight_merge(0)
-    sums.finish()
     both = grad_kv[y].astype(F32) + kv_low[...].astype(F32) + kv_high[...].astype(F32)
     grad_key = jnp.concatenate(
         [turn(both[:, c * 128 : (c + 1) * 128], cosine, -sine) for c in range(4)], axis=1
@@ -1041,13 +1266,36 @@
     dkv_out[:, 512:1024] = lax.dot_general(
         normed, grad_value, by_row, preferred_element_type=F32
     ).astype(BF)
+    sum_kv[0].begin()
+    sum_kv[1].begin()
     grad_normed += lax.dot_general(grad_key, wk[...], by_col, preferred_element_type=F32)
     grad_normed += lax.dot_general(grad_value, wv[...], by_col, preferred_element_type=F32)
     narrow_ref[2:3, :] = jnp.sum(grad_normed * tokens * scale, axis=0, keepdims=True)
+    sum_n.begin()
+    sum_q.third()
+    for one in late:
+        one.second()
+    weights.middle()
+    sum_o.fifth()
     scaled = grad_normed * ga_ref[...]
     pull = jnp.mean(scaled * tokens, axis=1, keepdims=True)
     input_ref[...] += scale * scaled - tokens * (scale * scale * scale) * pull
+    for one in late:
+        one.third()
+    sum_q.fourth()
+    sum_o.sixth(local_sem.at[0])
     layer_ref[...] = (hidden_ref[...] + plane.finish()).astype(BF)
+    for one in late:
+        one.fourth()
+    sum_q.fifth()
+    sum_o.seventh()
+    for one in late:
+        one.fifth()
+    sum_q.sixth(local_sem.at[1])
+    sum_o.eighth()
+    for i, one in enumerate(late):
+        one.sixth(local_sem.at[2 + i])
+    sum_q.seventh()
     weights.finish()
     gate_out[...] = (
         block(pg, 0)[...].astype(F32) + low_g[...].astype(F32) + high_g[...].astype(F32)
@@ -1056,6 +1304,13 @@
     down_out[...] = (
         down_block(pd, 0)[...].astype(F32) + low_d[...].astype(F32) + high_d[...].astype(F32)
     )
+    for one in late:
+        one.seventh()
+    sum_q.eighth()
+    for one in late:
+        one.eighth()
+    for one in everyone:
+        one.finish()
     net.drain()
 
 
@@ -1071,16 +1326,16 @@
         out_shape=(
             shape((TOK, D), BF),
             shape((TOK, D), F32),
+            shape((D, TOK), F32),
+            shape((D, TOK), F32),
+            shape((TOK, D), F32),
             shape((D, D), BF),
             shape((D, D), BF),
             shape((D, D), BF),
             shape((TOK, D), F32),
-            shape((D, TOK), F32),
-            shape((D, TOK), F32),
-            shape((TOK, D), F32),
         ),
         in_specs=[vmem] * 16 + [smem] + [any_space] * 9,
-        out_specs=(vmem,) * 9,
+        out_specs=(vmem,) * 5 + (any_space,) * 4,
         scratch_shapes=[
             low(8, 2 * TOK, 512),
             low(D, D),
@@ -1114,9 +1369,42 @@
             low(2, 64, D),
             low(TOK, D),
             low(TOK, D),
-            dma((48,)),
+            low(D, D),
+            low(D, D),
+            low(D, D),
+            pltpu.VMEM((TOK, D), F32),
+            low(512, D),
+            low(512, D),
+            low(2, 256, D),
+            pltpu.VMEM((64, D), F32),
+            low(128, D),
+            low(128, D),
+            low(2, 64, D),
+            pltpu.VMEM((16, D), F32),
+            low(128, D),
+            low(128, D),
+            low(2, 64, D),
+            pltpu.VMEM((16, D), F32),
+            low(128, D),
+            low(128, D),
+            low(2, 64, D),
+            pltpu.VMEM((16, D), F32),
+            low(16, 32, 256),
+            low(16, 32, 256),
+            low(2, 16, 16, 256),
+            pltpu.VMEM((16, 8, 128), F32),
+            low(128, D),
+            low(128, D),
+            low(2, 64, D),
+            pltpu.VMEM((16, D), F32),
+            dma((120,)),
             dma((42,)),
             dma((9,)),
+            dma((5, 15)),
+            dma((5, 16)),
+            dma((5, 16)),
+            dma((5, 16)),
+            dma((5, 16)),
         ],
         compiler_params=pltpu.CompilerParams(
             collective_id=4, has_side_effects=True, vmem_limit_bytes=VMEM_BYTES
@@ -1125,268 +1413,71 @@
     )(*operands, *arrays)
 
 
-def total_kernel(
-    a_hbm, b_hbm, c_hbm, s_hbm, a_out, b_out, c_out, s_out,
-    mine, other, mine_s, other_s, from_low, from_high, from_low_s, from_high_s, bounced, bounced_s,
-    spread, spread_s, done, done_s,
-    sib_send, sib_recv, ring_send, ring_recv, plane_send, plane_recv, back_send, back_recv,
-    round_send, round_recv, last_send, last_recv, local_sem,
+def results_kernel(
+    q_ref, o_ref, kv_ref, n_ref, layer_ref, input_ref, gate_ref, up_ref, down_ref,
+    q_out, o_out, k_out, v_out, router_out, one_out, two_out, count_out,
+    layer_out, input_out, gate_out, up_out, down_out,
 ):
-    dp, y = lax.axis_index("dp"), lax.axis_index("hid")
-    core = lax.rem(dp, 2)
-    here = (lax.div(dp, 8), y, lax.rem(lax.div(dp, 2), 4))
-
-    def at(spot, on=None):
-        spot = [wrap(v) for v in spot]
-        return (spot[0] * 8 + spot[2] * 2 + (core if on is None else on), spot[1])
-
-    def along(k, step):
-        return at([here[i] + (step if i == k else 0) for i in range(3)])
-
-    sibling = at(here, 1 - core)
-    ring = [(along(k, 1), along(k, -1)) for k in range(3)]
-    planes = [(1, 2), (0, 2), (0, 1)]
-    greeted = [sibling]
-    for dx in range(4):
-        for dy in range(4):
-            for dz in range(4):
-                if (dx or dy or dz) and not (dx and dy and dz):
-                    greeted.append(at([here[0] + dx, here[1] + dy, here[2] + dz]))
-    ins, results = (a_hbm, b_hbm, c_hbm, s_hbm), (a_out, b_out, c_out, s_out)
-    axes = (0, 1, 2, 0)
-    halves = [mine.at[k] for k in range(3)] + [mine_s]
-    theirs = [other.at[k] for k in range(3)] + [other_s]
-    lows = [from_low.at[k] for k in range(3)] + [from_low_s]
-    highs = [from_high.at[k] for k in range(3)] + [from_high_s]
-    hops = [bounced.at[k] for k in range(3)] + [bounced_s]
-    pieces = [spread.at[k] for k in range(3)] + [spread_s]
-    slabs = [done.at[k] for k in range(3)] + [done_s]
-    parts = range(4)
-    sizes = (128, 128, 128, 16)
-
-    def half_of(k, which):
-        return ins[k].at[pl.ds(pl.multiple_of(which * sizes[k] * 4, sizes[k] * 4), sizes[k] * 4)]
-
-
-    def remote(source, target, send, recv, to):
-        return pltpu.make_async_remote_copy(
-            src_ref=source, dst_ref=target, send_sem=send, recv_sem=recv,
-            device_id=to, device_id_type=MESH,
-        )
-
-    def arrived(ref, sem):
-        pltpu.make_async_copy(ref, ref, sem).wait()
-
-    loads = [
-        pltpu.make_async_copy(half_of(k, core), halves[k], local_sem.at[k]) for k in parts
-    ]
-    for load in loads:
-        load.start()
-    greet(greeted)
-    sent = []
-
-    def go(*copy):
-        copy = remote(*copy)
-        copy.start()
-        sent.append(copy)
-
-    for k in parts:
-        go(half_of(k, 1 - core), theirs[k], sib_send.at[k], sib_recv.at[k], sibling)
-
-    def rows_of(k, step):
-        start = pl.multiple_of(wrap(here[axes[k]] + step) * sizes[k], sizes[k])
-        return halves[k].at[pl.ds(start, sizes[k])]
-
-    los = [pl.ds(0, size // 2) for size in sizes]
-    his = [pl.ds(size // 2, size // 2) for size in sizes]
-
-    def add(target, *terms):
-        total = target[...].astype(F32)
-        for term in terms:
-            total += term[...].astype(F32)
-        target[...] = total.astype(target.dtype)
-
-    def merge_rows(k, step):
-        start = pl.multiple_of(wrap(here[axes[k]] + step) * sizes[k], sizes[k])
-        span = pl.ds(start, sizes[k])
-        add(halves[k].at[span], theirs[k].at[span])
-
-    for k in parts:
-        lo, hi = los[k], his[k]
-        loads[k].wait()
-        arrived(theirs[k], sib_recv.at[k])
-        plus, minus = ring[axes[k]]
-        merge_rows(k, 2)
-        far = rows_of(k, 2)
-        go(far.at[lo], hops[k].at[lo], ring_send.at[k, 0], ring_recv.at[k, 0], plus)
-        go(far.at[hi], hops[k].at[hi], ring_send.at[k, 1], ring_recv.at[k, 1], minus)
-        merge_rows(k, 1)
-        go(rows_of(k, 1).at[hi], lows[k].at[hi], ring_send.at[k, 2], ring_recv.at[k, 2], plus)
-        merge_rows(k, -1)
-        go(rows_of(k, -1).at[lo], highs[k].at[lo], ring_send.at[k, 3], ring_recv.at[k, 3], minus)
-        merge_rows(k, 0)
-    for k in parts:
-        lo, hi = los[k], his[k]
-        plus, minus = ring[axes[k]]
-        arrived(hops[k].at[lo], ring_recv.at[k, 0])
-        near = rows_of(k, 1).at[lo]
-        add(near, hops[k].at[lo])
-        go(near, lows[k].at[lo], ring_send.at[k, 4], ring_recv.at[k, 4], plus)
-        arrived(hops[k].at[hi], ring_recv.at[k, 1])
-        near = rows_of(k, -1).at[hi]
-        add(near, hops[k].at[hi])
-        go(near, highs[k].at[hi], ring_send.at[k, 5], ring_recv.at[k, 5], minus)
-
-    def piece(k, ref, u, v):
-        if k == 3:
-            row, lane = lax.div(u, 2) * 8, (lax.rem(u, 2) * 4 + v) * 128
-            return ref.at[pl.ds(pl.multiple_of(row, 8), 8), pl.ds(pl.multiple_of(lane, 128), 128)]
-        return ref.at[
-            pl.ds(pl.multiple_of(u * 32, 32), 32), pl.ds(pl.multiple_of(v * 256, 256), 256)
-        ]
-
-    def member(k, i):
-        u, v = planes[axes[k]]
-        spot = list(here)
-        spot[u] = wrap(here[u] + lax.div(i, 4))
-        spot[v] = wrap(here[v] + lax.rem(i, 4))
-        return spot[u], spot[v], at(spot)
-
-    def mirror(i):
-        return wrap(-lax.div(i, 4)) * 4 + wrap(-lax.rem(i, 4))
-
-    def piece_copy(k, i):
-        u, v, to = member(k, i)
-        return remote(
-            piece(k, rows_of(k, 0), u, v),
-            pieces[k].at[mirror(i)],
-            plane_send.at[k, i],
-            plane_recv.at[k, mirror(i)],
-            to,
-        )
-
-    def back_copy(k, i):
-        u, v = planes[axes[k]]
-        spot = piece(k, slabs[k], here[u], here[v])
-        return remote(spot, spot, back_send.at[k, i], back_recv.at[k, mirror(i)], member(k, i)[2])
-
-    def each(make, act):
-        def one(i, carry):
-            act(make(i))
-            return carry
-
-        lax.fori_loop(1, 16, one, 0)
-
-    for k in parts:
-        lo, hi = los[k], his[k]
-        for i in (2, 4):
-            arrived(lows[k].at[hi if i == 2 else lo], ring_recv.at[k, i])
-        for i in (3, 5):
-            arrived(highs[k].at[lo if i == 3 else hi], ring_recv.at[k, i])
-        add(rows_of(k, 0), lows[k], highs[k])
-        each(lambda i: piece_copy(k, i), lambda copy: copy.start())
-    for k in parts:
-        u, v = planes[axes[k]]
-        pieces[k][0] = piece(k, rows_of(k, 0), here[u], here[v])[...]
-        each(
-            lambda i: pltpu.make_async_copy(pieces[k].at[0], pieces[k].at[0], plane_recv.at[k, i]),
-            lambda copy: copy.wait(),
-        )
-        total = jnp.sum(pieces[k][...].astype(F32), axis=0)
-        piece(k, slabs[k], here[u], here[v])[...] = total.astype(slabs[k].dtype)
-        each(lambda i: back_copy(k, i), lambda copy: copy.start())
-
-    def final(k, step, span=None):
-        size = sizes[k]
-        start = core * size * 4 + wrap(here[axes[k]] + step) * size
-        if span is not None:
-            size = size // 2
-            start += span * size
-        return results[k].at[pl.ds(pl.multiple_of(start, size), size)]
-
-    stores = []
-    for k in parts:
-        plus, minus = ring[axes[k]]
-        each(
-            lambda i: pltpu.make_async_copy(pieces[k].at[0], pieces[k].at[0], back_recv.at[k, i]),
-            lambda copy: copy.wait(),
-        )
-        go(slabs[k], final(k, 0), round_send.at[k, 0], round_recv.at[k, 0], plus)
-        go(slabs[k], final(k, 0), round_send.at[k, 1], round_recv.at[k, 1], minus)
-        go(slabs[k], final(k, 0), last_send.at[k, 0], last_recv.at[k, 0], sibling)
-        store = pltpu.make_async_copy(slabs[k], final(k, 0), local_sem.at[k])
-        store.start()
-        stores.append(store)
-    for k in parts:
-        plus, minus = ring[axes[k]]
-        arrived(final(k, -1), round_recv.at[k, 0])
-        spot = final(k, -1, 0)
-        go(spot, spot, round_send.at[k, 2], round_recv.at[k, 2], plus)
-        go(final(k, -1), final(k, -1), last_send.at[k, 1], last_recv.at[k, 1], sibling)
-        arrived(final(k, 1), round_recv.at[k, 1])
-        spot = final(k, 1, 1)
-        go(spot, spot, round_send.at[k, 3], round_recv.at[k, 3], minus)
-        go(final(k, 1), final(k, 1), last_send.at[k, 2], last_recv.at[k, 2], sibling)
-    for k in parts:
-        arrived(final(k, 2, 0), round_recv.at[k, 2])
-        arrived(final(k, 2, 1), round_recv.at[k, 3])
-        go(final(k, 2), final(k, 2), last_send.at[k, 3], last_recv.at[k, 3], sibling)
-    for k in parts:
-        for i in range(4):
-            arrived(final(k, 0), last_recv.at[k, i])
-    for copy in sent:
-        copy.wait_send()
-    for k in parts:
-        each(lambda i: piece_copy(k, i), lambda copy: copy.wait_send())
-        each(lambda i: back_copy(k, i), lambda copy: copy.wait_send())
-    for store in stores:
-        store.wait()
-
-
-def total(a, b, c, s):
-    any_space = pl.BlockSpec(memory_space=pl.ANY)
+    layer_out[...] = layer_ref[...]
+    input_out[...] = input_ref[...]
+    gate_out[0] = gate_ref[...]
+    up_out[0] = up_ref[...]
+    down_out[0] = down_ref[...]
+    q_out[...] = q_ref[...].astype(F32)
+    o_out[...] = o_ref[...].astype(F32)
+    k_out[...] = kv_ref[:, 0:512].astype(F32)
+    v_out[...] = kv_ref[:, 512:1024].astype(F32)
+
+    @pl.when(pl.program_id(0) == 0)
+    def _():
+        for j in range(16):
+            router_out[2 * j : 2 * j + 2, :] = n_ref[8 * j : 8 * j + 2, :]
+        one_out[...] = n_ref[2:3, :]
+        two_out[...] = n_ref[3:4, :]
+        count_out[...] = n_ref[4:5, 0:EXPERTS].astype(jnp.int32)
+
+
+def results(q, o, kv, narrow, *own):
+    rows = 256
+    some = rows * TOK // D
+    first = lambda *size: pl.BlockSpec((1, *size), lambda i: (0, i, 0))
+    block = lambda width: pl.BlockSpec((rows, width), lambda i: (i, 0))
+    whole = lambda *size: pl.BlockSpec(size, lambda i: (0, 0))
     shape = jax.ShapeDtypeStruct
-    dma = pltpu.SemaphoreType.DMA
-    vmem = pltpu.VMEM
     return pl.pallas_call(
-        total_kernel,
-        out_shape=(shape((D, D), BF),) * 3 + (shape((TOK, D), F32),),
-        in_specs=[any_space] * 4,
-        out_specs=(any_space,) * 4,
-        scratch_shapes=[
-            vmem((3, 512, D), BF),
-            vmem((3, 512, D), BF),
-            vmem((64, D), F32),
-            vmem((64, D), F32),
-            vmem((3, 128, D), BF),
-            vmem((3, 128, D), BF),
-            vmem((16, D), F32),
-            vmem((16, D), F32),
-            vmem((3, 128, D), BF),
-            vmem((16, D), F32),
-            vmem((3, 16, 32, 256), BF),
-            vmem((16, 8, TOK), F32),
-            vmem((3, 128, D), BF),
-            vmem((16, D), F32),
-            dma((4,)),
-            dma((4,)),
-            dma((4, 6)),
-            dma((4, 6)),
-            dma((4, 16)),
-            dma((4, 16)),
-            dma((4, 16)),
-            dma((4, 16)),
-            dma((4, 4)),
-            dma((4, 4)),
-            dma((4, 4)),
-            dma((4, 4)),
-            dma((4,)),
+        results_kernel,
+        grid=(D // rows,),
+        out_shape=(
+            shape((D, D), F32),
+            shape((D, D), F32),
+            shape((D, 512), F32),
+            shape((D, 512), F32),
+            shape((EXPERTS, D), F32),
+            shape((1, D), F32),
+            shape((1, D), F32),
+            shape((1, EXPERTS), jnp.int32),
+            shape((TOK, D), BF),
+            shape((TOK, D), F32),
+            shape((1, D, TOK), F32),
+            shape((1, D, TOK), F32),
+            shape((1, TOK, D), F32),
+        ),
+        in_specs=[
+            block(D), block(D), block(D), whole(TOK, D),
+            pl.BlockSpec((some, D), lambda i: (i, 0)),
+            pl.BlockSpec((some, D), lambda i: (i, 0)),
+            block(TOK), block(TOK),
+            pl.BlockSpec((some, D), lambda i: (i, 0)),
         ],
-        compiler_params=pltpu.CompilerParams(
-            collective_id=2, has_side_effects=True, vmem_limit_bytes=VMEM_BYTES
+        out_specs=(
+            block(D), block(D), block(512), block(512),
+            whole(EXPERTS, D), whole(1, D), whole(1, D), whole(1, EXPERTS),
+            pl.BlockSpec((some, D), lambda i: (i, 0)),
+            pl.BlockSpec((some, D), lambda i: (i, 0)),
+            first(rows, TOK), first(rows, TOK), first(some, D),
         ),
-        name="total",
-    )(a, b, c, s)
+        name="results",
+    )(q, o, kv, narrow, *own)
 
 
 def shards(
@@ -1409,37 +1500,41 @@
         hidden, x, gates, mixed, query, kv, grad_rows, grad_gates, probs, out_parts, part_gate,
         part_up, part_down,
     ) = main(
-        tokens, w_query, w_key, w_value, w_output, gain_attn, gain_moe, router, cotangent, routes,
-        lengths, w_gate, w_up, w_down,
+        tokens, w_query, w_key, w_value, w_output, gain_attn, gain_moe, router.T, cotangent,
+        routes.T, lengths, w_gate, w_up, w_down,
     )
     cosine, sine = turn_tables()
-    layer_out, grad_input, sum_q, sum_o, sum_kv, narrow, grad_gate, grad_up, grad_down = back(
+    layer_out, grad_input, grad_gate, grad_up, grad_down, sum_q, sum_o, sum_kv, narrow = back(
         (
             grad_rows, grad_gates, x, gates, hidden, gain_moe.reshape(1, D),
-            gain_attn.reshape(1, D), router, cotangent, tokens, mixed, query, kv,
-            jnp.asarray(cosine), jnp.asarray(sine), routes, lengths,
+            gain_attn.reshape(1, D), router.T, cotangent, tokens, mixed, query, kv,
+            jnp.asarray(cosine), jnp.asarray(sine), routes.T, lengths,
         ),
         (
             probs, w_output, w_query, w_key, w_value, out_parts, part_gate, part_up,
             part_down.reshape(2, FF, D),
         ),
     )
-    sum_q, sum_o, sum_kv, narrow = total(sum_q, sum_o, sum_kv, narrow)
-    sum_kv = sum_kv.astype(F32)
+    (
+        grad_q, grad_o, grad_k, grad_v, grad_router, gain_one, gain_two, counts,
+        layer_out, grad_input, grad_gate, grad_up, grad_down,
+    ) = results(
+        sum_q, sum_o, sum_kv, narrow, layer_out, grad_input, grad_gate, grad_up, grad_down
+    )
     return (
         layer_out,
         grad_input,
-        sum_q.astype(F32),
-        sum_kv[:, :512],
-        sum_kv[:, 512:],
-        sum_o.astype(F32),
-        narrow[2],
-        narrow[3],
-        narrow.reshape(16, 8, D)[:, :2].reshape(EXPERTS, D).T,
-        grad_gate[None],
-        grad_up[None],
-        grad_down[None],
-        narrow[4, :TOK].reshape(16, 8)[:, :2].reshape(EXPERTS).astype(jnp.int32),
+        grad_q,
+        grad_k,
+        grad_v,
+        grad_o,
+        gain_one.reshape(D),
+        gain_two.reshape(D),
+        grad_router.T,
+        grad_gate,
+        grad_up,
+        grad_down,
+        counts.reshape(EXPERTS),
     )
 
 

time: 237 us -> 222 us (0.937)
  local copies, waits for them, and re-layouts: 14.2 us -> 0 us
  other arithmetic: 6.7 us -> 0 us
  Pallas kernels: 214 us -> 220 us
    pallas_call x1, Pallas kernels: 55.9 us -> 106 us  [back(): pl.pallas_call(back_kernel, out_shape=(shape((TOK, D), BF), shape((TOK, D...]
    pallas_call x1, Pallas kernels: 54.8 us -> 10 us  [results(): pl.pallas_call(results_kernel, grid=(D // rows,), out_shape=(shape((D, D)...]
    unnamed x21 -> x0, local copies, waits for them, and re-layouts: 7 us -> none
    convert_element_type x3 -> x0, other arithmetic: 6.7 us -> none  [the longest x1 4.22 us: shards(): sum_q.astype(F32)]
    slice x4 -> x0, local copies, waits for them, and re-layouts: 5.78 us -> none  [the longest x1 2.57 us: shards(): sum_kv[:, 512:]]
where the time goes in v5:
time: 222 us
  Pallas kernels  220 us (99%)
    pallas_call x1, Pallas kernels, back(): pl.pallas_call(back_kernel, out_shape=(shape((TOK, D), BF), shape((TOK, D...  106 us
    pallas_call x1, Pallas kernels, main(): pl.pallas_call(main_kernel, out_shape=(shape((TOK, D), F32), shape((TOK,...  104 us
    pallas_call x1, Pallas kernels, results(): pl.pallas_call(results_kernel, grid=(D // rows,), out_shape=(shape((D, D)...  10 us

profile of v5, /device:TPU:1, one launch (start us, length us, event | category | flops | bytes accessed | tf_op | source)
XLA Modules:
  0.0 221.5 jit_solution(17018099775593183887)
XLA Ops:
  1.3 103.9 %main.1 = (f32[128,1024]{1,0:T(8,128)}, bf16[128,1024]{1,0:T(8,128)(2,1)}, f32[128,128]{1,0:T(8,128)}, bf16[128,1024]{1,0:T(8,128)(2,1)}, bf16[128,1024]{1,0:T(8...) custom-call(bf16[128,1024]{1,0:T(8,128)(2,1)} %tok_ref.3, ...), custom_call_target="tpu_custom_call" | custom-call | tf_op jit(solution)/shard_map/main/pallas_call | solution.py:693
  105.2 106.2 %back.1 = (bf16[128,1024]{1,0:T(8,128)(2,1)}, f32[128,1024]{1,0:T(8,128)}, f32[1024,128]{1,0:T(8,128)}, f32[1024,128]{1,0:T(8,128)}, f32[128,1024]{1,0:T(8,128)}...) custom-call(f32[128,1024]{1,0:T(8,128)} %get-tuple-element.48.rows_r, ...), custom_call_target="tpu_custom_call" | custom-call | tf_op jit(solution)/shard_map/back/pallas_call | solution.py:1324
  211.4 10.0 %results.1 = (f32[1024,1024]{1,0:T(8,128)}, f32[1024,1024]{1,0:T(8,128)}, f32[1024,512]{1,0:T(8,128)}, f32[1024,512]{1,0:T(8,128)}, f32[32,1024]{1,0:T(8,128)}, ...) custom-call(bf16[1024,1024]{1,0:T(8,128)(2,1)} %get-tuple-element.61, ...), custom_call_target="tpu_custom_call" | custom-call | tf_op jit(solution)/shard_map/results/pallas_call | solution.py:1447

commit v6 on v5

--- a/solution.py
+++ b/solution.py
@@ -210,13 +210,14 @@
 
 def main_kernel(
     tok_ref, wq_hbm, wk_hbm, wv_hbm, wo_hbm, ga_ref, gm_ref, router_ref, cot_ref, routes_ref,
-    len_ref, cos_ref, sin_ref, wgs_hbm, wus_hbm, wds_hbm,
-    hidden_ref, x_ref, gates_ref, mixed_ref, query_ref, kv_ref, grad_out, gg_out,
-    probs_hbm, o_hbm, dwg_hbm, dwu_hbm, dwd_hbm,
+    len_ref, cos_hbm, sin_hbm, wgs_hbm, wus_hbm, wds_hbm,
+    gates_ref, grad_out, gg_out, hidden_hbm, x_hbm, mixed_hbm, query_hbm, kv_hbm,
+    probs_hbm, o_hbm, dwg_hbm, dwu_hbm, dwd_hbm, hop_g_hbm, hop_u_hbm, hop_d_hbm,
+    hidden_ref, x_ref, mixed_ref, query_ref, turns,
     wqo, wk, wv, u_own, kv, probs, bias, gt,
     xs, us, wg, wu, wd, gin, rank, ggo, picks, rows, slot_grads, acts, gparts, uparts,
     outs, pairs, o_buf, p_buf, rb, rc, rd, re, dwg, dwu,
-    send_sem, recv_sem, g_send, g_recv, gg_send, gg_recv, local_sem,
+    send_sem, recv_sem, g_send, g_recv, gg_send, gg_recv, local_sem, free_sem,
 ):
     p, q, y, core = place()
     spot = (p, q, y, core)
@@ -236,9 +237,15 @@
     }
     for load in loads.values():
         load.start()
+    first = pl.multiple_of(y * TOK, TOK)
+    tables = [
+        pltpu.make_async_copy(src.at[pl.ds(first, TOK)], turns.at[i], local_sem.at[16 + i])
+        for i, src in enumerate((cos_hbm, sin_hbm))
+    ]
+    for load in tables:
+        load.start()
     gather = PlaneGather(net, spot, us, 0)
     tokens_in = PlaneGather(net, spot, xs, 42)
-    first = pl.multiple_of(y * TOK, TOK)
     row = lax.broadcasted_iota(jnp.int32, (TOK, 1), 0) + y * TOK
     length = len_ref[0]
     u_own[...] = jnp.where(row < length, cot_ref[...].astype(F32), 0.0).astype(BF)
@@ -285,7 +292,9 @@
     send_weight(0)
     tokens = tok_ref[...].astype(F32)
     normed = (tokens * root(tokens) * ga_ref[...]).astype(BF)
-    cosine, sine = cos_ref[pl.ds(first, TOK), :], sin_ref[pl.ds(first, TOK), :]
+    for load in tables:
+        load.wait()
+    cosine, sine = turns[0], turns[1]
     loads["k"].wait()
     keys = jnp.dot(normed, wk[...], preferred_element_type=F32)
     for c in range(4):
@@ -379,7 +388,20 @@
     lax.fori_loop(1, 16, start_gate, 0)
     gin[p * 4 + q] = gt[my_chip]
 
-    kv_ref[...] = kv[...]
+    keeps = [
+        pltpu.make_async_copy(src, dst, local_sem.at[18 + i])
+        for i, (src, dst) in enumerate(
+            (
+                (hidden_ref, hidden_hbm),
+                (x_ref, x_hbm),
+                (mixed_ref, mixed_hbm),
+                (query_ref, query_hbm),
+                (kv, kv_hbm),
+            )
+        )
+    ]
+    for store in keeps:
+        store.start()
     tokens_in.second()
     pass_weight(1)
     tokens_in.third()
@@ -547,12 +569,6 @@
             for j in range(4):
                 bounce[j]().start()
 
-        @pl.when(g == 3)
-        def _():
-            for j in (3, 1, 2, 0):
-                add_bounce(j)
-                (to_up if j < 2 else to_down)[j]().start()
-
         return carry
 
     keep_own.wait()
@@ -572,7 +588,10 @@
     for copy in keep:
         copy.wait()
     lax.fori_loop(0, 4, step, 0)
-    lax.fori_loop(0, 2, output, 0)
+    net.drain()
+    pl.semaphore_signal(free_sem.at[0], inc=1, device_id=sibling, device_id_type=MESH)
+    for other in (ahead, behind):
+        pl.semaphore_signal(free_sem.at[1], inc=1, device_id=other, device_id_type=MESH)
 
     def weight_tile(e, t):
         cols = pl.ds(pl.multiple_of(t * 256, 256), 256)
@@ -580,7 +599,7 @@
         lhs = rows[e, :, cols]
         dwg[e, cols, :] = lax.dot_general(lhs, gparts[e], dims, preferred_element_type=F32).astype(BF)
         dwu[e, cols, :] = lax.dot_general(lhs, uparts[e], dims, preferred_element_type=F32).astype(BF)
-        us[4 * e : 4 * e + 4, :, cols] = (
+        us[pl.ds(4 * e, 4), :, cols] = (
             lax.dot_general(acts[e], slot_grads[e, :, cols], dims, preferred_element_type=F32)
             .astype(BF)
             .reshape(4, TOK, 256)
@@ -589,8 +608,77 @@
     def weight_grads(e):
         lax.fori_loop(0, 4, lambda t, c: (weight_tile(e, t), c)[1], 0)
 
-    net.drain()
-    weight_grads(0)
+    weight_grads(1 - core)
+    pl.semaphore_wait(free_sem.at[0], 1)
+    theirs = us.at[pl.ds(4 * (1 - core), 4)]
+    net.start(dwg.at[1 - core], wg.at[0], 76, sibling)
+    net.start(dwu.at[1 - core], wu.at[0], 77, sibling)
+    net.start(theirs, xs.at[pl.ds(8, 4)], 78, sibling)
+    weight_grads(core)
+    for j in (3, 1, 2, 0):
+        add_bounce(j)
+        (to_up if j < 2 else to_down)[j]().start()
+    lax.fori_loop(0, 2, output, 0)
+
+    def grad_block(ref, step, rows=None):
+        span = pl.ds(pl.multiple_of(wrap(y + step) * TOK, TOK), TOK)
+        return ref.at[:, span] if rows is None else ref.at[rows, span]
+
+    def weight_portion(step, which):
+        if which == 0:
+            return [grad_block(dwg.at[core], step), grad_block(dwu.at[core], step, top)]
+        return [grad_block(dwu.at[core], step, bottom), us.at[4 * core + wrap(y + step)]]
+
+    def weight_merge(step):
+        accumulate(grad_block(dwg.at[core], step), grad_block(wg.at[0], step))
+        accumulate(grad_block(dwu.at[core], step), grad_block(wu.at[0], step))
+        accumulate(us.at[4 * core + wrap(y + step)], xs.at[8 + wrap(y + step)])
+
+    hops = (wu.at[1, :, 0:128], wu.at[1, :, 128:256], xs.at[12])
+    ring = RingReduce(
+        net, 79, ahead, behind, weight_portion,
+        ([hops[0], wu.at[1, top, 128:256]], [wu.at[1, bottom, 128:256], hops[2]]), None, None,
+    )
+    for i, ref in enumerate((wg.at[0], wu.at[0], xs.at[pl.ds(8, 4)])):
+        net.arrived(ref, 76 + i)
+    weight_merge(2)
+    pl.semaphore_wait(free_sem.at[1], 2)
+    ring.begin()
+    for around in (1, -1, 0):
+        weight_merge(around)
+    stores = [
+        pltpu.make_async_copy(src, dst, local_sem.at[10 + i])
+        for i, (src, dst) in enumerate(
+            (
+                (dwg.at[core], dwg_hbm),
+                (dwu.at[core], dwu_hbm),
+                (us.at[pl.ds(4 * core, 4)], dwd_hbm),
+            )
+        )
+    ]
+    for store in stores:
+        store.start()
+    lax.fori_loop(2, 4, output, 0)
+
+    def gg_copy(i):
+        a, b = lax.div(i, 4), lax.rem(i, 4)
+        return pltpu.make_async_remote_copy(
+            src_ref=ggo.at[wrap(p + a) * 4 + wrap(q + b)],
+            dst_ref=gg_out.at[my_chip],
+            send_sem=gg_send.at[i],
+            recv_sem=gg_recv.at[wrap(-a) * 4 + wrap(-b)],
+            device_id=device(p + a, q + b, y, core),
+            device_id_type=MESH,
+        )
+
+    def start_gg(i, _):
+        gg_copy(i).start()
+        return 0
+
+    lax.fori_loop(1, 16, start_gg, 0)
+    gg_out[my_chip] = ggo[p * 4 + q]
+    o_store = pltpu.make_async_copy(o_buf, o_hbm, local_sem.at[9])
+    o_store.start()
 
     def gather_sum(j):
         net.arrived(rc.at[j], R + 4 + j)
@@ -618,41 +706,18 @@
     tail[2].start()
     gather_sum(1)
     tail[3].start()
-    lax.fori_loop(2, 4, output, 0)
-
-    def gg_copy(i):
-        a, b = lax.div(i, 4), lax.rem(i, 4)
-        return pltpu.make_async_remote_copy(
-            src_ref=ggo.at[wrap(p + a) * 4 + wrap(q + b)],
-            dst_ref=gg_out.at[my_chip],
-            send_sem=gg_send.at[i],
-            recv_sem=gg_recv.at[wrap(-a) * 4 + wrap(-b)],
-            device_id=device(p + a, q + b, y, core),
-            device_id_type=MESH,
-        )
-
-    def start_gg(i, _):
-        gg_copy(i).start()
-        return 0
-
-    lax.fori_loop(1, 16, start_gg, 0)
-    gg_out[my_chip] = ggo[p * 4 + q]
-    o_store = pltpu.make_async_copy(o_buf, o_hbm, local_sem.at[9])
-    o_store.start()
+    gather_sum(0)
     net.arrived(rd.at[lo], R + 12)
     next_slab[lo] = (next_slab[lo].astype(F32) + rd[lo].astype(F32)).astype(BF)
     tail[4].start()
     net.arrived(rd.at[hi], R + 13)
     prev_slab[hi] = (prev_slab[hi].astype(F32) + rd[hi].astype(F32)).astype(BF)
     tail[5].start()
-    gather_sum(0)
-    weight_grads(1)
-    stores = [
-        pltpu.make_async_copy(src, dst, local_sem.at[10 + i])
-        for i, (src, dst) in enumerate(((dwg, dwg_hbm), (dwu, dwu_hbm), (us.at[0:8], dwd_hbm)))
-    ]
-    for store in stores:
-        store.start()
+    ring.arrived(ring.hops[0], 0)
+    ring.arrived(ring.hops[1], 1)
+    for i, (src, dst) in enumerate(zip(hops, (hop_g_hbm, hop_u_hbm, hop_d_hbm))):
+        stores.append(pltpu.make_async_copy(src, dst, local_sem.at[13 + i]))
+        stores[-1].start()
     net.arrived(re.at[0, hi], R + 14)
     net.arrived(re.at[1, lo], R + 15)
     net.arrived(re.at[0, lo], R + 16)
@@ -675,10 +740,13 @@
         return 0
 
     lax.fori_loop(1, 16, drain_small, 0)
+    net.drain()
     o_store.wait()
     for store in stores:
         store.wait()
     keep_probs.wait()
+    for store in keeps:
+        store.wait()
 
 
 def main(tokens, wq, wk, wv, wo, ga, gm, router, cotangent, routes, lengths, wg, wu, wd):
@@ -693,23 +761,31 @@
     return pl.pallas_call(
         main_kernel,
         out_shape=(
+            shape((TOK, TOK), F32),
+            shape((TOK, D), F32),
+            shape((16, 8, TOK), F32),
             shape((TOK, D), F32),
             shape((TOK, D), BF),
-            shape((TOK, TOK), F32),
             shape((TOK, D), BF),
             shape((TOK, D), BF),
             shape((4, TOK, D), BF),
-            shape((TOK, D), F32),
-            shape((16, 8, TOK), F32),
             shape((8, 2 * TOK, 512), BF),
             shape((16, TOK, D), BF),
-            shape((2, D, FF), BF),
-            shape((2, D, FF), BF),
-            shape((8, TOK, D), BF),
+            shape((D, FF), BF),
+            shape((D, FF), BF),
+            shape((4, TOK, D), BF),
+            shape((D, TOK), BF),
+            shape((D, TOK), BF),
+            shape((TOK, D), BF),
         ),
-        in_specs=[vmem] + [any_space] * 4 + [vmem] * 5 + [smem] + [vmem] * 2 + [any_space] * 3,
-        out_specs=(vmem,) * 8 + (any_space,) * 5,
+        in_specs=[vmem] + [any_space] * 4 + [vmem] * 5 + [smem] + [any_space] * 5,
+        out_specs=(vmem,) * 3 + (any_space,) * 13,
         scratch_shapes=[
+            pltpu.VMEM((TOK, D), F32),
+            low(TOK, D),
+            low(TOK, D),
+            low(TOK, D),
+            pltpu.VMEM((2, TOK, TOK), F32),
             low(2, D, D),
             low(D, 512),
             low(D, 512),
@@ -743,12 +819,13 @@
             low(2, D, FF),
             low(2, D, FF),
             dma((100,)),
-            dma((76,)),
+            dma((83,)),
             dma((16,)),
             dma((16,)),
             dma((16,)),
             dma((16,)),
-            dma((13,)),
+            dma((23,)),
+            pltpu.SemaphoreType.REGULAR((2,)),
         ],
         compiler_params=pltpu.CompilerParams(
             collective_id=1, has_side_effects=True, vmem_limit_bytes=VMEM_BYTES
@@ -869,12 +946,13 @@
         self.send(self.portion(1, 1), self.lows[1], 2, self.ahead)
         self.send(self.portion(-1, 0), self.highs[0], 3, self.behind)
 
-    def middle(self):
+    def middle(self, here=False):
         for which, step, targets, to in (
             (0, 1, self.lows[0], self.ahead),
             (1, -1, self.highs[1], self.behind),
         ):
-            self.arrived(self.hops[which], which)
+            if not here:
+                self.arrived(self.hops[which], which)
             refs = self.portion(step, which)
             for ref, hop in zip(refs, self.hops[which]):
                 accumulate(ref, hop)
@@ -1064,12 +1142,15 @@
 
 
 def back_kernel(
-    rows_ref, gg_ref, x_ref, gates_ref, hidden_ref, gm_ref, ga_ref, router_ref, cot_ref, tok_ref,
-    mixed_ref, query_ref, kv_ref, cos_ref, sin_ref, routes_ref, len_ref,
+    rows_hbm, gg_ref, x_hbm, gates_ref, hidden_hbm, gm_ref, ga_ref, router_ref, cot_hbm, tok_hbm,
+    mixed_hbm, query_hbm, kv_hbm, cos_hbm, sin_hbm, routes_ref, len_ref,
     probs_hbm, wo_hbm, wq_hbm, wk_hbm, wv_hbm, o_hbm, pg_hbm, pu_hbm, pd_hbm,
-    layer_ref, input_ref, gate_out, up_out, down_out, q_hbm, o_sum_hbm, kv_hbm, narrow_hbm,
+    hop_g_hbm, hop_u_hbm, hop_d_hbm,
+    layer_hbm, input_hbm, gate_hbm, up_hbm, down_hbm, q_hbm, o_sum_hbm, kv_sum_hbm, narrow_hbm,
+    layer_ref, input_ref, gate_out, up_out, down_out,
+    rows_ref, x_ref, hidden_ref, cot_ref, tok_ref, mixed_ref, query_ref, kv_ref, turns,
     probs, wo, wq, wk, wv, o_buf, rb, rc, rd, re,
-    pg, pu, pd, sg, su, sd, hop_g, hop_ua, hop_ub, hop_d, low_g, low_u, low_d, high_g, high_u, high_d,
+    pg, pu, pd, hop_g, hop_u, hop_d, low_g, low_u, low_d, high_g, high_u, high_d,
     grad_mixed, grad_query, grad_kv, kv_hops, kv_low, kv_high,
     dq_out, do_out, dkv_out, narrow_ref,
     their_a, their_b, their_c, their_n, low_a, low_b, low_c, low_n, high_a, high_b, high_c, high_n,
@@ -1081,9 +1162,14 @@
     sibling = (chip_of(p, q, core) * 2 + 1 - core, y)
     ahead, behind = device(p, q, y + 1, core), device(p, q, y - 1, core)
     net = Sends(send_sem, recv_sem)
+    first = pl.multiple_of(y * TOK, TOK)
     pairs = (
         (o_hbm, o_buf), (wo_hbm, wo), (probs_hbm, probs), (wq_hbm, wq), (wk_hbm, wk), (wv_hbm, wv),
-        (pg_hbm.at[core], pg), (pu_hbm.at[core], pu), (pd_hbm.at[core], pd),
+        (pg_hbm, pg), (pu_hbm, pu), (pd_hbm, pd),
+        (hop_g_hbm, hop_g), (hop_u_hbm, hop_u), (hop_d_hbm, hop_d),
+        (rows_hbm, rows_ref), (x_hbm, x_ref), (hidden_hbm, hidden_ref), (cot_hbm, cot_ref),
+        (tok_hbm, tok_ref), (mixed_hbm, mixed_ref), (query_hbm, query_ref), (kv_hbm, kv_ref),
+        (cos_hbm.at[pl.ds(first, TOK)], turns.at[0]), (sin_hbm.at[pl.ds(first, TOK)], turns.at[1]),
     )
     loads = [pltpu.make_async_copy(s, d, local_sem.at[i]) for i, (s, d) in enumerate(pairs)]
     for load in loads:
@@ -1094,28 +1180,32 @@
         sems = [ref.at[k] for ref in (t_recv, plane_send, plane_recv, back_send, back_recv)]
         return Total(net, axis, source, result, span, rows, first, piece, buffers, sems)
 
-    sum_o = unit(
-        0, 2, do_out, o_sum_hbm, 512, 512, 0, (32, 256), their_a, low_a, high_a, hop_a, piece_a, done_a
-    )
+    sum_o = [
+        unit(
+            h, 2 * h, do_out, o_sum_hbm, 512, 256, 256 * h, (16, 256),
+            *[ref.at[h] for ref in (their_a, low_a, high_a, hop_a, piece_a, done_a)],
+        )
+        for h in range(2)
+    ]
     sum_q = unit(
-        1, 0, dq_out, q_hbm, 512, 512, 0, (32, 256), their_b, low_b, high_b, hop_b, piece_b, done_b
+        2, 1, dq_out, q_hbm, 512, 512, 0, (32, 256), their_b, low_b, high_b, hop_b, piece_b, done_b
     )
     sum_kv = [
         unit(
-            2 + h, 2 * h, dkv_out, kv_hbm, 512, 256, 256 * h, (16, 256),
+            3 + h, 2 * h, dkv_out, kv_sum_hbm, 512, 256, 256 * h, (16, 256),
             *[ref.at[h] for ref in (their_c, low_c, high_c, hop_c, piece_c, done_c)],
         )
         for h in range(2)
     ]
     sum_n = unit(
-        4, 1, narrow_ref, narrow_hbm, 64, 64, 0, (8, 128),
+        5, 0, narrow_ref, narrow_hbm, 64, 64, 0, (8, 128),
         their_n, low_n, high_n, hop_n, piece_n, done_n,
     )
     late = [*sum_kv, sum_n]
-    everyone = [sum_o, sum_q, *late]
-    here = sum_o.here
+    everyone = [*sum_o, sum_q, *late]
+    here = sum_q.here
     partners = [
-        sum_o.at([here[0] + i, here[1] + j, here[2] + k])
+        sum_q.at([here[0] + i, here[1] + j, here[2] + k])
         for i in range(4)
         for j in range(4)
         for k in range(4)
@@ -1124,10 +1214,31 @@
     greet(partners + [sibling])
     loads[0].wait()
     plane.begin()
-    for i, (source, target) in enumerate(((pg_hbm, sg), (pu_hbm, su), (pd_hbm, sd))):
-        net.start(source.at[1 - core], target, 18 + i, sibling)
-
-    first = pl.multiple_of(y * TOK, TOK)
+    for load in loads[6:16]:
+        load.wait()
+
+    def block(ref, step, rows=None):
+        span = pl.ds(pl.multiple_of(wrap(y + step) * TOK, TOK), TOK)
+        return ref.at[:, span] if rows is None else ref.at[rows, span]
+
+    def down_block(ref, step):
+        return ref.at[pl.ds(pl.multiple_of(wrap(y + step) * TOK, TOK), TOK)]
+
+    top, bottom = pl.ds(0, 512), pl.ds(512, 512)
+
+    def weight_portion(step, which):
+        if which == 0:
+            return [block(pg, step), block(pu, step, top)]
+        return [block(pu, step, bottom), down_block(pd, step)]
+
+    weights = RingReduce(
+        net, 24, ahead, behind, weight_portion,
+        ([hop_g, hop_u.at[top]], [hop_u.at[bottom], hop_d]),
+        ([low_g, low_u.at[top]], [low_u.at[bottom], low_d]),
+        ([high_g, high_u.at[top]], [high_u.at[bottom], high_d]),
+    )
+    weights.direct()
+
     row = lax.broadcasted_iota(jnp.int32, (TOK, 1), 0) + y * TOK
     upstream = jnp.where(row < len_ref[0], cot_ref[...].astype(F32), 0.0)
     gates = gates_ref[...]
@@ -1156,46 +1267,15 @@
     narrow_ref[3:4, :] = grad_gain_moe
     narrow_ref[4:5, :] = jnp.zeros((1, D), F32)
     narrow_ref[4:5, 0:TOK] = counts
+    for load in loads[16:]:
+        load.wait()
     do_out[...] = lax.dot_general(
         mixed_ref[...], low, by_row, preferred_element_type=F32
     ).astype(BF)
-    sum_o.begin()
-    plane.middle()
-
-    def block(ref, step, rows=None):
-        span = pl.ds(pl.multiple_of(wrap(y + step) * TOK, TOK), TOK)
-        return ref.at[:, span] if rows is None else ref.at[rows, span]
-
-    def down_block(ref, step):
-        return ref.at[pl.ds(pl.multiple_of(wrap(y + step) * TOK, TOK), TOK)]
-
-    top, bottom = pl.ds(0, 512), pl.ds(512, 512)
-
-    def weight_portion(step, which):
-        if which == 0:
-            return [block(pg, step), block(pu, step, top)]
-        return [block(pu, step, bottom), down_block(pd, step)]
-
-    def weight_merge(step):
-        accumulate(block(pg, step), block(sg, step))
-        accumulate(block(pu, step), block(su, step))
-        accumulate(down_block(pd, step), down_block(sd, step))
-
-    weights = RingReduce(
-        net, 24, ahead, behind, weight_portion,
-        ([hop_g, hop_ua], [hop_ub, hop_d]),
-        ([low_g, low_u.at[top]], [low_u.at[bottom], low_d]),
-        ([high_g, high_u.at[top]], [high_u.at[bottom], high_d]),
-    )
-    for load in loads[6:]:
-        load.wait()
-    for i, ref in enumerate((sg, su, sd)):
-        net.arrived(ref, 18 + i)
-    weight_merge(2)
-    weights.begin()
-    sum_o.second()
-
-    cosine, sine = cos_ref[pl.ds(first, TOK), :], sin_ref[pl.ds(first, TOK), :]
+    for one in sum_o:
+        one.begin()
+
+    cosine, sine = turns[0], turns[1]
     loads[2].wait()
 
     def attend(c, carry):
@@ -1234,8 +1314,9 @@
     )
     sums.begin()
     sums.direct()
-    plane.third()
-    sum_o.third()
+    for one in sum_o:
+        one.second()
+    plane.middle()
     tokens = tok_ref[...].astype(F32)
     scale = root(tokens)
     normed = (tokens * scale * ga_ref[...]).astype(BF)
@@ -1244,17 +1325,10 @@
     ).astype(BF)
     sum_q.begin()
     sums.middle()
-    plane.fourth()
-    sum_q.second()
     for load in loads[3:6]:
         load.wait()
     grad_normed = lax.dot_general(grad_query[...], wq[...], by_col, preferred_element_type=F32)
-    weight_merge(1)
-    weight_merge(-1)
-    weight_merge(0)
-    sum_o.fourth()
     sums.finish()
-    weights.direct()
     both = grad_kv[y].astype(F32) + kv_low[...].astype(F32) + kv_high[...].astype(F32)
     grad_key = jnp.concatenate(
         [turn(both[:, c * 128 : (c + 1) * 128], cosine, -sine) for c in range(4)], axis=1
@@ -1268,34 +1342,42 @@
     ).astype(BF)
     sum_kv[0].begin()
     sum_kv[1].begin()
+    sum_q.second()
+    weights.middle(here=True)
     grad_normed += lax.dot_general(grad_key, wk[...], by_col, preferred_element_type=F32)
     grad_normed += lax.dot_general(grad_value, wv[...], by_col, preferred_element_type=F32)
     narrow_ref[2:3, :] = jnp.sum(grad_normed * tokens * scale, axis=0, keepdims=True)
     sum_n.begin()
-    sum_q.third()
     for one in late:
         one.second()
-    weights.middle()
-    sum_o.fifth()
+    for one in sum_o:
+        one.third()
     scaled = grad_normed * ga_ref[...]
     pull = jnp.mean(scaled * tokens, axis=1, keepdims=True)
     input_ref[...] += scale * scaled - tokens * (scale * scale * scale) * pull
     for one in late:
         one.third()
-    sum_q.fourth()
-    sum_o.sixth(local_sem.at[0])
-    layer_ref[...] = (hidden_ref[...] + plane.finish()).astype(BF)
+    for one in sum_o:
+        one.fourth()
+    sum_q.third()
+    plane.third()
     for one in late:
         one.fourth()
-    sum_q.fifth()
-    sum_o.seventh()
+    for one in sum_o:
+        one.fifth()
+    plane.fourth()
+    sum_q.fourth()
     for one in late:
         one.fifth()
-    sum_q.sixth(local_sem.at[1])
-    sum_o.eighth()
+    for i, one in enumerate(sum_o):
+        one.sixth(local_sem.at[i])
+    layer_ref[...] = (hidden_ref[...] + plane.finish()).astype(BF)
+    sum_q.fifth()
     for i, one in enumerate(late):
-        one.sixth(local_sem.at[2 + i])
-    sum_q.seventh()
+        one.sixth(local_sem.at[3 + i])
+    for one in sum_o:
+        one.seventh()
+    sum_q.sixth(local_sem.at[2])
     weights.finish()
     gate_out[...] = (
         block(pg, 0)[...].astype(F32) + low_g[...].astype(F32) + high_g[...].astype(F32)
@@ -1304,14 +1386,33 @@
     down_out[...] = (
         down_block(pd, 0)[...].astype(F32) + low_d[...].astype(F32) + high_d[...].astype(F32)
     )
+    stores = [
+        pltpu.make_async_copy(src, dst, local_sem.at[9 + i])
+        for i, (src, dst) in enumerate(
+            (
+                (layer_ref, layer_hbm),
+                (input_ref, input_hbm),
+                (gate_out, gate_hbm),
+                (up_out, up_hbm),
+                (down_out, down_hbm),
+            )
+        )
+    ]
+    for store in stores:
+        store.start()
     for one in late:
         one.seventh()
-    sum_q.eighth()
+    for one in sum_o:
+        one.eighth()
+    sum_q.seventh()
     for one in late:
         one.eighth()
+    sum_q.eighth()
     for one in everyone:
         one.finish()
     net.drain()
+    for store in stores:
+        store.wait()
 
 
 def back(operands, arrays):
@@ -1334,9 +1435,26 @@
             shape((D, D), BF),
             shape((TOK, D), F32),
         ),
-        in_specs=[vmem] * 16 + [smem] + [any_space] * 9,
-        out_specs=(vmem,) * 5 + (any_space,) * 4,
+        in_specs=[
+            any_space, vmem, any_space, vmem, any_space, *[vmem] * 3, *[any_space] * 7, vmem, smem,
+            *[any_space] * 12,
+        ],
+        out_specs=(any_space,) * 9,
         scratch_shapes=[
+            low(TOK, D),
+            pltpu.VMEM((TOK, D), F32),
+            pltpu.VMEM((D, TOK), F32),
+            pltpu.VMEM((D, TOK), F32),
+            pltpu.VMEM((TOK, D), F32),
+            pltpu.VMEM((TOK, D), F32),
+            low(TOK, D),
+            pltpu.VMEM((TOK, D), F32),
+            low(TOK, D),
+            low(TOK, D),
+            low(TOK, D),
+            low(TOK, D),
+            low(4, TOK, D),
+            pltpu.VMEM((2, TOK, TOK), F32),
             low(8, 2 * TOK, 512),
             low(D, D),
             low(D, D),
@@ -1350,12 +1468,8 @@
             low(D, FF),
             low(D, FF),
             low(FF, D),
-            low(D, FF),
-            low(D, FF),
-            low(FF, D),
             low(D, TOK),
-            low(512, TOK),
-            low(512, TOK),
+            low(D, TOK),
             low(TOK, D),
             low(D, TOK),
             low(D, TOK),
@@ -1373,38 +1487,38 @@
             low(D, D),
             low(D, D),
             pltpu.VMEM((TOK, D), F32),
-            low(512, D),
+            low(2, 256, D),
             low(512, D),
             low(2, 256, D),
             pltpu.VMEM((64, D), F32),
-            low(128, D),
+            low(2, 64, D),
             low(128, D),
             low(2, 64, D),
             pltpu.VMEM((16, D), F32),
-            low(128, D),
+            low(2, 64, D),
             low(128, D),
             low(2, 64, D),
             pltpu.VMEM((16, D), F32),
-            low(128, D),
+            low(2, 64, D),
             low(128, D),
             low(2, 64, D),
             pltpu.VMEM((16, D), F32),
-            low(16, 32, 256),
+            low(2, 16, 16, 256),
             low(16, 32, 256),
             low(2, 16, 16, 256),
             pltpu.VMEM((16, 8, 128), F32),
-            low(128, D),
+            low(2, 64, D),
             low(128, D),
             low(2, 64, D),
             pltpu.VMEM((16, D), F32),
-            dma((120,)),
+            dma((160,)),
             dma((42,)),
-            dma((9,)),
-            dma((5, 15)),
-            dma((5, 16)),
-            dma((5, 16)),
-            dma((5, 16)),
-            dma((5, 16)),
+            dma((22,)),
+            dma((6, 15)),
+            dma((6, 16)),
+            dma((6, 16)),
+            dma((6, 16)),
+            dma((6, 16)),
         ],
         compiler_params=pltpu.CompilerParams(
             collective_id=4, has_side_effects=True, vmem_limit_bytes=VMEM_BYTES
@@ -1497,8 +1611,8 @@
     lengths,
 ):
     (
-        hidden, x, gates, mixed, query, kv, grad_rows, grad_gates, probs, out_parts, part_gate,
-        part_up, part_down,
+        gates, grad_rows, grad_gates, hidden, x, mixed, query, kv, probs, out_parts, part_gate,
+        part_up, part_down, *far_parts,
     ) = main(
         tokens, w_query, w_key, w_value, w_output, gain_attn, gain_moe, router.T, cotangent,
         routes.T, lengths, w_gate, w_up, w_down,
@@ -1512,7 +1626,8 @@
         ),
         (
             probs, w_output, w_query, w_key, w_value, out_parts, part_gate, part_up,
-            part_down.reshape(2, FF, D),
+            part_down.reshape(FF, D),
+            *far_parts,
         ),
     )
     (

time: 222 us -> 205 us (0.923)
  Pallas kernels: 220 us -> 203 us
    pallas_call x1, Pallas kernels: 106 us -> 89.3 us  [back(): pl.pallas_call(back_kernel, out_shape=(shape((TOK, D), BF), shape((TOK, D...]
where the time goes in v6:
time: 205 us; the launch traced here: 204 us
  Pallas kernels  203 us (99%)
    pallas_call x1, Pallas kernels, main(): pl.pallas_call(main_kernel, out_shape=(shape((TOK, TOK), F32), shape((TOK...  104 us
    pallas_call x1, Pallas kernels, back(): pl.pallas_call(back_kernel, out_shape=(shape((TOK, D), BF), shape((TOK, D...  89.3 us
    pallas_call x1, Pallas kernels, results(): pl.pallas_call(results_kernel, grid=(D // rows,), out_shape=(shape((D, D)...  10 us

profile of v6, /device:TPU:1, one launch (start us, length us, event | category | flops | bytes accessed | tf_op | source)
XLA Modules:
  0.0 204.4 jit_solution(15950869551900026147)
XLA Ops:
  1.3 103.6 %main.1 = (f32[128,128]{1,0:T(8,128)}, f32[128,1024]{1,0:T(8,128)}, f32[16,8,128]{2,1,0:T(8,128)}, f32[128,1024]{1,0:T(8,128)}, bf16[128,1024]{1,0:T(8,128)(2,1)...) custom-call(bf16[128,1024]{1,0:T(8,128)(2,1)} %tok_hbm.1, ...), custom_call_target="tpu_custom_call" | custom-call | tf_op jit(solution)/shard_map/main/pallas_call | solution.py:761
  104.9 89.3 %back.1 = (bf16[128,1024]{1,0:T(8,128)(2,1)}, f32[128,1024]{1,0:T(8,128)}, f32[1024,128]{1,0:T(8,128)}, f32[1024,128]{1,0:T(8,128)}, f32[128,1024]{1,0:T(8,128)}...) custom-call(f32[128,1024]{1,0:T(8,128)} %get-tuple-element.51.rows_h, ...), custom_call_target="tpu_custom_call" | custom-call | tf_op jit(solution)/shard_map/back/pallas_call | solution.py:1425
  194.3 10.0 %results.1 = (f32[1024,1024]{1,0:T(8,128)}, f32[1024,1024]{1,0:T(8,128)}, f32[1024,512]{1,0:T(8,128)}, f32[1024,512]{1,0:T(8,128)}, f32[32,1024]{1,0:T(8,128)}, ...) custom-call(bf16[1024,1024]{1,0:T(8,128)(2,1)} %get-tuple-element.67, ...), custom_call_target="tpu_custom_call" | custom-call | tf_op jit(solution)/shard_map/results/pallas_call | solution.py:1561

commit v7 on v6

--- a/solution.py
+++ b/solution.py
@@ -1180,16 +1180,16 @@
         sems = [ref.at[k] for ref in (t_recv, plane_send, plane_recv, back_send, back_recv)]
         return Total(net, axis, source, result, span, rows, first, piece, buffers, sems)
 
-    sum_o = [
+    sum_o = unit(
+        2, 1, do_out, o_sum_hbm, 512, 512, 0, (32, 256), their_b, low_b, high_b, hop_b, piece_b, done_b
+    )
+    sum_q = [
         unit(
-            h, 2 * h, do_out, o_sum_hbm, 512, 256, 256 * h, (16, 256),
+            h, 2 * h, dq_out, q_hbm, 512, 256, 256 * h, (16, 256),
             *[ref.at[h] for ref in (their_a, low_a, high_a, hop_a, piece_a, done_a)],
         )
         for h in range(2)
     ]
-    sum_q = unit(
-        2, 1, dq_out, q_hbm, 512, 512, 0, (32, 256), their_b, low_b, high_b, hop_b, piece_b, done_b
-    )
     sum_kv = [
         unit(
             3 + h, 2 * h, dkv_out, kv_sum_hbm, 512, 256, 256 * h, (16, 256),
@@ -1202,10 +1202,10 @@
         their_n, low_n, high_n, hop_n, piece_n, done_n,
     )
     late = [*sum_kv, sum_n]
-    everyone = [*sum_o, sum_q, *late]
-    here = sum_q.here
+    everyone = [*sum_q, sum_o, *late]
+    here = sum_o.here
     partners = [
-        sum_q.at([here[0] + i, here[1] + j, here[2] + k])
+        sum_o.at([here[0] + i, here[1] + j, here[2] + k])
         for i in range(4)
         for j in range(4)
         for k in range(4)
@@ -1272,8 +1272,7 @@
     do_out[...] = lax.dot_general(
         mixed_ref[...], low, by_row, preferred_element_type=F32
     ).astype(BF)
-    for one in sum_o:
-        one.begin()
+    sum_o.begin()
 
     cosine, sine = turns[0], turns[1]
     loads[2].wait()
@@ -1314,8 +1313,6 @@
     )
     sums.begin()
     sums.direct()
-    for one in sum_o:
-        one.second()
     plane.middle()
     tokens = tok_ref[...].astype(F32)
     scale = root(tokens)
@@ -1323,12 +1320,16 @@
     dq_out[...] = lax.dot_general(
         normed, grad_query[...], by_row, preferred_element_type=F32
     ).astype(BF)
-    sum_q.begin()
+    for one in sum_q:
+        one.begin()
     sums.middle()
     for load in loads[3:6]:
         load.wait()
     grad_normed = lax.dot_general(grad_query[...], wq[...], by_col, preferred_element_type=F32)
+    for one in sum_q:
+        one.second()
     sums.finish()
+    sum_o.second()
     both = grad_kv[y].astype(F32) + kv_low[...].astype(F32) + kv_high[...].astype(F32)
     grad_key = jnp.concatenate(
         [turn(both[:, c * 128 : (c + 1) * 128], cosine, -sine) for c in range(4)], axis=1
@@ -1342,42 +1343,41 @@
     ).astype(BF)
     sum_kv[0].begin()
     sum_kv[1].begin()
-    sum_q.second()
-    weights.middle(here=True)
     grad_normed += lax.dot_general(grad_key, wk[...], by_col, preferred_element_type=F32)
     grad_normed += lax.dot_general(grad_value, wv[...], by_col, preferred_element_type=F32)
     narrow_ref[2:3, :] = jnp.sum(grad_normed * tokens * scale, axis=0, keepdims=True)
     sum_n.begin()
     for one in late:
         one.second()
-    for one in sum_o:
+    for one in sum_q:
         one.third()
     scaled = grad_normed * ga_ref[...]
     pull = jnp.mean(scaled * tokens, axis=1, keepdims=True)
     input_ref[...] += scale * scaled - tokens * (scale * scale * scale) * pull
     for one in late:
         one.third()
-    for one in sum_o:
+    sum_o.third()
+    for one in sum_q:
         one.fourth()
-    sum_q.third()
     plane.third()
     for one in late:
         one.fourth()
-    for one in sum_o:
+    for one in sum_q:
         one.fifth()
     plane.fourth()
-    sum_q.fourth()
+    sum_o.fourth()
+    weights.middle(here=True)
     for one in late:
         one.fifth()
-    for i, one in enumerate(sum_o):
+    for i, one in enumerate(sum_q):
         one.sixth(local_sem.at[i])
     layer_ref[...] = (hidden_ref[...] + plane.finish()).astype(BF)
-    sum_q.fifth()
+    sum_o.fifth()
     for i, one in enumerate(late):
         one.sixth(local_sem.at[3 + i])
-    for one in sum_o:
+    for one in sum_q:
         one.seventh()
-    sum_q.sixth(local_sem.at[2])
+    sum_o.sixth(local_sem.at[2])
     weights.finish()
     gate_out[...] = (
         block(pg, 0)[...].astype(F32) + low_g[...].astype(F32) + high_g[...].astype(F32)
@@ -1402,12 +1402,12 @@
         store.start()
     for one in late:
         one.seventh()
-    for one in sum_o:
+    for one in sum_q:
         one.eighth()
-    sum_q.seventh()
+    sum_o.seventh()
     for one in late:
         one.eighth()
-    sum_q.eighth()
+    sum_o.eighth()
     for one in everyone:
         one.finish()
     net.drain()
@@ -1552,7 +1552,7 @@
 
 
 def results(q, o, kv, narrow, *own):
-    rows = 256
+    rows = 512
     some = rows * TOK // D
     first = lambda *size: pl.BlockSpec((1, *size), lambda i: (0, i, 0))
     block = lambda width: pl.BlockSpec((rows, width), lambda i: (i, 0))
@@ -1590,6 +1590,7 @@
             pl.BlockSpec((some, D), lambda i: (i, 0)),
             first(rows, TOK), first(rows, TOK), first(some, D),
         ),
+        compiler_params=pltpu.CompilerParams(vmem_limit_bytes=VMEM_BYTES),
         name="results",
     )(q, o, kv, narrow, *own)
 

time: 205 us -> 201 us (0.980)
  Pallas kernels: 203 us -> 199 us
    pallas_call x1, Pallas kernels: 89.3 us -> 86.3 us  [back(): pl.pallas_call(back_kernel, out_shape=(shape((TOK, D), BF), shape((TOK, D...]
where the time goes in v7:
time: 201 us; the launch traced here: 200 us
  Pallas kernels  199 us (99%)
    pallas_call x1, Pallas kernels, main(): pl.pallas_call(main_kernel, out_shape=(shape((TOK, TOK), F32), shape((TOK...  104 us
    pallas_call x1, Pallas kernels, back(): pl.pallas_call(back_kernel, out_shape=(shape((TOK, D), BF), shape((TOK, D...  86.3 us
    pallas_call x1, Pallas kernels, results(): pl.pallas_call(results_kernel, grid=(D // rows,), out_shape=(shape((D, D)...  8.96 us

profile of v7, /device:TPU:1, one launch (start us, length us, event | category | flops | bytes accessed | tf_op | source)
XLA Modules:
  0.0 200.3 jit_solution(2197175394652713386)
XLA Ops:
  1.3 103.6 %main.1 = (f32[128,128]{1,0:T(8,128)}, f32[128,1024]{1,0:T(8,128)}, f32[16,8,128]{2,1,0:T(8,128)}, f32[128,1024]{1,0:T(8,128)}, bf16[128,1024]{1,0:T(8,128)(2,1)...) custom-call(bf16[128,1024]{1,0:T(8,128)(2,1)} %tok_hbm.1, ...), custom_call_target="tpu_custom_call" | custom-call | tf_op jit(solution)/shard_map/main/pallas_call | solution.py:761
  104.9 86.3 %back.1 = (bf16[128,1024]{1,0:T(8,128)(2,1)}, f32[128,1024]{1,0:T(8,128)}, f32[1024,128]{1,0:T(8,128)}, f32[1024,128]{1,0:T(8,128)}, f32[128,1024]{1,0:T(8,128)}...) custom-call(f32[128,1024]{1,0:T(8,128)} %get-tuple-element.51.rows_h, ...), custom_call_target="tpu_custom_call" | custom-call | tf_op jit(solution)/shard_map/back/pallas_call | solution.py:1425
  191.2 9.0 %results.1 = (f32[1024,1024]{1,0:T(8,128)}, f32[1024,1024]{1,0:T(8,128)}, f32[1024,512]{1,0:T(8,128)}, f32[1024,512]{1,0:T(8,128)}, f32[32,1024]{1,0:T(8,128)}, ...) custom-call(bf16[1024,1024]{1,0:T(8,128)(2,1)} %get-tuple-element.67, ...), custom_call_target="tpu_custom_call" | custom-call | tf_op jit(solution)/shard_map/results/pallas_call | solution.py:1561

commit v8 on v7

--- a/solution.py
+++ b/solution.py
@@ -1172,8 +1172,9 @@
         (cos_hbm.at[pl.ds(first, TOK)], turns.at[0]), (sin_hbm.at[pl.ds(first, TOK)], turns.at[1]),
     )
     loads = [pltpu.make_async_copy(s, d, local_sem.at[i]) for i, (s, d) in enumerate(pairs)]
-    for load in loads:
-        load.start()
+    soon = (0, 12, 14, 15, 13, 1, 6, 7, 8, 9, 10, 11)
+    for i in soon:
+        loads[i].start()
     plane = PlaneReduce(net, spot, o_buf, rb, rc, rd, re, 0)
 
     def unit(k, axis, source, result, span, rows, first, piece, *buffers):
@@ -1238,6 +1239,8 @@
         ([high_g, high_u.at[top]], [high_u.at[bottom], high_d]),
     )
     weights.direct()
+    for i in (17, 18, 19, 20, 21, 16, 2, 3, 4, 5):
+        loads[i].start()
 
     row = lax.broadcasted_iota(jnp.int32, (TOK, 1), 0) + y * TOK
     upstream = jnp.where(row < len_ref[0], cot_ref[...].astype(F32), 0.0)
@@ -1329,7 +1332,6 @@
     for one in sum_q:
         one.second()
     sums.finish()
-    sum_o.second()
     both = grad_kv[y].astype(F32) + kv_low[...].astype(F32) + kv_high[...].astype(F32)
     grad_key = jnp.concatenate(
         [turn(both[:, c * 128 : (c + 1) * 128], cosine, -sine) for c in range(4)], axis=1
@@ -1343,18 +1345,19 @@
     ).astype(BF)
     sum_kv[0].begin()
     sum_kv[1].begin()
+    sum_o.second()
     grad_normed += lax.dot_general(grad_key, wk[...], by_col, preferred_element_type=F32)
     grad_normed += lax.dot_general(grad_value, wv[...], by_col, preferred_element_type=F32)
     narrow_ref[2:3, :] = jnp.sum(grad_normed * tokens * scale, axis=0, keepdims=True)
     sum_n.begin()
     for one in late:
         one.second()
-    for one in sum_q:
-        one.third()
     scaled = grad_normed * ga_ref[...]
     pull = jnp.mean(scaled * tokens, axis=1, keepdims=True)
     input_ref[...] += scale * scaled - tokens * (scale * scale * scale) * pull
     for one in late:
+        one.third()
+    for one in sum_q:
         one.third()
     sum_o.third()
     for one in sum_q:

time: 201 us -> 199 us (0.990)
  no operation moved by 1% of the time
where the time goes in v8:
time: 199 us
  Pallas kernels  197 us (99%)
    pallas_call x1, Pallas kernels, main(): pl.pallas_call(main_kernel, out_shape=(shape((TOK, TOK), F32), shape((TOK...  104 us
    pallas_call x1, Pallas kernels, back(): pl.pallas_call(back_kernel, out_shape=(shape((TOK, D), BF), shape((TOK, D...  84.5 us
    pallas_call x1, Pallas kernels, results(): pl.pallas_call(results_kernel, grid=(D // rows,), out_shape=(shape((D, D)...  8.96 us

profile of v8, /device:TPU:1, one launch (start us, length us, event | category | flops | bytes accessed | tf_op | source)
XLA Modules:
  0.0 198.6 jit_solution(10310137458484497580)
XLA Ops:
  1.3 103.6 %main.1 = (f32[128,128]{1,0:T(8,128)}, f32[128,1024]{1,0:T(8,128)}, f32[16,8,128]{2,1,0:T(8,128)}, f32[128,1024]{1,0:T(8,128)}, bf16[128,1024]{1,0:T(8,128)(2,1)...) custom-call(bf16[128,1024]{1,0:T(8,128)(2,1)} %tok_hbm.1, ...), custom_call_target="tpu_custom_call" | custom-call | tf_op jit(solution)/shard_map/main/pallas_call | solution.py:761
  104.9 84.5 %back.1 = (bf16[128,1024]{1,0:T(8,128)(2,1)}, f32[128,1024]{1,0:T(8,128)}, f32[1024,128]{1,0:T(8,128)}, f32[1024,128]{1,0:T(8,128)}, f32[128,1024]{1,0:T(8,128)}...) custom-call(f32[128,1024]{1,0:T(8,128)} %get-tuple-element.51.rows_h, ...), custom_call_target="tpu_custom_call" | custom-call | tf_op jit(solution)/shard_map/back/pallas_call | solution.py:1428
  189.4 9.0 %results.1 = (f32[1024,1024]{1,0:T(8,128)}, f32[1024,1024]{1,0:T(8,128)}, f32[1024,512]{1,0:T(8,128)}, f32[1024,512]{1,0:T(8,128)}, f32[32,1024]{1,0:T(8,128)}, ...) custom-call(bf16[1024,1024]{1,0:T(8,128)(2,1)} %get-tuple-element.67, ...), custom_call_target="tpu_custom_call" | custom-call | tf_op jit(solution)/shard_map/results/pallas_call | solution.py:1564
